TPU v7x, 32 devices: a whole 2x2x4 slice. The times are simulated.
32 devices in a mesh: scene: 2 (over x), tile: 8 (over z, y), frame: 2 (over core).
Axes of the slice: x: 2, y: 2, z: 4, core: 2. Of those that a mesh axis runs over, the one named last changes fastest.
Arguments:
- observed: float32 [64, 256, 2048], P('frame', ('scene', 'tile')), parts along dimension 1, may hold values from -6 to 6
- frame_shift: int32 [4, 64], P('scene', 'frame'), parts along dimension 0, may hold values from 0 to 3
- kernel_ids: int32 [2, 64], P('scene', 'frame'), parts along dimension 0, may hold values from 0 to 7
- groups: int32 [2, 64], P('scene', 'frame'), parts along dimension 0, may hold values from 0 to 3
- kernels: float32 [8, 5, 5], replicated, may hold values from 0 to 0.08
- gains: float32 [4], replicated, may hold values from 0.5 to 2
Outputs:
- solution: float32 [1024, 8192], P(('scene', 'tile'), 'frame'), parts along dimension 0
- residual: float32 [1024, 8192], P(('scene', 'tile'), 'frame'), parts along dimension 0
There are 2 independent parts, one for each index of `scene`. A program takes and returns all parts, laid end to end along the dimension named above; an argument that names none is the same for every part. Nothing has to cross between parts.
All inputs are finite; a program needn't handle non-finite values.
Results may differ from a plain program's by a relative error of at most 0.00026.
Values sent between devices are 32-bit elements; how exact they have to be, the bound alone decides.
No kernel may reach another device: no remote copies, remote signals or barrier semaphores. Data moves between devices by JAX's collectives and lax.ppermute only.
A program may use at most 128 MiB of HBM per device.

v0:
```python
import jax
import jax.numpy as jnp
from jax import lax
from jax.sharding import PartitionSpec as P

ITERS = 2


damping = 0.3
offsets = [(t, (t - 2) % 4, (t - 2) // 4) for t in range(8)]


def padded_2(cells, sides, width):
    for axis, dim in sides:
        count = lax.axis_size(axis)
        ends = count - 1
        head = lax.slice_in_dim(cells, 0, width, axis=dim)
        tail = lax.slice_in_dim(cells, cells.shape[dim] - width, cells.shape[dim], axis=dim)
        cells = jnp.concatenate(
            [
                lax.ppermute(tail, axis, [(i, (i + 1) % count) for i in range(ends)]),
                cells,
                lax.ppermute(head, axis, [((i + 1) % count, i) for i in range(ends)]),
            ],
            axis=dim,
        )
    return cells


def effective(frame_shift, kernel_ids, groups, kernels, gains):
    taps = jnp.arange(8, dtype=jnp.int32)
    span = jnp.arange(5, dtype=jnp.int32)
    rows = (taps[None, :, None] - frame_shift[0][:, None, None] == span[None, None, :]).astype(
        jnp.float32
    )
    cols = (taps[None, :, None] - frame_shift[1][:, None, None] == span[None, None, :]).astype(
        jnp.float32
    )
    count = kernels.shape[0]
    pick = (kernel_ids[0][:, None] == jnp.arange(count, dtype=jnp.int32)[None, :]).astype(
        jnp.float32
    )
    chosen = jnp.dot(pick, kernels.reshape(count, 25), precision=lax.Precision.HIGHEST).reshape(
        -1, 5, 5
    )
    member = (groups[0][:, None] == jnp.arange(gains.shape[0], dtype=jnp.int32)[None, :]).astype(
        jnp.float32
    )
    scale = jnp.dot(member, gains, precision=lax.Precision.HIGHEST)
    table = jnp.einsum("kra,kab,kcb->krc", rows, chosen, cols, precision=lax.Precision.HIGHEST)
    return (scale[:, None, None] * table).reshape(-1, 64)


def unphase(field):
    return field.transpose(2, 0, 3, 1).reshape(4 * field.shape[2], 4 * field.shape[3])


def forward_cells(extended, weights, count, width):
    stack = jnp.stack(
        [
            extended[pr, pc, 1 + qr : 1 + qr + count, 1 + qc : 1 + qc + width]
            for tr, pr, qr in offsets
            for tc, pc, qc in offsets
        ]
    )
    return jnp.einsum("kt,tij->kij", weights, stack, precision=lax.Precision.HIGHEST)


def forward(extended, weights, count):
    padded = jnp.pad(extended, ((0, 0), (0, 0), (0, 0), (1, 1)))
    return forward_cells(padded, weights, count, extended.shape[3])


def adjoint_cells(padded, weights, count, quarter):
    mixed = jnp.einsum("kt,kij->tij", weights, padded, precision=lax.Precision.HIGHEST)
    pieces = []
    for phase_row in range(4):
        for phase_col in range(4):
            total = jnp.zeros((count, quarter), jnp.float32)
            for tr, pr, qr in offsets:
                for tc, pc, qc in offsets:
                    if pr == phase_row and pc == phase_col:
                        total = (
                            total
                            + mixed[tr * 8 + tc, 1 - qr : 1 - qr + count, 1 - qc : 1 - qc + quarter]
                        )
            pieces.append(total)
    return jnp.stack(pieces).reshape(4, 4, count, quarter)


def adjoint(images, weights, count):
    padded = jnp.pad(images, ((0, 0), (0, 0), (1, 1)))
    return adjoint_cells(padded, weights, count, images.shape[2])


def per_device(observed, frame_shift, kernel_ids, groups, kernels, gains):
    spread = lax.axis_size("frame")
    member = lax.axis_index("frame")
    weights = effective(frame_shift, kernel_ids, groups, kernels, gains)
    count = observed.shape[1]
    half = observed.shape[2] // spread
    place = lax.axis_index("tile") * count + jnp.arange(count + 2, dtype=jnp.int32) - 1
    valid = ((place >= 0) & (place < lax.axis_size("tile") * count)).astype(jnp.float32)

    def combine(partial_value):
        return lax.psum(partial_value, "frame")

    def own_part(field):
        return lax.dynamic_slice_in_dim(field, member * half, half, 3)

    def squares(field):
        part = own_part(field)
        return lax.psum(jnp.sum(part * part), ("tile", "frame"))

    bordered = padded_2(observed, (("tile", 1),), 1)
    rhs = combine(adjoint(bordered, weights, count))
    solution = jnp.zeros_like(rhs)
    residual = rhs
    direction = rhs
    norm_now = squares(residual)
    for step in range(ITERS):
        complete = direction
        extended = padded_2(complete, (("tile", 2),), 2)
        images = forward(extended, weights, count + 2) * valid[None, :, None]
        image = combine(adjoint(images, weights, count)) + damping * direction
        product = lax.psum(jnp.sum(own_part(direction) * own_part(image)), ("tile", "frame"))
        alpha = norm_now / product
        solution = solution + alpha * direction
        residual = residual - alpha * image
        norm_next = squares(residual)
        direction = residual + norm_next / norm_now * direction
        norm_now = norm_next
    return (unphase(own_part(solution)), unphase(own_part(residual)))


def solution(mesh):
    return jax.shard_map(
        per_device,
        mesh=mesh,
        in_specs=(
            P("frame", ("scene", "tile"), None),
            P("scene", "frame"),
            P("scene", "frame"),
            P("scene", "frame"),
            P(),
            P(),
        ),
        out_specs=(P(("scene", "tile"), "frame"), P(("scene", "tile"), "frame")),
        check_vma=False,
    )
```

profile of v0, /device:TPU:0, one launch (start us, length us, event | category | flops | bytes accessed | tf_op | source)
XLA Modules:
  0.0 602.9 jit_solution(16647054532506621541)
XLA Ops:
  21.8 8.1 %collective-permute-done = f32[32,1,2048]{2,0,1:T(8,128)S(1)} collective-permute-done((f32[32,1,2048]{2,0,1:T(8,128)S(1)}, f32[32,1,2048]{2,0,1:T(8,128)S(1)}, u32[]{:S(2)}, u32[]{:S(2)}) %collective-permute-start) | collective-permute-done | bytes 262176 | tf_op jit(solution)/shard_map/ppermute | solution.py:21
  29.9 10.7 %fusion = f32[64,18,2050]{2,0,1:T(8,128)S(1)} fusion(f32[32,1,2048]{2,0,1:T(8,128)S(1)} %collective-permute-done.1, f32[32,16,2048]{2,0,1:T(8,128)} %copy-done.5, f32[32,1,2048]{2,0,1:T(8,128)S(1)} %collective-permute-done, f32[32,8,8]{0,2,1:T(8,128)S(1)} %copy.93), kind=kOutput, calls=%fused_computation.3 | convolution fusion | flops 916300800 | bytes 14173184 | tf_op jit(solution)/shard_map/kt,kij->tij/dot_general | solution.py:75
  52.1 6.4 %slice_add_fusion.96 = (f32[1,16,2048]{2,0,1:T(1,128)}, f32[1,16,2048]{2,0,1:T(1,128)}, f32[1,16,2048]{2,0,1:T(1,128)}, f32[1,16,2048]{2,0,1:T(1,128)}) fusion(f32[64,18,2050]{2,0,1:T(8,128)S(1)} %fusion), kind=kLoop, calls=%fused_computation.258 | loop fusion | flops 393216 | bytes 2621440 | tf_op jit(solution)/shard_map/add | solution.py:84
  69.9 23.5 %all-reduce.10.cloned.1.call-done = f32[4,4,16,2048]{3,0,2,1:T(4,128)} async-done(((f32[4,4,16,2048]{3,0,2,1:T(4,128)}), f32[4,4,16,2048]{3,0,2,1:T(4,128)}) %all-reduce.10.cloned.1.call-update) | async-done | bytes 2097168 | tf_op jit(solution)/shard_map/psum | solution.py:106
  99.5 10.3 %collective-permute-done.2 = f32[4,4,2,2048]{3,0,2,1:T(4,128)S(1)} collective-permute-done((f32[4,4,2,2048]{3,0,2,1:T(4,128)S(1)}, f32[4,4,2,2048]{3,0,2,1:T(4,128)S(1)}, u32[]{:S(2)}, u32[]{:S(2)}) %collective-permute-start.2) | collective-permute-done | bytes 262176 | tf_op jit(solution)/shard_map/ppermute | solution.py:21
  120.4 8.7 %slice_bitcast_fusion.80 = (f32[1,18,2048]{2,0,1:T(1,128)}, f32[1,18,2048]{2,0,1:T(1,128)}, f32[1,18,2048]{2,0,1:T(1,128)}, f32[1,18,2048]{2,0,1:T(1,128)}, f32[...) fusion(f32[4,4,20,2048]{3,0,2,1:T(4,128)S(1)} %get-tuple-elemen, ...), kind=kLoop, calls=%fused_computation.130 | loop fusion | bytes 5423104 | tf_op jit(solution)/shard_map/stack;squeeze | solution.py:59
  132.9 35.2 %stack.11 = f32[64,18,2048]{2,0,1:T(8,128)} concatenate(f32[1,18,2048]{2,0,1:T(1,128)S(1)} %get-tuple-element.119, f32[1,18,2048]{2,0,1:T(1,128)S(1)} %get-tuple-element.118, f32[1,18,2048]{2,0,1:T(1,128)} %get-tuple-element.183, f32[1,18,2048]{2,0,1:T(1,128)} %get-tuple-element.182, f32[1,18,2048]{2,0,1:T(1,128)} %get-tuple-element.181, f32[1,18,2048]{2,0,1:T(1,128)} %get-tuple-element.180, ...), dimensions={0} | concatenate | bytes 18874368 | tf_op jit(solution)/shard_map/stack | solution.py:59
  168.1 7.8 %convolution_multiply_fusion.1 = f32[32,18,2048]{2,0,1:T(8,128)S(1)} fusion(f32[64,18,2048]{2,0,1:T(8,128)} %stack.11, f32[18]{0:T(128)S(1)} %and_convert_fusion, f32[32,8,8]{0,2,1:T(8,128)S(1)} %copy.93), kind=kOutput, calls=%fused_computation.15 | convolution fusion | flops 907149312 | bytes 14164040 | tf_op jit(solution)/shard_map/kt,tij->kij/dot_general | solution.py:66
  175.9 8.4 %fusion.7 = f32[64,18,2050]{2,0,1:T(8,128)S(1)} fusion(f32[32,18,2048]{2,0,1:T(8,128)S(1)} %convolution_multiply_fusion.1, f32[32,8,8]{0,2,1:T(8,128)S(1)} %copy.93), kind=kOutput, calls=%fused_computation.11 | convolution fusion | flops 906854400 | bytes 14173184 | tf_op jit(solution)/shard_map/kt,kij->tij/dot_general | solution.py:75
  211.5 22.3 %all-reduce.12.cloned.1.call-done = f32[4,4,16,2048]{3,0,2,1:T(4,128)} async-done(((f32[4,4,16,2048]{3,0,2,1:T(4,128)}), f32[4,4,16,2048]{3,0,2,1:T(4,128)}) %all-reduce.12.cloned.1.call-update) | async-done | bytes 2097168 | tf_op jit(solution)/shard_map/psum | solution.py:106
  237.7 34.5 %all-reduce.5 = (f32[]{:T(128)}, f32[]{:T(128)}) all-reduce(f32[]{:T(128)} %get-tuple-element.3, f32[]{:T(128)} %get-tuple-element.2), channel_id=1, replica_groups=mesh['scene'=2,'tile'=8,'frame'=2] {'tile','frame'}, use_global_device_ids=true, to_apply=%region_2.3 | all-reduce | flops 2 | bytes 16 | tf_op jit(solution)/shard_map/psum | solution.py:113
  278.7 30.1 %psum.53 = f32[]{:T(128)} all-reduce(f32[]{:T(128)} %multiply_reduce_fusion.1), channel_id=1, replica_groups=mesh['scene'=2,'tile'=8,'frame'=2] {'tile','frame'}, use_global_device_ids=true, to_apply=%region_7.8 | all-reduce | flops 1 | bytes 8 | tf_op jit(solution)/shard_map/psum | solution.py:113
  316.1 10.2 %collective-permute-done.4 = f32[4,4,2,2048]{3,0,2,1:T(4,128)S(1)} collective-permute-done((f32[4,4,2,2048]{3,0,2,1:T(4,128)S(1)}, f32[4,4,2,2048]{3,0,2,1:T(4,128)S(1)}, u32[]{:S(2)}, u32[]{:S(2)}) %collective-permute-start.4) | collective-permute-done | bytes 262176 | tf_op jit(solution)/shard_map/ppermute | solution.py:21
  335.2 8.6 %slice_bitcast_fusion.48 = (f32[1,18,2048]{2,0,1:T(1,128)}, f32[1,18,2048]{2,0,1:T(1,128)}, f32[1,18,2048]{2,0,1:T(1,128)}, f32[1,18,2048]{2,0,1:T(1,128)}, f32[...) fusion(f32[4,4,20,2048]{3,0,2,1:T(4,128)S(1)} %pad_maximum_fusion), kind=kLoop, calls=%fused_computation.98 | loop fusion | bytes 5423104 | tf_op jit(solution)/shard_map/stack;squeeze | solution.py:59
  348.0 35.9 %stack.13 = f32[64,18,2048]{2,0,1:T(8,128)} concatenate(f32[1,18,2048]{2,0,1:T(1,128)} %get-tuple-element.87, f32[1,18,2048]{2,0,1:T(1,128)} %get-tuple-element.86, f32[1,18,2048]{2,0,1:T(1,128)} %get-tuple-element.167, f32[1,18,2048]{2,0,1:T(1,128)} %get-tuple-element.166, f32[1,18,2048]{2,0,1:T(1,128)} %get-tuple-element.165, f32[1,18,2048]{2,0,1:T(1,128)} %get-tuple-element.164, ...), dimensions={0} | concatenate | bytes 18874368 | tf_op jit(solution)/shard_map/stack | solution.py:59
  383.8 7.8 %convolution_multiply_fusion = f32[32,18,2048]{2,0,1:T(8,128)S(1)} fusion(f32[64,18,2048]{2,0,1:T(8,128)} %stack.13, f32[18]{0:T(128)S(1)} %and_convert_fusion, f32[32,8,8]{0,2,1:T(8,128)S(1)} %copy.93), kind=kOutput, calls=%fused_computation.14 | convolution fusion | flops 907149312 | bytes 14164040 | tf_op jit(solution)/shard_map/kt,tij->kij/dot_general | solution.py:66
  391.6 8.4 %fusion.5 = f32[64,18,2050]{2,0,1:T(8,128)S(1)} fusion(f32[32,18,2048]{2,0,1:T(8,128)S(1)} %convolution_multiply_fusion, f32[32,8,8]{0,2,1:T(8,128)S(1)} %copy.93), kind=kOutput, calls=%fused_computation.9 | convolution fusion | flops 906854400 | bytes 14173184 | tf_op jit(solution)/shard_map/kt,kij->tij/dot_general | solution.py:75
  417.3 7.6 %stack.14 = f32[16,16,2048]{2,0,1:T(8,128)} concatenate(f32[1,16,2048]{2,0,1:T(1,128)S(1)} %get-tuple-element.21, f32[1,16,2048]{2,0,1:T(1,128)S(1)} %get-tuple-element.17, f32[1,16,2048]{2,0,1:T(1,128)S(1)} %get-tuple-element.12, f32[1,16,2048]{2,0,1:T(1,128)} %get-tuple-element.7, f32[1,16,2048]{2,0,1:T(1,128)S(1)} %get-tuple-element.20, f32[1,16,2048]{2,0,1:T(1,128)S(1)} %get-tuple-element.15, ...), dimensions={0} | concatenate | bytes 4194304 | tf_op jit(solution)/shard_map/stack | solution.py:88
  430.3 20.5 %all-reduce.14.cloned.1.call-done = f32[4,4,16,2048]{3,0,2,1:T(4,128)} async-done(((f32[4,4,16,2048]{3,0,2,1:T(4,128)}), f32[4,4,16,2048]{3,0,2,1:T(4,128)}) %all-reduce.14.cloned.1.call-update) | async-done | bytes 2097168 | tf_op jit(solution)/shard_map/psum | solution.py:106
  456.0 34.5 %psum.55 = f32[]{:T(128)} all-reduce(f32[]{:T(128)} %multiply_reduce_fusion), channel_id=1, replica_groups=mesh['scene'=2,'tile'=8,'frame'=2] {'tile','frame'}, use_global_device_ids=true, to_apply=%region_10.11 | all-reduce | flops 1 | bytes 8 | tf_op jit(solution)/shard_map/psum | solution.py:126
  493.9 16.6 %copy.108 = f32[16,4,1024,4]{3,2,1,0:T(8,128)} copy(f32[16,4,1024,4]{2,1,0,3:T(4,128)S(1)} %subtract_bitcast_fusion) | data formatting | bytes 2097152 | tf_op jit(solution)/shard_map/transpose | solution.py:55
  510.5 33.6 %reshape.101 = f32[64,4096]{1,0:T(8,128)} reshape(f32[16,4,1024,4]{3,2,1,0:T(8,128)} %copy.108) | data formatting | bytes 2097152 | tf_op jit(solution)/shard_map/reshape | solution.py:55
  545.9 16.6 %copy.107 = f32[16,4,1024,4]{3,2,1,0:T(8,128)} copy(f32[16,4,1024,4]{2,1,0,3:T(4,128)S(1)} %add_bitcast_fusion) | data formatting | bytes 2097152 | tf_op jit(solution)/shard_map/transpose | solution.py:55
  562.5 33.6 %reshape.100 = f32[64,4096]{1,0:T(8,128)} reshape(f32[16,4,1024,4]{3,2,1,0:T(8,128)} %copy.107) | data formatting | bytes 2097152 | tf_op jit(solution)/shard_map/reshape | solution.py:55
  (92 shorter events, 144.8 us)
Async XLA Ops:
  7.2 14.0 %copy-start = (f32[4]{0:T(128)S(1)}, f32[4]{0:T(128)}, u32[]{:S(2)}) copy-start(f32[4]{0:T(128)} %param.11) | copy-start | bytes 52
  7.2 13.1 %copy-start.7 = (s32[2,32]{1,0:T(2,128)S(1)}, s32[2,32]{1,0:T(2,128)}, u32[]{:S(2)}) copy-start(s32[2,32]{1,0:T(2,128)} %param.7) | copy-start | bytes 772
  7.2 13.1 %copy-start.6 = (f32[8,5,5]{2,0,1:T(8,128)S(1)}, f32[8,5,5]{2,0,1:T(8,128)}, u32[]{:S(2)}) copy-start(f32[8,5,5]{2,0,1:T(8,128)} %param.10) | copy-start | bytes 2404
  7.2 13.3 %copy-start.8 = (s32[1,32]{1,0:T(1,128)S(1)}, s32[1,32]{1,0:T(1,128)}, u32[]{:S(2)}) copy-start(s32[1,32]{1,0:T(1,128)} %param.8) | copy-start | bytes 388
  7.2 14.0 %copy-start.9 = (s32[1,32]{1,0:T(1,128)S(1)}, s32[1,32]{1,0:T(1,128)}, u32[]{:S(2)}) copy-start(s32[1,32]{1,0:T(1,128)} %param.9) | copy-start | bytes 388
  7.2 86.2 %all-reduce.10.cloned.1.call-start = ((), (), s32[]{:S(2)}) async-start(), calls=%async_computation | async-start | bytes 4194304 | tf_op jit(solution)/shard_map/psum | solution.py:106
  11.9 2.0 copy-start.5
  13.9 16.0 %collective-permute-start = (f32[32,1,2048]{2,0,1:T(8,128)S(1)}, f32[32,1,2048]{2,0,1:T(8,128)S(1)}, u32[]{:S(2)}, u32[]{:S(2)}) collective-permute-start(f32[32,1,2048]{2,0,1:T(8,128)S(1)} %get-tuple-element.54), channel_id=1, source_target_pairs={{0,2},{2,4},{4,6},{6,8},{8,10},{10,12},{12,14},{1,3},{3,5},{5,7},{... | collective-permute-start | bytes 786440 | tf_op jit(solution)/shard_map/ppermute | solution.py:21
  18.8 11.2 %collective-permute-start.1 = (f32[32,1,2048]{2,0,1:T(8,128)S(1)}, f32[32,1,2048]{2,0,1:T(8,128)S(1)}, u32[]{:S(2)}, u32[]{:S(2)}) collective-permute-start(f32[32,1,2048]{2,0,1:T(8,128)S(1)} %get-tuple-element.55), channel_id=1, source_target_pairs={{2,0},{4,2},{6,4},{8,6},{10,8},{12,10},{14,12},{3,1},{5,3},{7,5},{... | collective-permute-start | bytes 786440 | tf_op jit(solution)/shard_map/ppermute | solution.py:23
  69.9 163.9 %all-reduce.12.cloned.1.call-start = ((), (), s32[]{:S(2)}) async-start(), calls=%async_computation.1 | async-start | bytes 4194304 | tf_op jit(solution)/shard_map/psum | solution.py:106
  94.5 15.3 %collective-permute-start.2 = (f32[4,4,2,2048]{3,0,2,1:T(4,128)S(1)}, f32[4,4,2,2048]{3,0,2,1:T(4,128)S(1)}, u32[]{:S(2)}, u32[]{:S(2)}) collective-permute-start(f32[4,4,2,2048]{3,0,2,1:T(4,128)S(1)} %get-tuple-element.190), channel_id=1, source_target_pairs={{0,2},{2,4},{4,6},{6,8},{8,10},{10,12},{12,14},{1,3},{3,5},{5,7},{... | collective-permute-start | bytes 786440 | tf_op jit(solution)/shard_map/ppermute | solution.py:21
  98.2 14.8 %collective-permute-start.3 = (f32[4,4,2,2048]{3,0,2,1:T(4,128)S(1)}, f32[4,4,2,2048]{3,0,2,1:T(4,128)S(1)}, u32[]{:S(2)}, u32[]{:S(2)}) collective-permute-start(f32[4,4,2,2048]{3,0,2,1:T(4,128)S(1)} %get-tuple-element.189), channel_id=1, source_target_pairs={{2,0},{4,2},{6,4},{8,6},{10,8},{12,10},{14,12},{3,1},{5,3},{7,5},{... | collective-permute-start | bytes 786440 | tf_op jit(solution)/shard_map/ppermute | solution.py:23
  208.8 25.1 %copy-start.2 = (f32[4,4,16,2048]{3,0,2,1:T(4,128)S(1)}, f32[4,4,16,2048]{3,0,2,1:T(4,128)}, u32[]{:S(2)}) copy-start(f32[4,4,16,2048]{3,0,2,1:T(4,128)} %all-reduce.10.cloned.1.call-done) | copy-start | bytes 6291460
  211.5 239.4 %all-reduce.14.cloned.1.call-start = ((), (), s32[]{:S(2)}) async-start(), calls=%async_computation.2 | async-start | bytes 4194304 | tf_op jit(solution)/shard_map/psum | solution.py:106
  276.2 1.3 copy-start.3
  313.4 12.8 %collective-permute-start.4 = (f32[4,4,2,2048]{3,0,2,1:T(4,128)S(1)}, f32[4,4,2,2048]{3,0,2,1:T(4,128)S(1)}, u32[]{:S(2)}, u32[]{:S(2)}) collective-permute-start(f32[4,4,2,2048]{3,0,2,1:T(4,128)S(1)} %get-tuple-element.184), channel_id=1, source_target_pairs={{0,2},{2,4},{4,6},{6,8},{8,10},{10,12},{12,14},{1,3},{3,5},{5,7},{... | collective-permute-start | bytes 786440 | tf_op jit(solution)/shard_map/ppermute | solution.py:21
  314.8 11.5 %collective-permute-start.5 = (f32[4,4,2,2048]{3,0,2,1:T(4,128)S(1)}, f32[4,4,2,2048]{3,0,2,1:T(4,128)S(1)}, u32[]{:S(2)}, u32[]{:S(2)}) collective-permute-start(f32[4,4,2,2048]{3,0,2,1:T(4,128)S(1)} %get-tuple-element.185), channel_id=1, source_target_pairs={{2,0},{4,2},{6,4},{8,6},{10,8},{12,10},{14,12},{3,1},{5,3},{7,5},{... | collective-permute-start | bytes 786440 | tf_op jit(solution)/shard_map/ppermute | solution.py:23
  453.5 1.3 copy-start.4
  562.5 33.6 %copy-start.1 = (f32[4]{0:T(128)S(1)}, f32[4]{0:T(128)}, u32[]{:S(2)}) copy-start(f32[4]{0:T(128)} %param.11) | copy-start | bytes 52
Sparse Core Ops, SparseCore 0:
  70.0 23.3 all-reduce.9
  211.6 22.2 all-reduce.11
  430.5 20.3 all-reduce.13
where the time goes:
time: 613 us; the launch traced here: 603 us
  local copies, waits for them, and re-layouts  256 us (42%)
  blocking collectives  99.1 us (16%)
  waiting for transfers between devices  94.9 us (15%)
  other arithmetic  76.1 us (12%)
  matrix products  44 us (7%)
  between operations  18.3 us (3%)
  starting transfers between devices  14 us (2%)
    another operation x10, local copies, waits for them, and re-layouts, forward_cells(): jnp.stack([extended[pr, pc, 1 + qr:1 + qr + count, 1 + qc:1 + qc + width]...  108 us
    reshape x2, local copies, waits for them, and re-layouts, unphase(): field.transpose(2, 0, 3, 1).reshape(4 * field.shape[2], 4 * field.shape[3])  67.2 us
    psum x3, waiting for transfers between devices, combine(): return lax.psum(partial_value, 'frame')  66.3 us
    psum x2, blocking collectives, squares(): return lax.psum(jnp.sum(part * part), ('tile', 'frame'))  64.6 us
    add x12, other arithmetic, adjoint_cells(): total + mixed[tr * 8 + tc, 1 - qr:1 - qr + count, 1 - qc:1 - qc + quarter]  52.5 us
    psum x1, blocking collectives, per_device(): lax.psum(jnp.sum(own_part(direction) * own_part(image)), ('tile', 'frame'))  34.5 us
    transpose x2, local copies, waits for them, and re-layouts, unphase(): field.transpose(2, 0, 3, 1).reshape(4 * field.shape[2], 4 * field.shape[3])  33.3 us
    ppermute x3, waiting for transfers between devices, padded_2(): lax.ppermute(tail, axis, [(i, (i + 1) % count) for i in range(ends)])  28.6 us
  transfers between devices with their start and end apart: 9, of which 6 were waited for; matrix products, arithmetic and copies ran while one was open for 1% of the time, Pallas kernels for 0%

commit v1 on v0

v1 whole, which is shorter than its diff:
```python
import functools

import jax
import jax.numpy as jnp
from jax import lax
from jax.experimental import pallas as pl
from jax.experimental.pallas import tpu as pltpu
from jax.sharding import PartitionSpec as P

DAMPING = 0.3
LANES = 128
HIGHEST = lax.Precision.HIGHEST
NT = (((1,), (1,)), ((), ()))
F32, BF16, I32 = jnp.float32, jnp.bfloat16, jnp.int32


def split(x):
    high = x.astype(BF16)
    return high, (x - high.astype(F32)).astype(BF16)


def paired(table):
    high, low = split(table)
    second = (lax.broadcasted_iota(I32, table.shape, 1) >> 5) & 1
    return jnp.concatenate([high, jnp.where(second == 0, low.astype(F32), 0.0).astype(BF16)], axis=0)


def row_phase(shape):
    return lax.broadcasted_iota(I32, shape, 0) & 3


def tap_table(shift, ids, members, kernels, gains):
    frames = shift.shape[1]
    copies = LANES // frames

    def tiled(x):
        return jnp.concatenate([x] * copies, axis=1)

    shape = (32, LANES)
    place = lax.broadcasted_iota(I32, shape, 0)
    lane = lax.broadcasted_iota(I32, shape, 1)
    group = place >> 3
    first = jnp.where(group == 0, 2, jnp.where(group == 1, 4, jnp.where(group == 2, 0, 6)))
    col = first + ((place >> 2) & 1)
    row = 2 + 4 * ((lane >> 5) - 1) + (place & 3)
    up = row - tiled(shift[0:1, :])
    along = col - tiled(shift[1:2, :])
    kind = tiled(ids[...])
    member = tiled(members[...])
    inside = (row >= 0) & (row < 8) & (up >= 0) & (up < 5) & (along >= 0) & (along < 5)
    count = kernels.shape[1]
    code = jnp.where(inside, kind * 25 + up * 5 + along, -1)
    total = jnp.zeros(shape, F32)
    for n in range(count):
        for a in range(5):
            for b in range(5):
                total = jnp.where(code == n * 25 + a * 5 + b, kernels[a, n, b], total)
    scale = jnp.zeros((1, LANES), F32)
    for g in range(gains.shape[0]):
        scale = jnp.where(member == g, gains[g], scale)
    return total * scale


def adjoint_kernel(shift, ids, members, kernels, gains, obs, own, send, landed, stack, mixed, sems):
    wide = obs.shape[1]
    frames = shift.shape[1]
    count = obs.shape[0] // frames
    half = wide // 2
    blocks = wide // LANES
    me = lax.axis_index("frame")

    def load(c):
        return pltpu.make_async_copy(
            obs.at[:, pl.ds(c * LANES, LANES)], landed.at[c], sems.at[c]
        )

    for c in range(blocks):
        load(c).start()
    table = tap_table(shift, ids, members, kernels, gains)
    for r in range(4):
        own[17 * 16 : 17 * 16 + 8, r * LANES : (r + 1) * LANES] = table[8 * r : 8 * r + 8]
        send[17 * 16 : 17 * 16 + 8, r * LANES : (r + 1) * LANES] = table[8 * r : 8 * r + 8]
    rest = own.shape[1] - 4 * LANES
    if rest > 0:
        own[17 * 16 : 17 * 16 + 8, 4 * LANES :] = jnp.zeros((8, rest), F32)
        send[17 * 16 : 17 * 16 + 8, 4 * LANES :] = jnp.zeros((8, rest), F32)
    source = lax.broadcasted_iota(I32, (LANES, 192), 0)
    target = lax.broadcasted_iota(I32, (LANES, 192), 1)
    pick = (source == (2 - (target >> 6)) * 32 + (target & 31)).astype(F32)
    left = paired(jnp.dot(table, pick, precision=HIGHEST, preferred_element_type=F32))

    nothing = jnp.zeros((128, wide), BF16)
    stack[0:128, :] = nothing
    stack[(count + 2) * 64 : (count + 4) * 64, :] = nothing
    for c in range(0, blocks, 2):
        load(c).wait()
        load(c + 1).wait()
        for r in range(count):
            for d in range(2):
                high, low = split(landed[c + d, pl.ds(r, frames, stride=count), :])
                cols = slice((c + d) * LANES, (c + d + 1) * LANES)
                stack[(r + 2) * 64 : (r + 2) * 64 + 32, cols] = high
                stack[(r + 2) * 64 + 32 : (r + 3) * 64, cols] = low
        cols = slice(c * LANES, (c + 2) * LANES)
        for r in range(count + 2):
            both = jnp.dot(left, stack[r * 64 : (r + 3) * 64, cols], preferred_element_type=F32)
            mixed[r * 32 : r * 32 + 32, cols] = both[:32] + both[32:]

    lane = lax.broadcasted_iota(I32, (8, wide), 1)
    near = lax.broadcasted_iota(I32, (8, LANES), 1) < 64

    def moved(r):
        t = mixed[r * 32 : r * 32 + 32, :]
        low = t[0:8] + jnp.where(lane == 0, 0.0, pltpu.roll(t[24:32], 1, 1))
        high = t[8:16] + jnp.where(lane == wide - 1, 0.0, pltpu.roll(t[16:24], wide - 1, 1))
        return low, high

    def put(at, value):
        first, second = value[:, :half], value[:, half:]
        own[at : at + 8, :half] = jnp.where(me == 0, first, second)
        send[at : at + 8, :half] = jnp.where(me == 0, second, first)
        first = jnp.where(near, value[:, half : half + LANES], 0.0)
        second = jnp.where(near, 0.0, value[:, half - LANES : half])
        own[at : at + 8, half:] = jnp.where(me == 0, first, second)
        send[at : at + 8, half:] = jnp.where(me == 0, second, first)

    for r in range(1, count + 1):
        low, high = moved(r)
        put((r - 1) * 16, low)
        put((r - 1) * 16 + 8, high)
    above, below = moved(0), moved(count + 1)
    put(count * 16, above[0] + below[0])
    put(count * 16 + 8, above[1] + below[1])


def border_kernel(own, other, first, second):
    count = (own.shape[0] - 24) // 16
    even = lax.rem(lax.axis_index("tile"), 2) == 0
    edge = own[count * 16 : count * 16 + 16] + other[count * 16 : count * 16 + 16]
    phase = row_phase((8, own.shape[1]))
    above = jnp.where(phase >= 2, edge[0:8], pltpu.roll(edge[8:16], 6, 0))
    below = jnp.where(phase < 2, edge[0:8], pltpu.roll(edge[8:16], 2, 0))
    top = own[0:32] + other[0:32]
    bottom = own[(count - 2) * 16 : count * 16] + other[(count - 2) * 16 : count * 16]
    first[0:32] = jnp.where(even, bottom, top)
    first[32:40] = jnp.where(even, below, above)
    second[0:32] = jnp.where(even, top, bottom)
    second[32:40] = jnp.where(even, above, below)


def operator_kernel(own, other, first, second, base, once, twice, sums, held, later, stack):
    ext = own.shape[1]
    half = ext - LANES
    count = (own.shape[0] - 24) // 16
    tile, tiles = lax.axis_index("tile"), lax.axis_size("tile")
    me = lax.axis_index("frame")
    even = lax.rem(tile, 2) == 0
    has_up = jnp.where(tile > 0, 1.0, 0.0).astype(F32)
    has_down = jnp.where(tile < tiles - 1, 1.0, 0.0).astype(F32)

    def both_tables(r):
        a = own[(count + 1) * 16 : (count + 1) * 16 + 8, r * LANES : (r + 1) * LANES]
        b = other[(count + 1) * 16 : (count + 1) * 16 + 8, r * LANES : (r + 1) * LANES]
        return a, b

    pieces = [both_tables(r) for r in range(4)]
    tables = [jnp.concatenate([p[d] for p in pieces], axis=0) for d in range(2)]
    earlier = [pltpu.roll(t, 32, 1) for t in tables]
    after = [pltpu.roll(t, LANES - 32, 1) for t in tables]
    block = lax.broadcasted_iota(I32, (32, LANES), 1) >> 5
    left = jnp.concatenate(
        [jnp.concatenate([t, jnp.where(block == 2, t, 0.0), jnp.where(block == 0, t, 0.0)], axis=0) for t in tables],
        axis=1,
    )
    right = jnp.concatenate(
        [jnp.concatenate([e, e, t, t, a, a], axis=0) for e, t, a in zip(earlier, tables, after)], axis=1
    )
    product = lax.dot_general(left, right, NT, precision=HIGHEST, preferred_element_type=F32)
    middle = (lax.broadcasted_iota(I32, (32, 192), 1) >> 6) == 1
    full = product[0:32]
    plain = paired(full)
    at_top = paired(full - (1.0 - has_up) * jnp.where(middle, product[32:64], 0.0))
    at_bottom = paired(full - (1.0 - has_down) * jnp.where(middle, product[64:96], 0.0))

    lane = lax.broadcasted_iota(I32, (8, LANES), 1)
    near = jnp.where(me == 0, jnp.where(lane < 64, 1.0, 0.0), jnp.where(lane < 64, 0.0, 1.0)).astype(F32)
    phase = row_phase((8, ext))

    def widen(value):
        return jnp.concatenate([value, value], axis=0)

    edge = own[count * 16 : count * 16 + 16] + other[count * 16 : count * 16 + 16]
    phase2 = row_phase((16, ext))
    up = jnp.where(even, second[...], first[...])
    down = jnp.where(even, first[...], second[...])
    held[0:16] = up[0:16]
    held[16:32] = up[16:32] + has_up * jnp.where(phase2 >= 2, edge, 0.0)
    for r in range(count):
        value = own[r * 16 : r * 16 + 16] + other[r * 16 : r * 16 + 16]
        if r == 0:
            e = up[32:40]
            value = value + jnp.where(phase2 < 2, jnp.concatenate([e, pltpu.roll(e, 6, 0)], axis=0), 0.0)
        if r == count - 1:
            e = down[32:40]
            value = value + jnp.where(phase2 >= 2, jnp.concatenate([e, pltpu.roll(e, 2, 0)], axis=0), 0.0)
        held[(r + 2) * 16 : (r + 3) * 16] = value
    held[(count + 2) * 16 : (count + 3) * 16] = down[0:16] + has_down * jnp.where(phase2 < 2, edge, 0.0)
    held[(count + 3) * 16 : (count + 4) * 16] = down[16:32]

    def expand(field, r):
        low, high = field[r * 16 : r * 16 + 8], field[r * 16 + 8 : r * 16 + 16]
        groups = jnp.concatenate([low, high, pltpu.roll(high, 1, 1), pltpu.roll(low, ext - 1, 1)], axis=0)
        a, b = split(groups)
        stack[r * 64 : r * 64 + 32] = a
        stack[r * 64 + 32 : r * 64 + 64] = b

    def masked(t):
        return jnp.concatenate([t[:, :half], t[:, half:] * near], axis=1)

    def apply(weights, field, r):
        both = jnp.dot(weights, stack[(r - 1) * 64 : (r + 2) * 64], preferred_element_type=F32)
        t = both[:32] + both[32:]
        low = t[0:8] + pltpu.roll(masked(t[24:32]), 1, 1)
        high = t[8:16] + pltpu.roll(masked(t[16:24]), ext - 1, 1)
        low = masked(low + DAMPING * field[r * 16 : r * 16 + 8])
        high = masked(high + DAMPING * field[r * 16 + 8 : r * 16 + 16])
        return jnp.concatenate([low, high], axis=0)

    def weights_of(r):
        return at_top if r == 0 else at_bottom if r == count - 1 else plain

    def folded(value):
        total = value[0:8, 0:LANES] + value[8:16, 0:LANES]
        for c in range(1, half // LANES):
            total = total + (value[0:8, c * LANES : (c + 1) * LANES] + value[8:16, c * LANES : (c + 1) * LANES])
        return total

    for r in range(count + 4):
        expand(held, r)
    totals = [jnp.zeros((8, LANES), F32) for _ in range(4)]
    for r in range(-1, count + 1):
        value = apply(weights_of(r), held, r + 2)
        if r == -1:
            value = value * has_up
        if r == count:
            value = value * has_down
        later[(r + 1) * 16 : (r + 2) * 16] = value
        if 0 <= r < count:
            once[r * 16 : r * 16 + 16] = value[:, :half]
            b = held[(r + 2) * 16 : (r + 3) * 16, :half]
            base[r * 16 : r * 16 + 16] = b
            totals[0] += folded(b * b)
            totals[1] += folded(b * value[:, :half])
            totals[2] += folded(value[:, :half] * value[:, :half])
    for r in range(count + 2):
        expand(later, r)
    for r in range(count):
        value = apply(weights_of(r), later, r + 1)[:, :half]
        twice[r * 16 : r * 16 + 16] = value
        totals[3] += folded(value * later[(r + 1) * 16 : (r + 2) * 16, :half])
    rows = jnp.concatenate([jnp.sum(t, axis=0, keepdims=True) for t in totals], axis=0)
    rows = jnp.concatenate([rows, jnp.zeros((4, LANES), F32)], axis=0)
    for p in range(sums.shape[0]):
        sums[p] = rows


def update_kernel(base, once, twice, sums, solution, residual, spread):
    @pl.when(pl.program_id(0) == 0)
    def _():
        source = lax.broadcasted_iota(I32, spread.shape, 0)
        target = lax.broadcasted_iota(I32, spread.shape, 1)
        hit = target == 4 * (source & (LANES - 1)) + (source >> 7)
        spread[...] = jnp.where(hit, 1.0, 0.0).astype(BF16)

    lanes = jnp.sum(sums[...], axis=0)

    def total(at):
        return jnp.sum(lanes[at : at + 1], axis=1, keepdims=True)

    bb, bm, mm, mmm = [total(at) for at in range(4)]
    alpha = bb / bm
    norm = alpha * alpha * mm - 2.0 * alpha * bm + bb
    beta = norm / bb
    grow = 1.0 + beta
    product = grow * grow * bm - 2.0 * grow * alpha * mm + alpha * alpha * mmm
    step = norm / product
    count = base.shape[0] // 16
    side = lax.broadcasted_iota(I32, (count // 2, 8, LANES), 1) < 4

    def arranged(x):
        x = x.reshape(count // 2, 4, 8, LANES)
        pieces = []
        for g in range(2):
            a, b = x[:, g], x[:, g + 2]
            pieces.append(jnp.where(side, a, pltpu.roll(b, 4, 1)).reshape(4 * count, LANES))
            pieces.append(jnp.where(side, pltpu.roll(a, 4, 1), b).reshape(4 * count, LANES))
        return split(jnp.concatenate(pieces, axis=1))

    for c in range(base.shape[1] // LANES):
        cols = slice(c * LANES, (c + 1) * LANES)
        b, m, mm_ = base[:, cols], once[:, cols], twice[:, cols]
        x = (alpha + step * grow) * b - (step * alpha) * m
        r = (b - alpha * m) - step * (grow * m - alpha * mm_)
        xh, xl = arranged(x)
        rh, rl = arranged(r)
        out = jnp.dot(jnp.concatenate([xh, xl, rh, rl], axis=0), spread[...], preferred_element_type=F32)
        n = 4 * count
        wide = slice(4 * c * LANES, 4 * (c + 1) * LANES)
        solution[:, wide] = out[0:n] + out[n : 2 * n]
        residual[:, wide] = out[2 * n : 3 * n] + out[3 * n : 4 * n]


def params():
    return pltpu.CompilerParams(vmem_limit_bytes=48 * 1024 * 1024)


def vmem(n):
    return [pl.BlockSpec(memory_space=pltpu.VMEM)] * n


def per_device(observed, frame_shift, kernel_ids, groups, kernels, gains):
    frames, count, wide = observed.shape
    half = wide // 2
    ext = half + LANES
    blocks = wide // LANES
    tiles, spread = lax.axis_size("tile"), lax.axis_size("frame")
    rows = (count + 1) * 16 + 8
    smem = pl.BlockSpec(memory_space=pltpu.SMEM)
    shape = jax.ShapeDtypeStruct

    own, send = pl.pallas_call(
        adjoint_kernel,
        out_shape=(shape((rows, ext), F32),) * 2,
        in_specs=vmem(3) + [smem, smem, pl.BlockSpec(memory_space=pl.ANY)],
        out_specs=tuple(vmem(2)),
        scratch_shapes=[
            pltpu.VMEM((blocks, frames * count, LANES), F32),
            pltpu.VMEM(((count + 4) * 64, wide), BF16),
            pltpu.VMEM(((count + 2) * 32, wide), F32),
            pltpu.SemaphoreType.DMA((blocks,)),
        ],
        compiler_params=params(),
        name="adjoint",
    )(frame_shift, kernel_ids, groups, kernels.transpose(1, 0, 2), gains, observed.reshape(frames * count, wide))
    other = lax.ppermute(send, "frame", [(0, 1), (1, 0)])

    first, second = pl.pallas_call(
        border_kernel,
        out_shape=(shape((40, ext), F32),) * 2,
        in_specs=vmem(2),
        out_specs=tuple(vmem(2)),
        compiler_params=params(),
        name="border",
    )(own, other)
    pairs = [(i, i ^ 1) for i in range(tiles) if i ^ 1 < tiles]
    odd_pairs = [p for i in range(1, tiles - 1, 2) for p in ((i, i + 1), (i + 1, i))]
    second = lax.ppermute(second, "tile", odd_pairs)
    first = lax.ppermute(first, "tile", pairs)

    peers = tiles * spread
    base, once, twice, sums = pl.pallas_call(
        operator_kernel,
        out_shape=(shape((count * 16, half), F32),) * 3 + (shape((peers, 8, LANES), F32),),
        in_specs=vmem(4),
        out_specs=tuple(vmem(4)),
        scratch_shapes=[
            pltpu.VMEM(((count + 4) * 16, ext), F32),
            pltpu.VMEM(((count + 2) * 16, ext), F32),
            pltpu.VMEM(((count + 4) * 64, ext), BF16),
        ],
        compiler_params=params(),
        name="operator",
    )(own, other, first, second)
    sums = lax.all_to_all(sums, ("tile", "frame"), 0, 0)

    steps = 4 if half % (4 * LANES) == 0 else 1
    part = half // steps
    solution, residual = pl.pallas_call(
        update_kernel,
        grid=(steps,),
        out_shape=(shape((count * 4, 4 * half), F32),) * 2,
        in_specs=[pl.BlockSpec((count * 16, part), lambda j: (0, j))] * 3
        + [pl.BlockSpec((peers, 8, LANES), lambda j: (0, 0, 0))],
        out_specs=(pl.BlockSpec((count * 4, 4 * part), lambda j: (0, j)),) * 2,
        scratch_shapes=[pltpu.VMEM((4 * LANES, 4 * LANES), BF16)],
        compiler_params=params(),
        name="update",
    )(base, once, twice, sums)
    return solution, residual


def solution(mesh):
    return jax.shard_map(
        per_device,
        mesh=mesh,
        in_specs=(
            P("frame", ("scene", "tile"), None),
            P("scene", "frame"),
            P("scene", "frame"),
            P("scene", "frame"),
            P(),
            P(),
        ),
        out_specs=(P(("scene", "tile"), "frame"), P(("scene", "tile"), "frame")),
        check_vma=False,
    )
```

time: 613 us -> 45.8 us (0.07); the launches traced: 603 us -> 45.5 us
  local copies, waits for them, and re-layouts: 256 us -> 3.36 us
  blocking collectives: 99.1 us -> 12.7 us
  waiting for transfers between devices: 94.9 us -> 10.1 us
  other arithmetic: 76.1 us -> 0 us
  matrix products: 44 us -> 0 us
  between operations: 18.3 us -> 0.67 us
  Pallas kernels: 0 us -> 14.5 us
  starting transfers between devices: 14 us -> 4.13 us
    another operation x15 -> x0, local copies, waits for them, and re-layouts: 131 us -> none  [the longest x10 108 us: forward_cells(): jnp.stack([extended[pr, pc, 1 + qr:1 + qr + count, 1 + qc:1 + qc + width]...]
    psum x3 -> x0, blocking collectives: 99.1 us -> none  [the longest x2 64.6 us: squares(): return lax.psum(jnp.sum(part * part), ('tile', 'frame'))]
    reshape x7 -> x0, local copies, waits for them, and re-layouts: 78.5 us -> none  [the longest x2 67.2 us: unphase(): field.transpose(2, 0, 3, 1).reshape(4 * field.shape[2], 4 * field.shape[3])]
    psum x3 -> x0, waiting for transfers between devices: 66.3 us -> none  [combine(): return lax.psum(partial_value, 'frame')]
    add x15 -> x0, other arithmetic: 61 us -> none  [the longest x12 52.5 us: adjoint_cells(): total + mixed[tr * 8 + tc, 1 - qr:1 - qr + count, 1 - qc:1 - qc + quarter]]
    dot_general x9 -> x0, matrix products: 44 us -> none  [the longest x3 27.5 us: adjoint_cells(): jnp.einsum('kt,kij->tij', weights, padded, precision=lax.Precision.HIGHEST)]
    transpose x2 -> x0, local copies, waits for them, and re-layouts: 33.3 us -> none  [unphase(): field.transpose(2, 0, 3, 1).reshape(4 * field.shape[2], 4 * field.shape[3])]
    ppermute x6 -> x3, waiting for transfers between devices: 28.6 us -> 10.1 us  [the longest x1 7.48 us: per_device(): first = lax.ppermute(first, 'tile', pairs)]
  transfers between devices with their start and end apart: 9 -> 3, of which waited for: 6 -> 2; matrix products, arithmetic and copies ran while one was open for 1% -> 0% of each run, Pallas kernels for 0% -> 0%
where the time goes in v1:
time: 45.8 us; the launch traced here: 45.5 us
  Pallas kernels  14.5 us (32%)
  blocking collectives  12.7 us (28%)
  waiting for transfers between devices  10.1 us (22%)
  starting transfers between devices  4.13 us (9%)
  local copies, waits for them, and re-layouts  3.36 us (7%)
  between operations  0.67 us (1%)
    all_to_all x1, blocking collectives, per_device(): sums = lax.all_to_all(sums, ('tile', 'frame'), 0, 0)  12.7 us
    ppermute x1, waiting for transfers between devices, per_device(): first = lax.ppermute(first, 'tile', pairs)  7.48 us
    pallas_call x1, Pallas kernels, per_device(): pl.pallas_call(adjoint_kernel, out_shape=(shape((rows, ext), F32),) * 2,...  6.81 us
    pallas_call x1, Pallas kernels, per_device(): pl.pallas_call(operator_kernel, out_shape=(shape((count * 16, half), F32)...  4.07 us
    pallas_call x1, Pallas kernels, per_device(): pl.pallas_call(update_kernel, grid=(steps,), out_shape=(shape((count * 4,...  3.62 us
    unnamed x10, local copies, waits for them, and re-layouts  3.36 us
    ppermute x1, starting transfers between devices, per_device(): first = lax.ppermute(first, 'tile', pairs)  2.97 us
    ppermute x1, waiting for transfers between devices, per_device(): other = lax.ppermute(send, 'frame', [(0, 1), (1, 0)])  2.63 us
  transfers between devices with their start and end apart: 3, of which 2 were waited for; matrix products, arithmetic and copies ran while one was open for 0% of the time, Pallas kernels for 0%

profile of v1, /device:TPU:0, one launch (start us, length us, event | category | flops | bytes accessed | tf_op | source)
XLA Modules:
  0.0 45.5 jit_solution(10447095471643483941)
XLA Ops:
  0.6 0.0 copy-start
  0.6 0.7 %copy-done = f32[8,5,5]{2,0,1:T(8,128)S(1)} copy-done((f32[8,5,5]{2,0,1:T(8,128)S(1)}, f32[8,5,5]{2,0,1:T(8,128)}, u32[]{:S(2)}) %copy-start) | copy-done | bytes 824
  1.4 0.0 copy-start.1
  1.4 0.7 %copy-done.1 = s32[2,32]{1,0:T(2,128)S(1)} copy-done((s32[2,32]{1,0:T(2,128)S(1)}, s32[2,32]{1,0:T(2,128)}, u32[]{:S(2)}) %copy-start.1) | copy-done | bytes 280
  2.0 0.0 copy-start.2
  2.0 0.7 %copy-done.2 = s32[1,32]{1,0:T(1,128)S(1)} copy-done((s32[1,32]{1,0:T(1,128)S(1)}, s32[1,32]{1,0:T(1,128)}, u32[]{:S(2)}) %copy-start.2) | copy-done | bytes 152
  2.7 0.0 copy-start.3
  2.7 0.7 %copy-done.3 = s32[1,32]{1,0:T(1,128)S(1)} copy-done((s32[1,32]{1,0:T(1,128)S(1)}, s32[1,32]{1,0:T(1,128)}, u32[]{:S(2)}) %copy-start.3) | copy-done | bytes 152
  3.4 0.0 copy-start.4
  3.4 0.7 %copy-done.4 = f32[4]{0:T(128)S(1)} copy-done((f32[4]{0:T(128)S(1)}, f32[4]{0:T(128)}, u32[]{:S(2)}) %copy-start.4) | copy-done | bytes 40
  4.0 6.8 %adjoint.1 = (f32[280,1152]{1,0:T(8,128)S(1)}, f32[280,1152]{1,0:T(8,128)S(1)}) custom-call(s32[2,32]{1,0:T(2,128)S(1)} %copy-done.1, s32[1,32]{1,0:T(1,128)S(1)} %copy-done.2, s32[1,32]{1,0:T(1,128)S(1)} %copy-done.3, f32[5,8,5]{2,1,0:T(8,128)S(1)} %bitcast.2, f32[4]{0:T(128)S(1)} %copy-done.4, f32[512,2048]{1,0:T(8,128)} %bitcast.3), custom_call_target="tpu_custom_call" | custom-call | tf_op jit(solution)/shard_map/adjoint/pallas_call | solution.py:331
  10.8 0.5 %collective-permute-start = (f32[280,1152]{1,0:T(8,128)S(1)}, f32[280,1152]{1,0:T(8,128)S(1)}, u32[]{:S(2)}, u32[]{:S(2)}) collective-permute-start(f32[280,1152]{1,0:T(8,128)S(1)} %get-tuple-element.11), channel_id=1, source_target_pairs={{0,1},{1,0},{2,3},{3,2},{4,5},{5,4},{6,7},{7,6},{8,9},{9,8},{10,11... | collective-permute-start | bytes 3870728 | tf_op jit(solution)/shard_map/ppermute | solution.py:345
  11.3 2.6 %collective-permute-done.other = f32[280,1152]{1,0:T(8,128)S(1)} collective-permute-done((f32[280,1152]{1,0:T(8,128)S(1)}, f32[280,1152]{1,0:T(8,128)S(1)}, u32[]{:S(2)}, u32[]{:S(2)}) %collective-permute-start) | collective-permute-done | bytes 1290272 | tf_op jit(solution)/shard_map/ppermute | solution.py:345
  14.0 3.0 %collective-permute-start.1 = (f32[40,1152]{1,0:T(8,128)S(1)}, f32[40,1152]{1,0:T(8,128)S(1)}, u32[]{:S(2)}, u32[]{:S(2)}) collective-permute-start(f32[40,1152]{1,0:T(8,128)S(1)} %get-tuple-element.12), channel_id=1, source_target_pairs={{0,2},{2,0},{4,6},{6,4},{8,10},{10,8},{12,14},{14,12},{1,3},{3,1},... | collective-permute-start | bytes 552968 | tf_op jit(solution)/shard_map/ppermute | solution.py:358
  17.0 0.7 %collective-permute-start.2 = (f32[40,1152]{1,0:T(8,128)S(1)}, f32[40,1152]{1,0:T(8,128)S(1)}, u32[]{:S(2)}, u32[]{:S(2)}) collective-permute-start(f32[40,1152]{1,0:T(8,128)S(1)} %get-tuple-element.13), channel_id=1, source_target_pairs={{2,4},{4,2},{6,8},{8,6},{10,12},{12,10},{3,5},{5,3},{7,9},{9,7},{1... | collective-permute-start | bytes 552968 | tf_op jit(solution)/shard_map/ppermute | solution.py:357
  17.7 7.5 %collective-permute-done.1.first = f32[40,1152]{1,0:T(8,128)S(1)} collective-permute-done((f32[40,1152]{1,0:T(8,128)S(1)}, f32[40,1152]{1,0:T(8,128)S(1)}, u32[]{:S(2)}, u32[]{:S(2)}) %collective-permute-start.1) | collective-permute-done | bytes 184352 | tf_op jit(solution)/shard_map/ppermute | solution.py:358
  25.1 0.0 collective-permute-done.2.second
  25.1 4.1 %operator.1 = (f32[256,1024]{1,0:T(8,128)S(1)}, f32[256,1024]{1,0:T(8,128)S(1)}, f32[256,1024]{1,0:T(8,128)S(1)}, f32[16,8,128]{2,1,0:T(8,128)S(1)}) custom-call(f32[280,1152]{1,0:T(8,128)S(1)} %get-tuple-element.10.own, f32[280,1152]{1,0:T(8,128)S(1)} %collective-permute-done.other, f32[40,1152]{1,0:T(8,128)S(1)} %collective-permute-done.1.first, ...), custom_call_target="tpu_custom_call" | custom-call | tf_op jit(solution)/shard_map/operator/pallas_call | solution.py:361
  29.2 12.7 %all_to_all.5.sums = f32[16,8,128]{2,1,0:T(8,128)S(1)} all-to-all(f32[16,8,128]{2,1,0:T(8,128)S(1)} %get-tuple-element.17), channel_id=1, replica_groups=mesh['scene'=2,'tile'=8,'frame'=2] {'tile','frame'}, dimensions={0} | all-to-all | bytes 131072 | tf_op jit(solution)/shard_map/all_to_all | solution.py:374
  41.9 3.6 %update.1 = (f32[64,4096]{1,0:T(8,128)}, f32[64,4096]{1,0:T(8,128)}) custom-call(f32[256,1024]{1,0:T(8,128)S(1)} %get-tuple-element.14.base, f32[256,1024]{1,0:T(8,128)S(1)} %get-tuple-element.15.once, f32[256,1024]{1,0:T(8,128)S(1)} %get-tuple-element.16.twice, f32[16,8,128]{2,1,0:T(8,128)S(1)} %all_to_all.5.sums), custom_call_target="tpu_custom_call" | custom-call | tf_op jit(solution)/shard_map/update/pallas_call | solution.py:378
  (1 shorter events, 0.0 us)
Async XLA Ops:
  0.6 0.7 %copy-start = (f32[8,5,5]{2,0,1:T(8,128)S(1)}, f32[8,5,5]{2,0,1:T(8,128)}, u32[]{:S(2)}) copy-start(f32[8,5,5]{2,0,1:T(8,128)} %param.10) | copy-start | bytes 2404
  1.4 0.7 %copy-start.1 = (s32[2,32]{1,0:T(2,128)S(1)}, s32[2,32]{1,0:T(2,128)}, u32[]{:S(2)}) copy-start(s32[2,32]{1,0:T(2,128)} %shift.1) | copy-start | bytes 772
  2.0 0.7 %copy-start.2 = (s32[1,32]{1,0:T(1,128)S(1)}, s32[1,32]{1,0:T(1,128)}, u32[]{:S(2)}) copy-start(s32[1,32]{1,0:T(1,128)} %ids.1) | copy-start | bytes 388
  2.7 0.7 %copy-start.3 = (s32[1,32]{1,0:T(1,128)S(1)}, s32[1,32]{1,0:T(1,128)}, u32[]{:S(2)}) copy-start(s32[1,32]{1,0:T(1,128)} %members.1) | copy-start | bytes 388
  3.4 0.7 %copy-start.4 = (f32[4]{0:T(128)S(1)}, f32[4]{0:T(128)}, u32[]{:S(2)}) copy-start(f32[4]{0:T(128)} %gains.1) | copy-start | bytes 52
  10.8 3.1 %collective-permute-start = (f32[280,1152]{1,0:T(8,128)S(1)}, f32[280,1152]{1,0:T(8,128)S(1)}, u32[]{:S(2)}, u32[]{:S(2)}) collective-permute-start(f32[280,1152]{1,0:T(8,128)S(1)} %get-tuple-element.11), channel_id=1, source_target_pairs={{0,1},{1,0},{2,3},{3,2},{4,5},{5,4},{6,7},{7,6},{8,9},{9,8},{10,11... | collective-permute-start | bytes 3870728 | tf_op jit(solution)/shard_map/ppermute | solution.py:345
  14.0 11.1 %collective-permute-start.1 = (f32[40,1152]{1,0:T(8,128)S(1)}, f32[40,1152]{1,0:T(8,128)S(1)}, u32[]{:S(2)}, u32[]{:S(2)}) collective-permute-start(f32[40,1152]{1,0:T(8,128)S(1)} %get-tuple-element.12), channel_id=1, source_target_pairs={{0,2},{2,0},{4,6},{6,4},{8,10},{10,8},{12,14},{14,12},{1,3},{3,1},... | collective-permute-start | bytes 552968 | tf_op jit(solution)/shard_map/ppermute | solution.py:358
  17.0 8.2 %collective-permute-start.2 = (f32[40,1152]{1,0:T(8,128)S(1)}, f32[40,1152]{1,0:T(8,128)S(1)}, u32[]{:S(2)}, u32[]{:S(2)}) collective-permute-start(f32[40,1152]{1,0:T(8,128)S(1)} %get-tuple-element.13), channel_id=1, source_target_pairs={{2,4},{4,2},{6,8},{8,6},{10,12},{12,10},{3,5},{5,3},{7,9},{9,7},{1... | collective-permute-start | bytes 552968 | tf_op jit(solution)/shard_map/ppermute | solution.py:357

commit v2 on v1

--- a/solution.py
+++ b/solution.py
@@ -61,7 +61,10 @@
     return total * scale
 
 
-def adjoint_kernel(shift, ids, members, kernels, gains, obs, own, send, landed, stack, mixed, sems):
+def adjoint_kernel(
+    far_shift, far_ids, far_members, far_kernels, far_gains, obs, own, send,
+    landed, stack, mixed, sems, shift, ids, members, kernels, gains, small_sems,
+):
     wide = obs.shape[1]
     frames = shift.shape[1]
     count = obs.shape[0] // frames
@@ -74,8 +77,18 @@
             obs.at[:, pl.ds(c * LANES, LANES)], landed.at[c], sems.at[c]
         )
 
+    small = [
+        pltpu.make_async_copy(far, near, small_sems.at[i])
+        for i, (far, near) in enumerate(
+            [(far_kernels, kernels), (far_gains, gains), (far_shift, shift), (far_ids, ids), (far_members, members)]
+        )
+    ]
+    for copy in small:
+        copy.start()
     for c in range(blocks):
         load(c).start()
+    for copy in small:
+        copy.wait()
     table = tap_table(shift, ids, members, kernels, gains)
     for r in range(4):
         own[17 * 16 : 17 * 16 + 8, r * LANES : (r + 1) * LANES] = table[8 * r : 8 * r + 8]
@@ -148,7 +161,7 @@
     second[32:40] = jnp.where(even, above, below)
 
 
-def operator_kernel(own, other, first, second, base, once, twice, sums, held, later, stack):
+def operator_kernel(own, other, first, second, base, once, twice, spread, sums, held, later, stack):
     ext = own.shape[1]
     half = ext - LANES
     count = (own.shape[0] - 24) // 16
@@ -182,6 +195,10 @@
     at_top = paired(full - (1.0 - has_up) * jnp.where(middle, product[32:64], 0.0))
     at_bottom = paired(full - (1.0 - has_down) * jnp.where(middle, product[64:96], 0.0))
 
+    source = lax.broadcasted_iota(I32, spread.shape, 0)
+    target = lax.broadcasted_iota(I32, spread.shape, 1)
+    hit = target == 4 * (source & (LANES - 1)) + (source >> 7)
+    spread[...] = jnp.where(hit, 1.0, 0.0).astype(BF16)
     lane = lax.broadcasted_iota(I32, (8, LANES), 1)
     near = jnp.where(me == 0, jnp.where(lane < 64, 1.0, 0.0), jnp.where(lane < 64, 0.0, 1.0)).astype(F32)
     phase = row_phase((8, ext))
@@ -264,14 +281,7 @@
         sums[p] = rows
 
 
-def update_kernel(base, once, twice, sums, solution, residual, spread):
-    @pl.when(pl.program_id(0) == 0)
-    def _():
-        source = lax.broadcasted_iota(I32, spread.shape, 0)
-        target = lax.broadcasted_iota(I32, spread.shape, 1)
-        hit = target == 4 * (source & (LANES - 1)) + (source >> 7)
-        spread[...] = jnp.where(hit, 1.0, 0.0).astype(BF16)
-
+def update_kernel(base, once, twice, spread, sums, solution, residual, near_x, near_r, sems):
     lanes = jnp.sum(sums[...], axis=0)
 
     def total(at):
@@ -295,6 +305,13 @@
             pieces.append(jnp.where(side, a, pltpu.roll(b, 4, 1)).reshape(4 * count, LANES))
             pieces.append(jnp.where(side, pltpu.roll(a, 4, 1), b).reshape(4 * count, LANES))
         return split(jnp.concatenate(pieces, axis=1))
+
+    def stores(c):
+        wide = pl.ds(4 * c * LANES, 4 * LANES)
+        return [
+            pltpu.make_async_copy(near.at[:, wide], far.at[:, wide], sems.at[i, c])
+            for i, (near, far) in enumerate([(near_x, solution), (near_r, residual)])
+        ]
 
     for c in range(base.shape[1] // LANES):
         cols = slice(c * LANES, (c + 1) * LANES)
@@ -306,12 +323,17 @@
         out = jnp.dot(jnp.concatenate([xh, xl, rh, rl], axis=0), spread[...], preferred_element_type=F32)
         n = 4 * count
         wide = slice(4 * c * LANES, 4 * (c + 1) * LANES)
-        solution[:, wide] = out[0:n] + out[n : 2 * n]
-        residual[:, wide] = out[2 * n : 3 * n] + out[3 * n : 4 * n]
-
-
-def params():
-    return pltpu.CompilerParams(vmem_limit_bytes=48 * 1024 * 1024)
+        near_x[:, wide] = out[0:n] + out[n : 2 * n]
+        near_r[:, wide] = out[2 * n : 3 * n] + out[3 * n : 4 * n]
+        for copy in stores(c):
+            copy.start()
+    for c in range(base.shape[1] // LANES):
+        for copy in stores(c):
+            copy.wait()
+
+
+def params(mebibytes=24):
+    return pltpu.CompilerParams(vmem_limit_bytes=mebibytes * 1024 * 1024)
 
 
 def vmem(n):
@@ -325,23 +347,34 @@
     blocks = wide // LANES
     tiles, spread = lax.axis_size("tile"), lax.axis_size("frame")
     rows = (count + 1) * 16 + 8
-    smem = pl.BlockSpec(memory_space=pltpu.SMEM)
+    far = pl.BlockSpec(memory_space=pltpu.HBM)
     shape = jax.ShapeDtypeStruct
 
     own, send = pl.pallas_call(
         adjoint_kernel,
         out_shape=(shape((rows, ext), F32),) * 2,
-        in_specs=vmem(3) + [smem, smem, pl.BlockSpec(memory_space=pl.ANY)],
+        in_specs=[far] * 6,
         out_specs=tuple(vmem(2)),
         scratch_shapes=[
             pltpu.VMEM((blocks, frames * count, LANES), F32),
             pltpu.VMEM(((count + 4) * 64, wide), BF16),
             pltpu.VMEM(((count + 2) * 32, wide), F32),
             pltpu.SemaphoreType.DMA((blocks,)),
+            pltpu.VMEM(frame_shift.shape, I32),
+            pltpu.VMEM(kernel_ids.shape, I32),
+            pltpu.VMEM(groups.shape, I32),
+            pltpu.SMEM((5, kernels.shape[0], 5), F32),
+            pltpu.SMEM(gains.shape, F32),
+            pltpu.SemaphoreType.DMA((5,)),
         ],
         compiler_params=params(),
         name="adjoint",
-    )(frame_shift, kernel_ids, groups, kernels.transpose(1, 0, 2), gains, observed.reshape(frames * count, wide))
+    )(
+        *(
+            pltpu.with_memory_space_constraint(x, pltpu.HBM)
+            for x in (frame_shift, kernel_ids, groups, kernels.transpose(1, 0, 2), gains, observed.reshape(-1, wide))
+        )
+    )
     other = lax.ppermute(send, "frame", [(0, 1), (1, 0)])
 
     first, second = pl.pallas_call(
@@ -358,11 +391,12 @@
     first = lax.ppermute(first, "tile", pairs)
 
     peers = tiles * spread
-    base, once, twice, sums = pl.pallas_call(
+    base, once, twice, spreading, sums = pl.pallas_call(
         operator_kernel,
-        out_shape=(shape((count * 16, half), F32),) * 3 + (shape((peers, 8, LANES), F32),),
+        out_shape=(shape((count * 16, half), F32),) * 3
+        + (shape((4 * LANES, 4 * LANES), BF16), shape((peers, 8, LANES), F32)),
         in_specs=vmem(4),
-        out_specs=tuple(vmem(4)),
+        out_specs=tuple(vmem(5)),
         scratch_shapes=[
             pltpu.VMEM(((count + 4) * 16, ext), F32),
             pltpu.VMEM(((count + 2) * 16, ext), F32),
@@ -373,19 +407,16 @@
     )(own, other, first, second)
     sums = lax.all_to_all(sums, ("tile", "frame"), 0, 0)
 
-    steps = 4 if half % (4 * LANES) == 0 else 1
-    part = half // steps
     solution, residual = pl.pallas_call(
         update_kernel,
-        grid=(steps,),
         out_shape=(shape((count * 4, 4 * half), F32),) * 2,
-        in_specs=[pl.BlockSpec((count * 16, part), lambda j: (0, j))] * 3
-        + [pl.BlockSpec((peers, 8, LANES), lambda j: (0, 0, 0))],
-        out_specs=(pl.BlockSpec((count * 4, 4 * part), lambda j: (0, j)),) * 2,
-        scratch_shapes=[pltpu.VMEM((4 * LANES, 4 * LANES), BF16)],
+        in_specs=vmem(5),
+        out_specs=(far,) * 2,
+        scratch_shapes=[pltpu.VMEM((count * 4, 4 * half), F32)] * 2
+        + [pltpu.SemaphoreType.DMA((2, half // LANES))],
         compiler_params=params(),
         name="update",
-    )(base, once, twice, sums)
+    )(base, once, twice, spreading, sums)
     return solution, residual
 
 

time: 45.8 us -> 41.5 us (0.906)
  local copies, waits for them, and re-layouts: 3.36 us -> 0 us
  Pallas kernels: 14.5 us -> 13.7 us
    unnamed x10 -> x0, local copies, waits for them, and re-layouts: 3.36 us -> none
    pallas_call x1, Pallas kernels: 3.62 us -> 2.28 us  [per_device(): pl.pallas_call(update_kernel, out_shape=(shape((count * 4, 4 * half), F32...]
where the time goes in v2:
time: 41.5 us; the launch traced here: 41.3 us
  Pallas kernels  13.7 us (33%)
  blocking collectives  12.7 us (31%)
  waiting for transfers between devices  10.1 us (24%)
  starting transfers between devices  4.13 us (10%)
  between operations  0.66 us (2%)
    all_to_all x1, blocking collectives, per_device(): sums = lax.all_to_all(sums, ('tile', 'frame'), 0, 0)  12.7 us
    ppermute x1, waiting for transfers between devices, per_device(): first = lax.ppermute(first, 'tile', pairs)  7.48 us
    pallas_call x1, Pallas kernels, per_device(): pl.pallas_call(adjoint_kernel, out_shape=(shape((rows, ext), F32),) * 2,...  7.08 us
    pallas_call x1, Pallas kernels, per_device(): pl.pallas_call(operator_kernel, out_shape=(shape((count * 16, half), F32)...  4.32 us
    ppermute x1, starting transfers between devices, per_device(): first = lax.ppermute(first, 'tile', pairs)  2.95 us
    ppermute x1, waiting for transfers between devices, per_device(): other = lax.ppermute(send, 'frame', [(0, 1), (1, 0)])  2.63 us
    pallas_call x1, Pallas kernels, per_device(): pl.pallas_call(update_kernel, out_shape=(shape((count * 4, 4 * half), F32...  2.28 us
  transfers between devices with their start and end apart: 3, of which 2 were waited for; matrix products, arithmetic and copies ran while one was open for 0% of the time, Pallas kernels for 0%

profile of v2, /device:TPU:0, one launch (start us, length us, event | category | flops | bytes accessed | tf_op | source)
XLA Modules:
  0.0 41.3 jit_solution(14970912792488049203)
XLA Ops:
  0.6 7.1 %adjoint.1 = (f32[280,1152]{1,0:T(8,128)S(1)}, f32[280,1152]{1,0:T(8,128)S(1)}) custom-call(s32[2,32]{1,0:T(2,128)} %far_shift.1, s32[1,32]{1,0:T(1,128)} %far_ids.1, s32[1,32]{1,0:T(1,128)} %far_members.1, f32[5,8,5]{2,1,0:T(8,128)} %bitcast.3, f32[4]{0:T(128)} %far_gains.1, f32[512,2048]{1,0:T(8,128)} %bitcast.2), custom_call_target="tpu_custom_call" | custom-call | tf_op jit(solution)/shard_map/adjoint/pallas_call | solution.py:353
  7.7 0.5 %collective-permute-start = (f32[280,1152]{1,0:T(8,128)S(1)}, f32[280,1152]{1,0:T(8,128)S(1)}, u32[]{:S(2)}, u32[]{:S(2)}) collective-permute-start(f32[280,1152]{1,0:T(8,128)S(1)} %get-tuple-element.12), channel_id=1, source_target_pairs={{0,1},{1,0},{2,3},{3,2},{4,5},{5,4},{6,7},{7,6},{8,9},{9,8},{10,11... | collective-permute-start | bytes 3870728 | tf_op jit(solution)/shard_map/ppermute | solution.py:378
  8.2 2.6 %collective-permute-done.other = f32[280,1152]{1,0:T(8,128)S(1)} collective-permute-done((f32[280,1152]{1,0:T(8,128)S(1)}, f32[280,1152]{1,0:T(8,128)S(1)}, u32[]{:S(2)}, u32[]{:S(2)}) %collective-permute-start) | collective-permute-done | bytes 1290272 | tf_op jit(solution)/shard_map/ppermute | solution.py:378
  10.9 2.9 %collective-permute-start.1 = (f32[40,1152]{1,0:T(8,128)S(1)}, f32[40,1152]{1,0:T(8,128)S(1)}, u32[]{:S(2)}, u32[]{:S(2)}) collective-permute-start(f32[40,1152]{1,0:T(8,128)S(1)} %get-tuple-element.13), channel_id=1, source_target_pairs={{0,2},{2,0},{4,6},{6,4},{8,10},{10,8},{12,14},{14,12},{1,3},{3,1},... | collective-permute-start | bytes 552968 | tf_op jit(solution)/shard_map/ppermute | solution.py:391
  13.9 0.7 %collective-permute-start.2 = (f32[40,1152]{1,0:T(8,128)S(1)}, f32[40,1152]{1,0:T(8,128)S(1)}, u32[]{:S(2)}, u32[]{:S(2)}) collective-permute-start(f32[40,1152]{1,0:T(8,128)S(1)} %get-tuple-element.14), channel_id=1, source_target_pairs={{2,4},{4,2},{6,8},{8,6},{10,12},{12,10},{3,5},{5,3},{7,9},{9,7},{1... | collective-permute-start | bytes 552968 | tf_op jit(solution)/shard_map/ppermute | solution.py:390
  14.5 7.5 %collective-permute-done.1.first = f32[40,1152]{1,0:T(8,128)S(1)} collective-permute-done((f32[40,1152]{1,0:T(8,128)S(1)}, f32[40,1152]{1,0:T(8,128)S(1)}, u32[]{:S(2)}, u32[]{:S(2)}) %collective-permute-start.1) | collective-permute-done | bytes 184352 | tf_op jit(solution)/shard_map/ppermute | solution.py:391
  22.0 0.0 collective-permute-done.2.second
  22.0 4.3 %operator.1 = (f32[256,1024]{1,0:T(8,128)S(1)}, f32[256,1024]{1,0:T(8,128)S(1)}, f32[256,1024]{1,0:T(8,128)S(1)}, bf16[512,512]{1,0:T(8,128)(2,1)S(1)}, f32[16,8,128]{2,1,0:T(8,128)S(1)}) custom-call(f32[280,1152]{1,0:T(8,128)S(1)} %get-tuple-element.11.own, f32[280,1152]{1,0:T(8,128)S(1)} %collective-permute-done.other, ...), custom_call_target="tpu_custom_call" | custom-call | tf_op jit(solution)/shard_map/operator/pallas_call | solution.py:394
  26.4 12.7 %all_to_all.5.sums = f32[16,8,128]{2,1,0:T(8,128)S(1)} all-to-all(f32[16,8,128]{2,1,0:T(8,128)S(1)} %get-tuple-element.19), channel_id=1, replica_groups=mesh['scene'=2,'tile'=8,'frame'=2] {'tile','frame'}, dimensions={0} | all-to-all | bytes 131072 | tf_op jit(solution)/shard_map/all_to_all | solution.py:408
  39.1 2.3 %update.1 = (f32[64,4096]{1,0:T(8,128)}, f32[64,4096]{1,0:T(8,128)}) custom-call(f32[256,1024]{1,0:T(8,128)S(1)} %get-tuple-element.15.base, f32[256,1024]{1,0:T(8,128)S(1)} %get-tuple-element.16.once, f32[256,1024]{1,0:T(8,128)S(1)} %get-tuple-element.17.twice, bf16[512,512]{1,0:T(8,128)(2,1)S(1)} %get-tuple-element.18.spread, f32[16,8,128]{2,1,0:T(8,128)S(1)} %all_to_all.5.sums), custom_call_target="tpu_custom_call" | custom-call | tf_op jit(solution)/shard_map/update/pallas_call | solution.py:410
  (1 shorter events, 0.0 us)
Async XLA Ops:
  7.7 3.2 %collective-permute-start = (f32[280,1152]{1,0:T(8,128)S(1)}, f32[280,1152]{1,0:T(8,128)S(1)}, u32[]{:S(2)}, u32[]{:S(2)}) collective-permute-start(f32[280,1152]{1,0:T(8,128)S(1)} %get-tuple-element.12), channel_id=1, source_target_pairs={{0,1},{1,0},{2,3},{3,2},{4,5},{5,4},{6,7},{7,6},{8,9},{9,8},{10,11... | collective-permute-start | bytes 3870728 | tf_op jit(solution)/shard_map/ppermute | solution.py:378
  10.9 11.1 %collective-permute-start.1 = (f32[40,1152]{1,0:T(8,128)S(1)}, f32[40,1152]{1,0:T(8,128)S(1)}, u32[]{:S(2)}, u32[]{:S(2)}) collective-permute-start(f32[40,1152]{1,0:T(8,128)S(1)} %get-tuple-element.13), channel_id=1, source_target_pairs={{0,2},{2,0},{4,6},{6,4},{8,10},{10,8},{12,14},{14,12},{1,3},{3,1},... | collective-permute-start | bytes 552968 | tf_op jit(solution)/shard_map/ppermute | solution.py:391
  13.9 8.2 %collective-permute-start.2 = (f32[40,1152]{1,0:T(8,128)S(1)}, f32[40,1152]{1,0:T(8,128)S(1)}, u32[]{:S(2)}, u32[]{:S(2)}) collective-permute-start(f32[40,1152]{1,0:T(8,128)S(1)} %get-tuple-element.14), channel_id=1, source_target_pairs={{2,4},{4,2},{6,8},{8,6},{10,12},{12,10},{3,5},{5,3},{7,9},{9,7},{1... | collective-permute-start | bytes 552968 | tf_op jit(solution)/shard_map/ppermute | solution.py:390

commit v3 on v2

v3 whole, which is shorter than its diff:
```python
import functools

import jax
import jax.numpy as jnp
from jax import lax
from jax.experimental import pallas as pl
from jax.experimental.pallas import tpu as pltpu
from jax.sharding import PartitionSpec as P

DAMPING = 0.3
LANES = 128
HIGHEST = lax.Precision.HIGHEST
NT = (((1,), (1,)), ((), ()))
F32, BF16, I32 = jnp.float32, jnp.bfloat16, jnp.int32


def split(x):
    high = x.astype(BF16)
    return high, (x - high.astype(F32)).astype(BF16)


def paired(table):
    high, low = split(table)
    second = (lax.broadcasted_iota(I32, table.shape, 1) >> 5) & 1
    return jnp.concatenate([high, jnp.where(second == 0, low.astype(F32), 0.0).astype(BF16)], axis=0)


def row_phase(shape):
    return lax.broadcasted_iota(I32, shape, 0) & 3


def tap_table(shift, ids, members, kernels, gains):
    frames = shift.shape[1]
    copies = LANES // frames

    def tiled(x):
        return jnp.concatenate([x] * copies, axis=1)

    shape = (32, LANES)
    place = lax.broadcasted_iota(I32, shape, 0)
    lane = lax.broadcasted_iota(I32, shape, 1)
    group = place >> 3
    first = jnp.where(group == 0, 2, jnp.where(group == 1, 4, jnp.where(group == 2, 0, 6)))
    col = first + ((place >> 2) & 1)
    row = 2 + 4 * ((lane >> 5) - 1) + (place & 3)
    up = row - tiled(shift[0:1, :])
    along = col - tiled(shift[1:2, :])
    kind = tiled(ids[...])
    member = tiled(members[...])
    inside = (row >= 0) & (row < 8) & (up >= 0) & (up < 5) & (along >= 0) & (along < 5)
    count = kernels.shape[1]
    code = jnp.where(inside, kind * 25 + up * 5 + along, -1)
    total = jnp.zeros(shape, F32)
    for n in range(count):
        for a in range(5):
            for b in range(5):
                total = jnp.where(code == n * 25 + a * 5 + b, kernels[a, n, b], total)
    scale = jnp.zeros((1, LANES), F32)
    for g in range(gains.shape[0]):
        scale = jnp.where(member == g, gains[g], scale)
    return total * scale


def put_halves(own, send, at, value, me, near):
    half = value.shape[1] // 2
    first, second = value[:, :half], value[:, half:]
    own[at : at + 8, :half] = jnp.where(me == 0, first, second)
    send[at : at + 8, :half] = jnp.where(me == 0, second, first)
    first = jnp.where(near, value[:, half : half + LANES], 0.0)
    second = jnp.where(near, 0.0, value[:, half - LANES : half])
    own[at : at + 8, half:] = jnp.where(me == 0, first, second)
    send[at : at + 8, half:] = jnp.where(me == 0, second, first)


def moved_image(t, lane):
    wide = t.shape[1]
    low = t[0:8] + jnp.where(lane == 0, 0.0, pltpu.roll(t[24:32], 1, 1))
    high = t[8:16] + jnp.where(lane == wide - 1, 0.0, pltpu.roll(t[16:24], wide - 1, 1))
    return low, high


def two_rows(weights, columns):
    both = jnp.dot(weights, columns, preferred_element_type=F32)
    return both[0:32] + both[32:64], both[64:96] + both[96:128]


def one_row(weights, columns):
    both = jnp.dot(weights[0:64, 0:192], columns, preferred_element_type=F32)
    return both[0:32] + both[32:64]


def keep(stack, at, cols, high, low):
    stack[at * 64 : at * 64 + 32, cols] = high
    stack[at * 64 + 32 : at * 64 + 64, cols] = low


def outer_kernel(
    far_shift, far_ids, far_members, far_kernels, far_gains, obs, landed, own, send, weights,
    top, bottom, mixed, sems, shift, ids, members, kernels, gains, small_sems,
):
    wide = obs.shape[1]
    frames = shift.shape[1]
    count = obs.shape[0] // frames
    blocks = wide // LANES
    me = lax.axis_index("frame")

    def load(c):
        return pltpu.make_async_copy(obs.at[:, pl.ds(c * LANES, LANES)], landed.at[c], sems.at[c])

    small = [
        pltpu.make_async_copy(far, near, small_sems.at[i])
        for i, (far, near) in enumerate(
            [(far_kernels, kernels), (far_gains, gains), (far_shift, shift), (far_ids, ids), (far_members, members)]
        )
    ]
    for copy in small:
        copy.start()
    for c in range(blocks):
        load(c).start()
    nothing = jnp.zeros((128, wide), BF16)
    top[0:128, :] = nothing
    bottom[192:320, :] = nothing
    for copy in small:
        copy.wait()
    table = tap_table(shift, ids, members, kernels, gains)
    for r in range(4):
        own[80:88, r * LANES : (r + 1) * LANES] = table[8 * r : 8 * r + 8]
        send[80:88, r * LANES : (r + 1) * LANES] = table[8 * r : 8 * r + 8]
    rest = own.shape[1] - 4 * LANES
    if rest > 0:
        own[80:88, 4 * LANES :] = jnp.zeros((8, rest), F32)
        send[80:88, 4 * LANES :] = jnp.zeros((8, rest), F32)
    source = lax.broadcasted_iota(I32, (LANES, 512), 0)
    target = lax.broadcasted_iota(I32, (LANES, 512), 1)
    place = (target & 255) - 64 * (target >> 8)
    pick = (source == (2 - (place >> 6)) * 32 + (place & 31)) & (place >= 0) & (place < 192)
    both = jnp.dot(table, pick.astype(F32), precision=HIGHEST, preferred_element_type=F32)
    left = jnp.concatenate([paired(both[:, 0:256]), paired(both[:, 256:512])], axis=0)
    weights[...] = left

    for c in range(0, blocks, 2):
        load(c).wait()
        load(c + 1).wait()
        for d in range(2):
            cols = slice((c + d) * LANES, (c + d + 1) * LANES)
            for r in range(3):
                keep(top, 2 + r, cols, *split(landed[c + d, pl.ds(r, frames, stride=count), :]))
                keep(bottom, r, cols, *split(landed[c + d, pl.ds(count - 3 + r, frames, stride=count), :]))
        cols = slice(c * LANES, (c + 2) * LANES)
        a, b = two_rows(left, top[0:256, cols])
        mixed[0:32, cols] = a
        mixed[32:64, cols] = b
        mixed[64:96, cols] = one_row(left, top[128:320, cols])
        mixed[96:128, cols] = one_row(left, bottom[0:192, cols])
        a, b = two_rows(left, bottom[64:320, cols])
        mixed[128:160, cols] = a
        mixed[160:192, cols] = b

    lane = lax.broadcasted_iota(I32, (8, wide), 1)
    near = lax.broadcasted_iota(I32, (8, LANES), 1) < 64
    above, below = moved_image(mixed[0:32, :], lane), moved_image(mixed[160:192, :], lane)
    for g in range(2):
        put_halves(own, send, 8 * g, above[g] + below[g], me, near)
    for r in range(1, 5):
        image = moved_image(mixed[r * 32 : r * 32 + 32, :], lane)
        for g in range(2):
            put_halves(own, send, r * 16 + 8 * g, image[g], me, near)


def inner_rows(first, landed, weights, own, send, at, stack, mixed):
    blocks, wide = landed.shape[0], stack.shape[1]
    frames = 32
    count = landed.shape[1] // frames
    rows = mixed.shape[0] // 32
    left = weights[...]
    for c in range(0, blocks, 2):
        for d in range(2):
            cols = slice((c + d) * LANES, (c + d + 1) * LANES)
            for r in range(rows + 2):
                keep(stack, r, cols, *split(landed[c + d, pl.ds(first - 1 + r, frames, stride=count), :]))
        cols = slice(c * LANES, (c + 2) * LANES)
        for r in range(0, rows, 2):
            a, b = two_rows(left, stack[r * 64 : r * 64 + 256, cols])
            mixed[r * 32 : r * 32 + 32, cols] = a
            mixed[r * 32 + 32 : r * 32 + 64, cols] = b
    lane = lax.broadcasted_iota(I32, (8, wide), 1)
    near = lax.broadcasted_iota(I32, (8, LANES), 1) < 64
    me = lax.axis_index("frame")
    for r in range(rows):
        image = moved_image(mixed[r * 32 : r * 32 + 32, :], lane)
        for g in range(2):
            put_halves(own, send.at[at : at + rows * 16], r * 16 + 8 * g, image[g], me, near)


def early_kernel(first, landed, weights, own, send, stack, mixed):
    inner_rows(first, landed, weights, own, send, 0, stack, mixed)


def late_kernel(first, landed, weights, sent, after, own, send, stack, mixed):
    rows = sent.shape[0]
    send[0:rows] = sent[...]
    inner_rows(first, landed, weights, own, send, rows, stack, mixed)


def border_kernel(own, other, first, second):
    even = lax.rem(lax.axis_index("tile"), 2) == 0
    edge = own[0:16] + other[0:16]
    phase = row_phase((8, own.shape[1]))
    above = jnp.where(phase >= 2, edge[0:8], pltpu.roll(edge[8:16], 6, 0))
    below = jnp.where(phase < 2, edge[0:8], pltpu.roll(edge[8:16], 2, 0))
    top = own[16:48] + other[16:48]
    bottom = own[48:80] + other[48:80]
    first[0:32] = jnp.where(even, bottom, top)
    first[32:40] = jnp.where(even, below, above)
    second[0:32] = jnp.where(even, top, bottom)
    second[32:40] = jnp.where(even, above, below)


def halo_mask():
    lane = lax.broadcasted_iota(I32, (8, LANES), 1)
    here = lax.axis_index("frame") == 0
    return jnp.where(here, jnp.where(lane < 64, 1.0, 0.0), jnp.where(lane < 64, 0.0, 1.0)).astype(F32)


def expand(stack, at, value):
    ext = value.shape[1]
    low, high = value[0:8], value[8:16]
    groups = jnp.concatenate([low, high, pltpu.roll(high, 1, 1), pltpu.roll(low, ext - 1, 1)], axis=0)
    keep(stack, at, slice(None), *split(groups))


def finished(t, field, near):
    ext = t.shape[1]
    half = ext - LANES

    def masked(x):
        return jnp.concatenate([x[:, :half], x[:, half:] * near], axis=1)

    low = t[0:8] + pltpu.roll(masked(t[24:32]), 1, 1)
    high = t[8:16] + pltpu.roll(masked(t[16:24]), ext - 1, 1)
    return jnp.concatenate(
        [masked(low + DAMPING * field[0:8]), masked(high + DAMPING * field[8:16])], axis=0
    )


def folded(a, b):
    total = None
    for c in range(0, a.shape[1] - LANES + 1, LANES):
        for g in (0, 8):
            term = a[g : g + 8, c : c + LANES] * b[g : g + 8, c : c + LANES]
            total = term if total is None else total + term
    return total


def interior_kernel(
    own1, other1, own_early, own_late, other2, base, once, twice, stack1, stack2, tables, spread, sums
):
    ext = own1.shape[1]
    half = ext - LANES
    early = own_early.shape[0] // 16
    inner = other2.shape[0] // 16
    tile, tiles = lax.axis_index("tile"), lax.axis_size("tile")
    no_up = jnp.where(tile > 0, 0.0, 1.0).astype(F32)
    no_down = jnp.where(tile < tiles - 1, 0.0, 1.0).astype(F32)

    taps = [
        jnp.concatenate([ref[80:88, r * LANES : (r + 1) * LANES] for r in range(4)], axis=0) for ref in (own1, other1)
    ]
    block = lax.broadcasted_iota(I32, (32, LANES), 1) >> 5
    left = jnp.concatenate(
        [jnp.concatenate([t, jnp.where(block == 2, t, 0.0), jnp.where(block == 0, t, 0.0)], axis=0) for t in taps],
        axis=1,
    )
    empty = jnp.zeros((64, LANES), F32)
    right = []
    for t in taps:
        e, a = pltpu.roll(t, 32, 1), pltpu.roll(t, LANES - 32, 1)
        right.append(jnp.concatenate([e, e, t, t, a, a, empty, empty, e, e, t, t, a, a], axis=0))
    product = lax.dot_general(
        left, jnp.concatenate(right, axis=1), NT, precision=HIGHEST, preferred_element_type=F32
    )
    lane = lax.broadcasted_iota(I32, (32, 512), 1)
    middle = ((lane >> 6) == 1) | ((lane >> 6) == 6)
    full = product[0:32]
    at_top = full - no_up * jnp.where(middle, product[32:64], 0.0)
    at_bottom = full - no_down * jnp.where(middle, product[64:96], 0.0)
    plain_a, plain_b = paired(full[:, 0:256]), paired(full[:, 256:512])
    top_a, top_b = paired(at_top[:, 0:256]), paired(at_top[:, 256:512])
    bottom_a, bottom_b = paired(at_bottom[:, 0:256]), paired(at_bottom[:, 256:512])
    pairs = [(plain_a, plain_b), (plain_a, top_b), (top_a, plain_b), (plain_a, bottom_b), (bottom_a, plain_b)]
    for i, (a, b) in enumerate(pairs):
        tables[i * 128 : i * 128 + 64] = a
        tables[i * 128 + 64 : i * 128 + 128] = b
    plain = jnp.concatenate([plain_a, plain_b], axis=0)

    source = lax.broadcasted_iota(I32, spread.shape, 0)
    target = lax.broadcasted_iota(I32, spread.shape, 1)
    hit = target == 4 * (source & (LANES - 1)) + (source >> 7)
    spread[...] = jnp.where(hit, 1.0, 0.0).astype(BF16)
    near = halo_mask()
    totals = [jnp.zeros((8, LANES), F32) for _ in range(4)]

    for r in range(inner + 2):
        if r == 0:
            value = own1[32:48] + other1[32:48]
        elif r == inner + 1:
            value = own1[48:64] + other1[48:64]
        else:
            at = (r - 1) * 16
            mine = own_early if r - 1 < early else own_late
            off = at if r - 1 < early else at - early * 16
            value = mine[off : off + 16] + other2[at : at + 16]
        base[r * 16 : r * 16 + 16] = value
        totals[0] += folded(value[:, :half], value[:, :half])
        expand(stack1, r, value)
    for r in range(0, inner, 2):
        images = two_rows(plain, stack1[r * 64 : r * 64 + 256])
        for d in range(2):
            field = base[(r + d + 1) * 16 : (r + d + 2) * 16]
            value = finished(images[d], field, near)
            once[(r + d) * 16 : (r + d + 1) * 16] = value
            totals[1] += folded(field[:, :half], value[:, :half])
            totals[2] += folded(value[:, :half], value[:, :half])
            expand(stack2, r + d, value)
    for r in range(0, inner - 2, 2):
        images = two_rows(plain, stack2[r * 64 : r * 64 + 256])
        for d in range(2):
            field = once[(r + d + 1) * 16 : (r + d + 2) * 16]
            value = finished(images[d], field, near)[:, :half]
            twice[(r + d) * 16 : (r + d + 1) * 16] = value
            totals[3] += folded(field[:, :half], value)
    for i in range(4):
        sums[i * 8 : i * 8 + 8] = totals[i]


def rim_kernel(
    own, other, first, second, base, once, stack1, stack2, tables, partial,
    base_rim, once_rim, twice_rim, sums, above1, below1, above2, below2,
):
    ext = own.shape[1]
    half = ext - LANES
    inner = base.shape[0] // 16
    tile, tiles = lax.axis_index("tile"), lax.axis_size("tile")
    even = lax.rem(tile, 2) == 0
    has_up = jnp.where(tile > 0, 1.0, 0.0).astype(F32)
    has_down = jnp.where(tile < tiles - 1, 1.0, 0.0).astype(F32)
    near = halo_mask()
    phase = row_phase((16, ext))
    totals = [partial[i * 8 : i * 8 + 8] for i in range(4)]
    plain = tables[0:128]

    above1[192:320] = stack1[0:128]
    below1[0:128] = stack1[(inner - 2) * 64 : inner * 64]
    above2[192:320] = stack2[0:128]
    below2[0:128] = stack2[(inner - 4) * 64 : (inner - 2) * 64]

    edge = own[0:16] + other[0:16]
    up = jnp.where(even, second[...], first[...])
    down = jnp.where(even, first[...], second[...])
    rows = {-2: up[0:16]}
    rows[-1] = up[16:32] + has_up * jnp.where(phase >= 2, edge, 0.0)
    e = up[32:40]
    spare = jnp.where(phase < 2, jnp.concatenate([e, pltpu.roll(e, 6, 0)], axis=0), 0.0)
    rows[0] = own[16:32] + other[16:32] + spare
    rows[1] = base[0:16]
    e = down[32:40]
    spare = jnp.where(phase >= 2, jnp.concatenate([e, pltpu.roll(e, 2, 0)], axis=0), 0.0)
    low_rows = {0: base[(inner - 1) * 16 : inner * 16]}
    low_rows[1] = own[64:80] + other[64:80] + spare
    low_rows[2] = down[0:16] + has_down * jnp.where(phase < 2, edge, 0.0)
    low_rows[3] = down[16:32]
    for i in range(3):
        expand(above1, i, rows[i - 2])
        expand(below1, i + 2, low_rows[i + 1])
    base_rim[0:16] = rows[0][:, :half]
    base_rim[16:32] = low_rows[1][:, :half]
    totals[0] += folded(rows[0][:, :half], rows[0][:, :half])
    totals[0] += folded(low_rows[1][:, :half], low_rows[1][:, :half])

    a, b = two_rows(tables[128:256], above1[0:256])
    c = one_row(plain, above1[128:320])
    high = [finished(a, rows[-1], near) * has_up, finished(b, rows[0], near), finished(c, rows[1], near)]
    a = one_row(plain, below1[0:192])
    b, c = two_rows(tables[512:640], below1[64:320])
    deep = [
        finished(a, low_rows[0], near),
        finished(b, low_rows[1], near),
        finished(c, low_rows[2], near) * has_down,
    ]
    for i in range(3):
        expand(above2, i, high[i])
        expand(below2, i + 2, deep[i])
    pieces = [(rows[0], high[1]), (rows[1], high[2]), (low_rows[0], deep[0]), (low_rows[1], deep[1])]
    for i, (field, value) in enumerate(pieces):
        once_rim[i * 16 : i * 16 + 16] = value[:, :half]
        totals[1] += folded(field[:, :half], value[:, :half])
        totals[2] += folded(value[:, :half], value[:, :half])

    a, b = two_rows(tables[256:384], above2[0:256])
    c = one_row(plain, above2[128:320])
    d = one_row(plain, below2[0:192])
    e, f = two_rows(tables[384:512], below2[64:320])
    fields = [high[1], high[2], once[0:16], once[(inner - 3) * 16 : (inner - 2) * 16], deep[0], deep[1]]
    for i, (t, field) in enumerate(zip([a, b, c, d, e, f], fields)):
        value = finished(t, field, near)[:, :half]
        twice_rim[i * 16 : i * 16 + 16] = value
        totals[3] += folded(field[:, :half], value)
    lines = jnp.concatenate([jnp.sum(t, axis=0, keepdims=True) for t in totals], axis=0)
    lines = jnp.concatenate([lines, jnp.zeros((4, LANES), F32)], axis=0)
    for p in range(sums.shape[0]):
        sums[p] = lines


def update_kernel(base, once, twice, base_rim, once_rim, twice_rim, spread, sums, solution, residual, near_x, near_r, sems):
    lanes = jnp.sum(sums[...], axis=0)

    def total(at):
        return jnp.sum(lanes[at : at + 1], axis=1, keepdims=True)

    bb, bm, mm, mmm = [total(at) for at in range(4)]
    alpha = bb / bm
    norm = alpha * alpha * mm - 2.0 * alpha * bm + bb
    beta = norm / bb
    grow = 1.0 + beta
    product = grow * grow * bm - 2.0 * grow * alpha * mm + alpha * alpha * mmm
    step = norm / product
    count = base.shape[0] // 16 + 2
    half = base_rim.shape[1]
    side = lax.broadcasted_iota(I32, (count // 2, 8, LANES), 1) < 4

    def arranged(x):
        x = x.reshape(count // 2, 4, 8, LANES)
        pieces = []
        for g in range(2):
            a, b = x[:, g], x[:, g + 2]
            pieces.append(jnp.where(side, a, pltpu.roll(b, 4, 1)).reshape(4 * count, LANES))
            pieces.append(jnp.where(side, pltpu.roll(a, 4, 1), b).reshape(4 * count, LANES))
        return split(jnp.concatenate(pieces, axis=1))

    def stores(c):
        wide = pl.ds(4 * c * LANES, 4 * LANES)
        return [
            pltpu.make_async_copy(near.at[:, wide], far.at[:, wide], sems.at[i, c])
            for i, (near, far) in enumerate([(near_x, solution), (near_r, residual)])
        ]

    def rows_of(middle, rim, cols):
        n = rim.shape[0] // 2
        return jnp.concatenate([rim[0:n, cols], middle[:, cols], rim[n : 2 * n, cols]], axis=0)

    for c in range(half // LANES):
        cols = slice(c * LANES, (c + 1) * LANES)
        b, m, mm_ = rows_of(base, base_rim, cols), rows_of(once, once_rim, cols), rows_of(twice, twice_rim, cols)
        x = (alpha + step * grow) * b - (step * alpha) * m
        r = (b - alpha * m) - step * (grow * m - alpha * mm_)
        xh, xl = arranged(x)
        rh, rl = arranged(r)
        out = jnp.dot(jnp.concatenate([xh, xl, rh, rl], axis=0), spread[...], preferred_element_type=F32)
        n = 4 * count
        wide = slice(4 * c * LANES, 4 * (c + 1) * LANES)
        near_x[:, wide] = out[0:n] + out[n : 2 * n]
        near_r[:, wide] = out[2 * n : 3 * n] + out[3 * n : 4 * n]
        for copy in stores(c):
            copy.start()
    for c in range(half // LANES):
        for copy in stores(c):
            copy.wait()


def params(mebibytes=24):
    return pltpu.CompilerParams(vmem_limit_bytes=mebibytes * 1024 * 1024)


def cost(units):
    return pl.CostEstimate(flops=int(units * 10**9), bytes_accessed=int(units * 2**22), transcendentals=0)


def vmem(n):
    return [pl.BlockSpec(memory_space=pltpu.VMEM)] * n


def per_device(observed, frame_shift, kernel_ids, groups, kernels, gains):
    frames, count, wide = observed.shape
    half = wide // 2
    ext = half + LANES
    blocks = wide // LANES
    tiles, spread = lax.axis_size("tile"), lax.axis_size("frame")
    far = pl.BlockSpec(memory_space=pltpu.HBM)
    shape = jax.ShapeDtypeStruct
    inner = count - 4
    early = inner // 4 * 2
    late = inner - early

    landed, own, send, weights = pl.pallas_call(
        outer_kernel,
        out_shape=(
            shape((blocks, frames * count, LANES), F32),
            shape((88, ext), F32),
            shape((88, ext), F32),
            shape((128, 256), BF16),
        ),
        in_specs=[far] * 6,
        out_specs=tuple(vmem(4)),
        scratch_shapes=[
            pltpu.VMEM((320, wide), BF16),
            pltpu.VMEM((320, wide), BF16),
            pltpu.VMEM((192, wide), F32),
            pltpu.SemaphoreType.DMA((blocks,)),
            pltpu.VMEM(frame_shift.shape, I32),
            pltpu.VMEM(kernel_ids.shape, I32),
            pltpu.VMEM(groups.shape, I32),
            pltpu.SMEM((5, kernels.shape[0], 5), F32),
            pltpu.SMEM(gains.shape, F32),
            pltpu.SemaphoreType.DMA((5,)),
        ],
        compiler_params=params(),
        name="outer",
    )(
        *(
            pltpu.with_memory_space_constraint(x, pltpu.HBM)
            for x in (frame_shift, kernel_ids, groups, kernels.transpose(1, 0, 2), gains, observed.reshape(-1, wide))
        )
    )
    other = lax.ppermute(send, "frame", [(0, 1), (1, 0)])

    def inner_scratch(rows):
        return [pltpu.VMEM(((rows + 2) * 64, wide), BF16), pltpu.VMEM((rows * 32, wide), F32)]

    own_early, sent = pl.pallas_call(
        functools.partial(early_kernel, 2),
        out_shape=(shape((early * 16, ext), F32),) * 2,
        in_specs=vmem(2),
        out_specs=tuple(vmem(2)),
        scratch_shapes=inner_scratch(early),
        compiler_params=params(),
        cost_estimate=cost(1),
        name="early",
    )(landed, weights)
    first, second = pl.pallas_call(
        border_kernel,
        out_shape=(shape((40, ext), F32),) * 2,
        in_specs=vmem(2),
        out_specs=tuple(vmem(2)),
        compiler_params=params(),
        name="border",
    )(own, other)
    own_late, send2 = pl.pallas_call(
        functools.partial(late_kernel, 2 + early),
        out_shape=(shape((late * 16, ext), F32), shape((inner * 16, ext), F32)),
        in_specs=vmem(4),
        out_specs=tuple(vmem(2)),
        scratch_shapes=inner_scratch(late),
        compiler_params=params(),
        cost_estimate=cost(1),
        name="late",
    )(landed, weights, sent, first)
    pairs = [(i, i ^ 1) for i in range(tiles) if i ^ 1 < tiles]
    odd_pairs = [p for i in range(1, tiles - 1, 2) for p in ((i, i + 1), (i + 1, i))]
    second = lax.ppermute(second, "tile", odd_pairs)
    first = lax.ppermute(first, "tile", pairs)
    other2 = lax.ppermute(send2, "frame", [(0, 1), (1, 0)])

    base, once, twice, stack1, stack2, tables, spreading, partial = pl.pallas_call(
        interior_kernel,
        out_shape=(
            shape(((inner + 2) * 16, ext), F32),
            shape((inner * 16, ext), F32),
            shape(((inner - 2) * 16, half), F32),
            shape(((inner + 2) * 64, ext), BF16),
            shape((inner * 64, ext), BF16),
            shape((5 * 128, 256), BF16),
            shape((4 * LANES, 4 * LANES), BF16),
            shape((32, LANES), F32),
        ),
        in_specs=vmem(5),
        out_specs=tuple(vmem(8)),
        compiler_params=params(),
        cost_estimate=cost(2),
        name="interior",
    )(own, other, own_early, own_late, other2)
    peers = tiles * spread
    base_rim, once_rim, twice_rim, sums = pl.pallas_call(
        rim_kernel,
        out_shape=(
            shape((32, half), F32),
            shape((64, half), F32),
            shape((96, half), F32),
            shape((peers, 8, LANES), F32),
        ),
        in_specs=vmem(10),
        out_specs=tuple(vmem(4)),
        scratch_shapes=[pltpu.VMEM((320, ext), BF16)] * 4,
        compiler_params=params(),
        name="rim",
    )(own, other, first, second, base, once, stack1, stack2, tables, partial)
    sums = lax.all_to_all(sums, ("tile", "frame"), 0, 0)

    solution, residual = pl.pallas_call(
        update_kernel,
        out_shape=(shape((count * 4, 4 * half), F32),) * 2,
        in_specs=vmem(8),
        out_specs=(far,) * 2,
        scratch_shapes=[pltpu.VMEM((count * 4, 4 * half), F32)] * 2
        + [pltpu.SemaphoreType.DMA((2, half // LANES))],
        compiler_params=params(),
        name="update",
    )(base, once, twice, base_rim, once_rim, twice_rim, spreading, sums)
    return solution, residual


def solution(mesh):
    return jax.shard_map(
        per_device,
        mesh=mesh,
        in_specs=(
            P("frame", ("scene", "tile"), None),
            P("scene", "frame"),
            P("scene", "frame"),
            P("scene", "frame"),
            P(),
            P(),
        ),
        out_specs=(P(("scene", "tile"), "frame"), P(("scene", "tile"), "frame")),
        check_vma=False,
    )
```

time: 41.5 us -> 37.4 us (0.901)
  waiting for transfers between devices: 10.1 us -> 5 us
  Pallas kernels: 13.7 us -> 14.5 us
    ppermute x1, waiting for transfers between devices: 2.63 us -> 0.01 us  [per_device(): other = lax.ppermute(send, 'frame', [(0, 1), (1, 0)])]
    ppermute x1, waiting for transfers between devices: 7.48 us -> 4.99 us  [per_device(): first = lax.ppermute(first, 'tile', pairs)]
    pallas_call x2 -> x5, Pallas kernels: 11.4 us -> 12.2 us  [the longest x1 5.28 us: per_device(): pl.pallas_call(outer_kernel, out_shape=(shape((blocks, frames * count, LA...]
  transfers between devices with their start and end apart: 3 -> 4, of which waited for: 2 -> 1; matrix products, arithmetic and copies ran while one was open for 0% -> 0% of each run, Pallas kernels for 0% -> 11%
where the time goes in v3:
time: 37.4 us; the launch traced here: 37.2 us
  Pallas kernels  14.5 us (39%)
  blocking collectives  12.7 us (34%)
  waiting for transfers between devices  5 us (13%)
  starting transfers between devices  4.27 us (11%)
  between operations  0.69 us (2%)
    all_to_all x1, blocking collectives, per_device(): sums = lax.all_to_all(sums, ('tile', 'frame'), 0, 0)  12.7 us
    pallas_call x1, Pallas kernels, per_device(): pl.pallas_call(outer_kernel, out_shape=(shape((blocks, frames * count, LA...  5.28 us
    ppermute x1, waiting for transfers between devices, per_device(): first = lax.ppermute(first, 'tile', pairs)  4.99 us
    ppermute x1, starting transfers between devices, per_device(): first = lax.ppermute(first, 'tile', pairs)  2.79 us
    pallas_call x1, Pallas kernels, per_device(): pl.pallas_call(interior_kernel, out_shape=(shape(((inner + 2) * 16, ext),...  2.56 us
    pallas_call x1, Pallas kernels, per_device(): pl.pallas_call(update_kernel, out_shape=(shape((count * 4, 4 * half), F32...  2.24 us
    pallas_call x1, Pallas kernels, per_device(): pl.pallas_call(functools.partial(late_kernel, 2 + early), out_shape=(shap...  1.56 us
    pallas_call x1, Pallas kernels, per_device(): pl.pallas_call(functools.partial(early_kernel, 2), out_shape=(shape((earl...  1.48 us
  transfers between devices with their start and end apart: 4, of which 1 were waited for; matrix products, arithmetic and copies ran while one was open for 0% of the time, Pallas kernels for 11%

profile of v3, /device:TPU:0, one launch (start us, length us, event | category | flops | bytes accessed | tf_op | source)
XLA Modules:
  0.0 37.2 jit_solution(2032431511086809414)
XLA Ops:
  0.6 5.3 %outer.1 = (f32[16,512,128]{2,1,0:T(8,128)S(1)}, f32[88,1152]{1,0:T(8,128)S(1)}, f32[88,1152]{1,0:T(8,128)S(1)}, bf16[128,256]{1,0:T(8,128)(2,1)S(1)}) custom-call(s32[2,32]{1,0:T(2,128)} %far_shift.1, s32[1,32]{1,0:T(1,128)} %far_ids.1, s32[1,32]{1,0:T(1,128)} %far_members.1, f32[5,8,5]{2,1,0:T(8,128)} %bitcast.3, f32[4]{0:T(128)} %far_gains.1, ...), custom_call_target="tpu_custom_call" | custom-call | tf_op jit(solution)/shard_map/outer/pallas_call | solution.py:494
  5.9 0.5 %collective-permute-start = (f32[88,1152]{1,0:T(8,128)S(1)}, f32[88,1152]{1,0:T(8,128)S(1)}, u32[]{:S(2)}, u32[]{:S(2)}) collective-permute-start(f32[88,1152]{1,0:T(8,128)S(1)} %get-tuple-element.25), channel_id=1, source_target_pairs={{0,1},{1,0},{2,3},{3,2},{4,5},{5,4},{6,7},{7,6},{8,9},{9,8},{10,11... | collective-permute-start | bytes 1216520 | tf_op jit(solution)/shard_map/ppermute | solution.py:524
  6.4 1.5 %early.1 = (f32[96,1152]{1,0:T(8,128)S(1)}, f32[96,1152]{1,0:T(8,128)S(1)}) custom-call(f32[16,512,128]{2,1,0:T(8,128)S(1)} %get-tuple-element.26.landed, bf16[128,256]{1,0:T(8,128)(2,1)S(1)} %get-tuple-element.27.weights), custom_call_target="tpu_custom_call" | custom-call | flops 1000000000 | bytes 4194304 | tf_op jit(solution)/shard_map/early/pallas_call | solution.py:529
  7.9 0.0 collective-permute-done.other.other1
  7.9 0.1 border.1
  8.0 1.6 %late.1 = (f32[96,1152]{1,0:T(8,128)S(1)}, f32[192,1152]{1,0:T(8,128)S(1)}) custom-call(f32[16,512,128]{2,1,0:T(8,128)S(1)} %get-tuple-element.26.landed, bf16[128,256]{1,0:T(8,128)(2,1)S(1)} %get-tuple-element.27.weights, f32[96,1152]{1,0:T(8,128)S(1)} %get-tuple-element.29.sent, f32[40,1152]{1,0:T(8,128)S(1)} %get-tuple-element.30.after), custom_call_target="tpu_custom_call" | custom-call | flops 1000000000 | bytes 4194304 | tf_op jit(solution)/shard_map/late/pallas_call | solution.py:547
  9.6 0.3 collective-permute-start.1
  9.9 2.8 %collective-permute-start.2 = (f32[40,1152]{1,0:T(8,128)S(1)}, f32[40,1152]{1,0:T(8,128)S(1)}, u32[]{:S(2)}, u32[]{:S(2)}) collective-permute-start(f32[40,1152]{1,0:T(8,128)S(1)} %get-tuple-element.30.after), channel_id=1, source_target_pairs={{0,2},{2,0},{4,6},{6,4},{8,10},{10,8},{12,14},{14,12},{1,3},{3,1},... | collective-permute-start | bytes 552968 | tf_op jit(solution)/shard_map/ppermute | solution.py:560
  12.7 0.7 %collective-permute-start.3 = (f32[40,1152]{1,0:T(8,128)S(1)}, f32[40,1152]{1,0:T(8,128)S(1)}, u32[]{:S(2)}, u32[]{:S(2)}) collective-permute-start(f32[40,1152]{1,0:T(8,128)S(1)} %get-tuple-element.36), channel_id=1, source_target_pairs={{2,4},{4,2},{6,8},{8,6},{10,12},{12,10},{3,5},{5,3},{7,9},{9,7},{1... | collective-permute-start | bytes 552968 | tf_op jit(solution)/shard_map/ppermute | solution.py:559
  13.3 0.0 collective-permute-done.1.other2
  13.3 2.6 %interior.1 = (f32[224,1152]{1,0:T(8,128)S(1)}, f32[192,1152]{1,0:T(8,128)S(1)}, f32[160,1024]{1,0:T(8,128)S(1)}, bf16[896,1152]{1,0:T(8,128)(2,1)S(1)}, bf16[76...) custom-call(f32[88,1152]{1,0:T(8,128)S(1)} %get-tuple-element.24.own, ...), custom_call_target="tpu_custom_call" | custom-call | flops 2000000000 | bytes 8388608 | tf_op jit(solution)/shard_map/interior/pallas_call | solution.py:563
  15.9 0.0 collective-permute-done.3.second
  15.9 5.0 %collective-permute-done.2.first = f32[40,1152]{1,0:T(8,128)S(1)} collective-permute-done((f32[40,1152]{1,0:T(8,128)S(1)}, f32[40,1152]{1,0:T(8,128)S(1)}, u32[]{:S(2)}, u32[]{:S(2)}) %collective-permute-start.2) | collective-permute-done | bytes 184352 | tf_op jit(solution)/shard_map/ppermute | solution.py:560
  20.9 1.3 %rim.1 = (f32[32,1024]{1,0:T(8,128)S(1)}, f32[64,1024]{1,0:T(8,128)S(1)}, f32[96,1024]{1,0:T(8,128)S(1)}, f32[16,8,128]{2,1,0:T(8,128)S(1)}) custom-call(f32[88,1152]{1,0:T(8,128)S(1)} %get-tuple-element.24.own.own1, f32[88,1152]{1,0:T(8,128)S(1)} %collective-permute-done.other.other1, f32[40,1152]{1,0:T(8,128)S(1)} %collective-permute-done.2.first, ...), custom_call_target="tpu_custom_call" | custom-call | tf_op jit(solution)/shard_map/rim/pallas_call | solution.py:582
  22.2 12.7 %all_to_all.5.sums = f32[16,8,128]{2,1,0:T(8,128)S(1)} all-to-all(f32[16,8,128]{2,1,0:T(8,128)S(1)} %get-tuple-element.45), channel_id=1, replica_groups=mesh['scene'=2,'tile'=8,'frame'=2] {'tile','frame'}, dimensions={0} | all-to-all | bytes 131072 | tf_op jit(solution)/shard_map/all_to_all | solution.py:596
  35.0 2.2 %update.1 = (f32[64,4096]{1,0:T(8,128)}, f32[64,4096]{1,0:T(8,128)}) custom-call(f32[224,1152]{1,0:T(8,128)S(1)} %get-tuple-element.33.base, f32[192,1152]{1,0:T(8,128)S(1)} %get-tuple-element.34.once, f32[160,1024]{1,0:T(8,128)S(1)} %get-tuple-element.35.twice, f32[32,1024]{1,0:T(8,128)S(1)} %get-tuple-element.41.base_rim, ...), custom_call_target="tpu_custom_call" | custom-call | tf_op jit(solution)/shard_map/update/pallas_call | solution.py:598
Async XLA Ops:
  5.9 2.0 %collective-permute-start = (f32[88,1152]{1,0:T(8,128)S(1)}, f32[88,1152]{1,0:T(8,128)S(1)}, u32[]{:S(2)}, u32[]{:S(2)}) collective-permute-start(f32[88,1152]{1,0:T(8,128)S(1)} %get-tuple-element.25), channel_id=1, source_target_pairs={{0,1},{1,0},{2,3},{3,2},{4,5},{5,4},{6,7},{7,6},{8,9},{9,8},{10,11... | collective-permute-start | bytes 1216520 | tf_op jit(solution)/shard_map/ppermute | solution.py:524
  9.6 3.8 %collective-permute-start.1 = (f32[192,1152]{1,0:T(8,128)S(1)}, f32[192,1152]{1,0:T(8,128)S(1)}, u32[]{:S(2)}, u32[]{:S(2)}) collective-permute-start(f32[192,1152]{1,0:T(8,128)S(1)} %get-tuple-element.32), channel_id=1, source_target_pairs={{0,1},{1,0},{2,3},{3,2},{4,5},{5,4},{6,7},{7,6},{8,9},{9,8},{10,11... | collective-permute-start | bytes 2654216 | tf_op jit(solution)/shard_map/ppermute | solution.py:561
  9.9 11.0 %collective-permute-start.2 = (f32[40,1152]{1,0:T(8,128)S(1)}, f32[40,1152]{1,0:T(8,128)S(1)}, u32[]{:S(2)}, u32[]{:S(2)}) collective-permute-start(f32[40,1152]{1,0:T(8,128)S(1)} %get-tuple-element.30.after), channel_id=1, source_target_pairs={{0,2},{2,0},{4,6},{6,4},{8,10},{10,8},{12,14},{14,12},{1,3},{3,1},... | collective-permute-start | bytes 552968 | tf_op jit(solution)/shard_map/ppermute | solution.py:560
  12.7 3.2 %collective-permute-start.3 = (f32[40,1152]{1,0:T(8,128)S(1)}, f32[40,1152]{1,0:T(8,128)S(1)}, u32[]{:S(2)}, u32[]{:S(2)}) collective-permute-start(f32[40,1152]{1,0:T(8,128)S(1)} %get-tuple-element.36), channel_id=1, source_target_pairs={{2,4},{4,2},{6,8},{8,6},{10,12},{12,10},{3,5},{5,3},{7,9},{9,7},{1... | collective-permute-start | bytes 552968 | tf_op jit(solution)/shard_map/ppermute | solution.py:559

commit v4 on v3

--- a/solution.py
+++ b/solution.py
@@ -61,21 +61,26 @@
     return total * scale
 
 
-def put_halves(own, send, at, value, me, near):
+def put_halves(own, send, at, value, me):
     half = value.shape[1] // 2
-    first, second = value[:, :half], value[:, half:]
-    own[at : at + 8, :half] = jnp.where(me == 0, first, second)
-    send[at : at + 8, :half] = jnp.where(me == 0, second, first)
-    first = jnp.where(near, value[:, half : half + LANES], 0.0)
-    second = jnp.where(near, 0.0, value[:, half - LANES : half])
-    own[at : at + 8, half:] = jnp.where(me == 0, first, second)
-    send[at : at + 8, half:] = jnp.where(me == 0, second, first)
-
-
-def moved_image(t, lane):
+    near = lax.broadcasted_iota(I32, (8, LANES), 1) < 64
+    own[at : at + 8, :half] = value[:, :half]
+    send[at : at + 8, :half] = value[:, half:]
+    after = jnp.where(near, value[:, half : half + LANES], 0.0)
+    before = jnp.where(near, 0.0, value[:, 2 * half - LANES :])
+    own[at : at + 8, half:] = jnp.where(me == 0, after, before)
+    before = jnp.where(near, 0.0, value[:, half - LANES : half])
+    after = jnp.where(near, value[:, 0:LANES], 0.0)
+    send[at : at + 8, half:] = jnp.where(me == 0, before, after)
+
+
+def moved_image(t, me):
     wide = t.shape[1]
-    low = t[0:8] + jnp.where(lane == 0, 0.0, pltpu.roll(t[24:32], 1, 1))
-    high = t[8:16] + jnp.where(lane == wide - 1, 0.0, pltpu.roll(t[16:24], wide - 1, 1))
+    half = wide // 2
+    lane = lax.broadcasted_iota(I32, (8, wide), 1)
+    low = t[0:8] + jnp.where(lane == jnp.where(me == 0, 0, half), 0.0, pltpu.roll(t[24:32], 1, 1))
+    last = jnp.where(me == 0, wide - 1, half - 1)
+    high = t[8:16] + jnp.where(lane == last, 0.0, pltpu.roll(t[16:24], wide - 1, 1))
     return low, high
 
 
@@ -94,8 +99,17 @@
     stack[at * 64 + 32 : at * 64 + 64, cols] = low
 
 
+def adjoint_weights(table):
+    source = lax.broadcasted_iota(I32, (LANES, 512), 0)
+    target = lax.broadcasted_iota(I32, (LANES, 512), 1)
+    place = (target & 255) - 64 * (target >> 8)
+    pick = (source == (2 - (place >> 6)) * 32 + (place & 31)) & (place >= 0) & (place < 192)
+    both = jnp.dot(table, pick.astype(F32), precision=HIGHEST, preferred_element_type=F32)
+    return jnp.concatenate([paired(both[:, 0:256]), paired(both[:, 256:512])], axis=0)
+
+
 def outer_kernel(
-    far_shift, far_ids, far_members, far_kernels, far_gains, obs, landed, own, send, weights,
+    far_shift, far_ids, far_members, far_kernels, far_gains, obs, mine, theirs, own, send, weights,
     top, bottom, mixed, sems, shift, ids, members, kernels, gains, small_sems,
 ):
     wide = obs.shape[1]
@@ -104,8 +118,20 @@
     blocks = wide // LANES
     me = lax.axis_index("frame")
 
+    half = wide // 2
+
     def load(c):
-        return pltpu.make_async_copy(obs.at[:, pl.ds(c * LANES, LANES)], landed.at[c], sems.at[c])
+        if c < blocks:
+            start = jnp.where(me == 0, 0, half) if c < blocks // 2 else jnp.where(me == 0, half, 0)
+            start = start + (c % (blocks // 2)) * LANES
+            target = mine if c < blocks // 2 else theirs
+            at = c % (blocks // 2)
+        else:
+            start = jnp.where(me == c - blocks, half, half - LANES)
+            target = mine if c == blocks else theirs
+            at = blocks // 2
+        source = obs.at[:, pl.ds(pl.multiple_of(start, LANES), LANES)]
+        return pltpu.make_async_copy(source, target.at[at], sems.at[c])
 
     small = [
         pltpu.make_async_copy(far, near, small_sems.at[i])
@@ -115,7 +141,7 @@
     ]
     for copy in small:
         copy.start()
-    for c in range(blocks):
+    for c in range(blocks + 2):
         load(c).start()
     nothing = jnp.zeros((128, wide), BF16)
     top[0:128, :] = nothing
@@ -130,12 +156,7 @@
     if rest > 0:
         own[80:88, 4 * LANES :] = jnp.zeros((8, rest), F32)
         send[80:88, 4 * LANES :] = jnp.zeros((8, rest), F32)
-    source = lax.broadcasted_iota(I32, (LANES, 512), 0)
-    target = lax.broadcasted_iota(I32, (LANES, 512), 1)
-    place = (target & 255) - 64 * (target >> 8)
-    pick = (source == (2 - (place >> 6)) * 32 + (place & 31)) & (place >= 0) & (place < 192)
-    both = jnp.dot(table, pick.astype(F32), precision=HIGHEST, preferred_element_type=F32)
-    left = jnp.concatenate([paired(both[:, 0:256]), paired(both[:, 256:512])], axis=0)
+    left = adjoint_weights(table)
     weights[...] = left
 
     for c in range(0, blocks, 2):
@@ -143,9 +164,10 @@
         load(c + 1).wait()
         for d in range(2):
             cols = slice((c + d) * LANES, (c + d + 1) * LANES)
+            landed, at = (mine, c + d) if c < blocks // 2 else (theirs, c + d - blocks // 2)
             for r in range(3):
-                keep(top, 2 + r, cols, *split(landed[c + d, pl.ds(r, frames, stride=count), :]))
-                keep(bottom, r, cols, *split(landed[c + d, pl.ds(count - 3 + r, frames, stride=count), :]))
+                keep(top, 2 + r, cols, *split(landed[at, pl.ds(r, frames, stride=count), :]))
+                keep(bottom, r, cols, *split(landed[at, pl.ds(count - 3 + r, frames, stride=count), :]))
         cols = slice(c * LANES, (c + 2) * LANES)
         a, b = two_rows(left, top[0:256, cols])
         mixed[0:32, cols] = a
@@ -156,53 +178,40 @@
         mixed[128:160, cols] = a
         mixed[160:192, cols] = b
 
-    lane = lax.broadcasted_iota(I32, (8, wide), 1)
-    near = lax.broadcasted_iota(I32, (8, LANES), 1) < 64
-    above, below = moved_image(mixed[0:32, :], lane), moved_image(mixed[160:192, :], lane)
+    above, below = moved_image(mixed[0:32, :], me), moved_image(mixed[160:192, :], me)
     for g in range(2):
-        put_halves(own, send, 8 * g, above[g] + below[g], me, near)
+        put_halves(own, send, 8 * g, above[g] + below[g], me)
     for r in range(1, 5):
-        image = moved_image(mixed[r * 32 : r * 32 + 32, :], lane)
+        image = moved_image(mixed[r * 32 : r * 32 + 32, :], me)
         for g in range(2):
-            put_halves(own, send, r * 16 + 8 * g, image[g], me, near)
-
-
-def inner_rows(first, landed, weights, own, send, at, stack, mixed):
-    blocks, wide = landed.shape[0], stack.shape[1]
-    frames = 32
-    count = landed.shape[1] // frames
+            put_halves(own, send, r * 16 + 8 * g, image[g], me)
+    load(blocks).wait()
+    load(blocks + 1).wait()
+
+
+def inner_sums(landed, left, stack, mixed):
+    blocks = landed.shape[0]
     rows = mixed.shape[0] // 32
-    left = weights[...]
+    count = rows + 4
+    frames = landed.shape[1] // count
     for c in range(0, blocks, 2):
-        for d in range(2):
+        pair = min(2, blocks - c)
+        for d in range(pair):
             cols = slice((c + d) * LANES, (c + d + 1) * LANES)
             for r in range(rows + 2):
-                keep(stack, r, cols, *split(landed[c + d, pl.ds(first - 1 + r, frames, stride=count), :]))
-        cols = slice(c * LANES, (c + 2) * LANES)
+                keep(stack, r, cols, *split(landed[c + d, pl.ds(1 + r, frames, stride=count), :]))
+        cols = slice(c * LANES, (c + pair) * LANES)
         for r in range(0, rows, 2):
             a, b = two_rows(left, stack[r * 64 : r * 64 + 256, cols])
             mixed[r * 32 : r * 32 + 32, cols] = a
             mixed[r * 32 + 32 : r * 32 + 64, cols] = b
-    lane = lax.broadcasted_iota(I32, (8, wide), 1)
-    near = lax.broadcasted_iota(I32, (8, LANES), 1) < 64
-    me = lax.axis_index("frame")
-    for r in range(rows):
-        image = moved_image(mixed[r * 32 : r * 32 + 32, :], lane)
-        for g in range(2):
-            put_halves(own, send.at[at : at + rows * 16], r * 16 + 8 * g, image[g], me, near)
-
-
-def early_kernel(first, landed, weights, own, send, stack, mixed):
-    inner_rows(first, landed, weights, own, send, 0, stack, mixed)
-
-
-def late_kernel(first, landed, weights, sent, after, own, send, stack, mixed):
-    rows = sent.shape[0]
-    send[0:rows] = sent[...]
-    inner_rows(first, landed, weights, own, send, rows, stack, mixed)
-
-
-def border_kernel(own, other, first, second):
+
+
+def early_kernel(landed, weights, mixed, stack):
+    inner_sums(landed, weights[...], stack, mixed)
+
+
+def border_kernel(own, other, passed, first, second, onward):
     even = lax.rem(lax.axis_index("tile"), 2) == 0
     edge = own[0:16] + other[0:16]
     phase = row_phase((8, own.shape[1]))
@@ -229,7 +238,7 @@
     keep(stack, at, slice(None), *split(groups))
 
 
-def finished(t, field, near):
+def assembled(t, near, field=None):
     ext = t.shape[1]
     half = ext - LANES
 
@@ -238,9 +247,13 @@
 
     low = t[0:8] + pltpu.roll(masked(t[24:32]), 1, 1)
     high = t[8:16] + pltpu.roll(masked(t[16:24]), ext - 1, 1)
-    return jnp.concatenate(
-        [masked(low + DAMPING * field[0:8]), masked(high + DAMPING * field[8:16])], axis=0
-    )
+    if field is not None:
+        low, high = low + DAMPING * field[0:8], high + DAMPING * field[8:16]
+    return jnp.concatenate([masked(low), masked(high)], axis=0)
+
+
+def finished(t, field, near):
+    return assembled(t, near, field)
 
 
 def folded(a, b):
@@ -253,12 +266,11 @@
 
 
 def interior_kernel(
-    own1, other1, own_early, own_late, other2, base, once, twice, stack1, stack2, tables, spread, sums
+    own1, other1, ours, landed, base, once, twice, stack1, stack2, tables, spread, sums, stack, mixed
 ):
     ext = own1.shape[1]
     half = ext - LANES
-    early = own_early.shape[0] // 16
-    inner = other2.shape[0] // 16
+    inner = ours.shape[0] // 32
     tile, tiles = lax.axis_index("tile"), lax.axis_size("tile")
     no_up = jnp.where(tile > 0, 0.0, 1.0).astype(F32)
     no_down = jnp.where(tile < tiles - 1, 0.0, 1.0).astype(F32)
@@ -266,6 +278,7 @@
     taps = [
         jnp.concatenate([ref[80:88, r * LANES : (r + 1) * LANES] for r in range(4)], axis=0) for ref in (own1, other1)
     ]
+    inner_sums(landed, adjoint_weights(taps[1]), stack, mixed)
     block = lax.broadcasted_iota(I32, (32, LANES), 1) >> 5
     left = jnp.concatenate(
         [jnp.concatenate([t, jnp.where(block == 2, t, 0.0), jnp.where(block == 0, t, 0.0)], axis=0) for t in taps],
@@ -306,10 +319,8 @@
         elif r == inner + 1:
             value = own1[48:64] + other1[48:64]
         else:
-            at = (r - 1) * 16
-            mine = own_early if r - 1 < early else own_late
-            off = at if r - 1 < early else at - early * 16
-            value = mine[off : off + 16] + other2[at : at + 16]
+            at = (r - 1) * 32
+            value = assembled(ours[at : at + 32] + mixed[at : at + 32], near)
         base[r * 16 : r * 16 + 16] = value
         totals[0] += folded(value[:, :half], value[:, :half])
         expand(stack1, r, value)
@@ -488,24 +499,23 @@
     far = pl.BlockSpec(memory_space=pltpu.HBM)
     shape = jax.ShapeDtypeStruct
     inner = count - 4
-    early = inner // 4 * 2
-    late = inner - early
-
-    landed, own, send, weights = pl.pallas_call(
+
+    mine, theirs, own, send, weights = pl.pallas_call(
         outer_kernel,
         out_shape=(
-            shape((blocks, frames * count, LANES), F32),
+            shape((blocks // 2 + 1, frames * count, LANES), F32),
+            shape((blocks // 2 + 1, frames * count, LANES), F32),
             shape((88, ext), F32),
             shape((88, ext), F32),
             shape((128, 256), BF16),
         ),
         in_specs=[far] * 6,
-        out_specs=tuple(vmem(4)),
+        out_specs=tuple(vmem(5)),
         scratch_shapes=[
             pltpu.VMEM((320, wide), BF16),
             pltpu.VMEM((320, wide), BF16),
             pltpu.VMEM((192, wide), F32),
-            pltpu.SemaphoreType.DMA((blocks,)),
+            pltpu.SemaphoreType.DMA((blocks + 2,)),
             pltpu.VMEM(frame_shift.shape, I32),
             pltpu.VMEM(kernel_ids.shape, I32),
             pltpu.VMEM(groups.shape, I32),
@@ -523,42 +533,30 @@
     )
     other = lax.ppermute(send, "frame", [(0, 1), (1, 0)])
 
-    def inner_scratch(rows):
-        return [pltpu.VMEM(((rows + 2) * 64, wide), BF16), pltpu.VMEM((rows * 32, wide), F32)]
-
-    own_early, sent = pl.pallas_call(
-        functools.partial(early_kernel, 2),
-        out_shape=(shape((early * 16, ext), F32),) * 2,
+    ours = pl.pallas_call(
+        early_kernel,
+        out_shape=shape((inner * 32, ext), F32),
         in_specs=vmem(2),
-        out_specs=tuple(vmem(2)),
-        scratch_shapes=inner_scratch(early),
+        out_specs=vmem(1)[0],
+        scratch_shapes=[pltpu.VMEM(((inner + 2) * 64, ext), BF16)],
         compiler_params=params(),
         cost_estimate=cost(1),
         name="early",
-    )(landed, weights)
-    first, second = pl.pallas_call(
+    )(mine, weights)
+    first, second, theirs = pl.pallas_call(
         border_kernel,
-        out_shape=(shape((40, ext), F32),) * 2,
-        in_specs=vmem(2),
-        out_specs=tuple(vmem(2)),
+        out_shape=(shape((40, ext), F32), shape((40, ext), F32), shape(theirs.shape, F32)),
+        in_specs=vmem(3),
+        out_specs=tuple(vmem(3)),
+        input_output_aliases={2: 2},
         compiler_params=params(),
         name="border",
-    )(own, other)
-    own_late, send2 = pl.pallas_call(
-        functools.partial(late_kernel, 2 + early),
-        out_shape=(shape((late * 16, ext), F32), shape((inner * 16, ext), F32)),
-        in_specs=vmem(4),
-        out_specs=tuple(vmem(2)),
-        scratch_shapes=inner_scratch(late),
-        compiler_params=params(),
-        cost_estimate=cost(1),
-        name="late",
-    )(landed, weights, sent, first)
+    )(own, other, theirs)
+    theirs = lax.ppermute(theirs, "frame", [(0, 1), (1, 0)])
     pairs = [(i, i ^ 1) for i in range(tiles) if i ^ 1 < tiles]
     odd_pairs = [p for i in range(1, tiles - 1, 2) for p in ((i, i + 1), (i + 1, i))]
     second = lax.ppermute(second, "tile", odd_pairs)
     first = lax.ppermute(first, "tile", pairs)
-    other2 = lax.ppermute(send2, "frame", [(0, 1), (1, 0)])
 
     base, once, twice, stack1, stack2, tables, spreading, partial = pl.pallas_call(
         interior_kernel,
@@ -572,12 +570,13 @@
             shape((4 * LANES, 4 * LANES), BF16),
             shape((32, LANES), F32),
         ),
-        in_specs=vmem(5),
+        in_specs=vmem(4),
         out_specs=tuple(vmem(8)),
+        scratch_shapes=[pltpu.VMEM(((inner + 2) * 64, ext), BF16), pltpu.VMEM((inner * 32, ext), F32)],
         compiler_params=params(),
-        cost_estimate=cost(2),
+        cost_estimate=cost(0.01),
         name="interior",
-    )(own, other, own_early, own_late, other2)
+    )(own, other, ours, theirs)
     peers = tiles * spread
     base_rim, once_rim, twice_rim, sums = pl.pallas_call(
         rim_kernel,

time: 37.4 us -> 35.9 us (0.960)
  waiting for transfers between devices: 5 us -> 3.5 us
    ppermute x1, waiting for transfers between devices: 4.99 us -> 2.12 us  [per_device(): first = lax.ppermute(first, 'tile', pairs)]
    pallas_call x1, Pallas kernels: 2.56 us -> 4.22 us  [per_device(): pl.pallas_call(interior_kernel, out_shape=(shape(((inner + 2) * 16, ext),...]
    pallas_call x4 -> x3, Pallas kernels: 8.39 us -> 6.76 us  [the longest x1 5.38 us: per_device(): pl.pallas_call(outer_kernel, out_shape=(shape((blocks // 2 + 1, frames *...]
    ppermute x1, waiting for transfers between devices: 0.01 us -> 1.37 us  [per_device(): other = lax.ppermute(send, 'frame', [(0, 1), (1, 0)])]
  transfers between devices with their start and end apart: 4 -> 4, of which waited for: 1 -> 2; matrix products, arithmetic and copies ran while one was open for 0% -> 0% of each run, Pallas kernels for 11% -> 16%
where the time goes in v4:
time: 35.9 us; the launch traced here: 35.7 us
  Pallas kernels  14.5 us (40%)
  blocking collectives  12.7 us (35%)
  starting transfers between devices  4.28 us (12%)
  waiting for transfers between devices  3.5 us (10%)
  between operations  0.68 us (2%)
    all_to_all x1, blocking collectives, per_device(): sums = lax.all_to_all(sums, ('tile', 'frame'), 0, 0)  12.7 us
    pallas_call x1, Pallas kernels, per_device(): pl.pallas_call(outer_kernel, out_shape=(shape((blocks // 2 + 1, frames *...  5.38 us
    pallas_call x1, Pallas kernels, per_device(): pl.pallas_call(interior_kernel, out_shape=(shape(((inner + 2) * 16, ext),...  4.22 us
    ppermute x1, starting transfers between devices, per_device(): first = lax.ppermute(first, 'tile', pairs)  2.67 us
    pallas_call x1, Pallas kernels, per_device(): pl.pallas_call(update_kernel, out_shape=(shape((count * 4, 4 * half), F32...  2.24 us
    ppermute x1, waiting for transfers between devices, per_device(): first = lax.ppermute(first, 'tile', pairs)  2.12 us
    ppermute x1, waiting for transfers between devices, per_device(): other = lax.ppermute(send, 'frame', [(0, 1), (1, 0)])  1.37 us
    pallas_call x1, Pallas kernels, per_device(): pl.pallas_call(early_kernel, out_shape=shape((inner * 32, ext), F32), in_...  1.33 us
  transfers between devices with their start and end apart: 4, of which 2 were waited for; matrix products, arithmetic and copies ran while one was open for 0% of the time, Pallas kernels for 16%

profile of v4, /device:TPU:0, one launch (start us, length us, event | category | flops | bytes accessed | tf_op | source)
XLA Modules:
  0.0 35.7 jit_solution(18338892463100754053)
XLA Ops:
  0.6 5.4 %outer.1 = (f32[9,512,128]{2,1,0:T(8,128)S(1)}, f32[9,512,128]{2,1,0:T(8,128)S(1)}, f32[88,1152]{1,0:T(8,128)S(1)}, f32[88,1152]{1,0:T(8,128)S(1)}, bf16[128,256]{1,0:T(8,128)(2,1)S(1)}) custom-call(s32[2,32]{1,0:T(2,128)} %far_shift.1, s32[1,32]{1,0:T(1,128)} %far_ids.1, s32[1,32]{1,0:T(1,128)} %far_members.1, f32[5,8,5]{2,1,0:T(8,128)} %bitcast.3, ...), custom_call_target="tpu_custom_call" | custom-call | tf_op jit(solution)/shard_map/outer/pallas_call | solution.py:503
  6.0 0.5 %collective-permute-start = (f32[88,1152]{1,0:T(8,128)S(1)}, f32[88,1152]{1,0:T(8,128)S(1)}, u32[]{:S(2)}, u32[]{:S(2)}) collective-permute-start(f32[88,1152]{1,0:T(8,128)S(1)} %get-tuple-element.23), channel_id=1, source_target_pairs={{0,1},{1,0},{2,3},{3,2},{4,5},{5,4},{6,7},{7,6},{8,9},{9,8},{10,11... | collective-permute-start | bytes 1216520 | tf_op jit(solution)/shard_map/ppermute | solution.py:534
  6.5 1.4 %collective-permute-done.other.other1 = f32[88,1152]{1,0:T(8,128)S(1)} collective-permute-done((f32[88,1152]{1,0:T(8,128)S(1)}, f32[88,1152]{1,0:T(8,128)S(1)}, u32[]{:S(2)}, u32[]{:S(2)}) %collective-permute-start) | collective-permute-done | bytes 405536 | tf_op jit(solution)/shard_map/ppermute | solution.py:534
  7.9 0.1 border.1
  8.0 0.4 %collective-permute-start.1 = (f32[9,512,128]{2,1,0:T(8,128)S(1)}, f32[9,512,128]{2,1,0:T(8,128)S(1)}, u32[]{:S(2)}, u32[]{:S(2)}) collective-permute-start(f32[9,512,128]{2,1,0:T(8,128)S(1)} %get-tuple-element.27), channel_id=1, source_target_pairs={{0,1},{1,0},{2,3},{3,2},{4,5},{5,4},{6,7},{7,6},{8,9},{9,8},{10,11... | collective-permute-start | bytes 7077896 | tf_op jit(solution)/shard_map/ppermute | solution.py:555
  8.4 2.7 %collective-permute-start.2 = (f32[40,1152]{1,0:T(8,128)S(1)}, f32[40,1152]{1,0:T(8,128)S(1)}, u32[]{:S(2)}, u32[]{:S(2)}) collective-permute-start(f32[40,1152]{1,0:T(8,128)S(1)} %get-tuple-element.31), channel_id=1, source_target_pairs={{0,2},{2,0},{4,6},{6,4},{8,10},{10,8},{12,14},{14,12},{1,3},{3,1},... | collective-permute-start | bytes 552968 | tf_op jit(solution)/shard_map/ppermute | solution.py:559
  11.1 0.7 %collective-permute-start.3 = (f32[40,1152]{1,0:T(8,128)S(1)}, f32[40,1152]{1,0:T(8,128)S(1)}, u32[]{:S(2)}, u32[]{:S(2)}) collective-permute-start(f32[40,1152]{1,0:T(8,128)S(1)} %get-tuple-element.32), channel_id=1, source_target_pairs={{2,4},{4,2},{6,8},{8,6},{10,12},{12,10},{3,5},{5,3},{7,9},{9,7},{1... | collective-permute-start | bytes 552968 | tf_op jit(solution)/shard_map/ppermute | solution.py:558
  11.7 1.3 %early.1.ours = f32[384,1152]{1,0:T(8,128)S(1)} custom-call(f32[9,512,128]{2,1,0:T(8,128)S(1)} %get-tuple-element.24.landed, bf16[128,256]{1,0:T(8,128)(2,1)S(1)} %get-tuple-element.25.weights), custom_call_target="tpu_custom_call" | custom-call | flops 1000000000 | bytes 4194304 | tf_op jit(solution)/shard_map/early/pallas_call | solution.py:536
  13.1 0.0 collective-permute-done.1.landed
  13.1 4.2 %interior.1 = (f32[224,1152]{1,0:T(8,128)S(1)}, f32[192,1152]{1,0:T(8,128)S(1)}, f32[160,1024]{1,0:T(8,128)S(1)}, bf16[896,1152]{1,0:T(8,128)(2,1)S(1)}, bf16[76...) custom-call(f32[88,1152]{1,0:T(8,128)S(1)} %get-tuple-element.22.own, ...), custom_call_target="tpu_custom_call" | custom-call | flops 10000000 | bytes 41943 | tf_op jit(solution)/shard_map/interior/pallas_call | solution.py:561
  17.3 2.1 %collective-permute-done.2.first = f32[40,1152]{1,0:T(8,128)S(1)} collective-permute-done((f32[40,1152]{1,0:T(8,128)S(1)}, f32[40,1152]{1,0:T(8,128)S(1)}, u32[]{:S(2)}, u32[]{:S(2)}) %collective-permute-start.2) | collective-permute-done | bytes 184352 | tf_op jit(solution)/shard_map/ppermute | solution.py:559
  19.4 0.0 collective-permute-done.3.second
  19.4 1.3 %rim.1 = (f32[32,1024]{1,0:T(8,128)S(1)}, f32[64,1024]{1,0:T(8,128)S(1)}, f32[96,1024]{1,0:T(8,128)S(1)}, f32[16,8,128]{2,1,0:T(8,128)S(1)}) custom-call(f32[88,1152]{1,0:T(8,128)S(1)} %get-tuple-element.22.own.own1, f32[88,1152]{1,0:T(8,128)S(1)} %collective-permute-done.other.other1, f32[40,1152]{1,0:T(8,128)S(1)} %collective-permute-done.2.first, ...), custom_call_target="tpu_custom_call" | custom-call | tf_op jit(solution)/shard_map/rim/pallas_call | solution.py:581
  20.7 12.7 %all_to_all.5.sums = f32[16,8,128]{2,1,0:T(8,128)S(1)} all-to-all(f32[16,8,128]{2,1,0:T(8,128)S(1)} %get-tuple-element.41), channel_id=1, replica_groups=mesh['scene'=2,'tile'=8,'frame'=2] {'tile','frame'}, dimensions={0} | all-to-all | bytes 131072 | tf_op jit(solution)/shard_map/all_to_all | solution.py:595
  33.4 2.2 %update.1 = (f32[64,4096]{1,0:T(8,128)}, f32[64,4096]{1,0:T(8,128)}) custom-call(f32[224,1152]{1,0:T(8,128)S(1)} %get-tuple-element.28.base, f32[192,1152]{1,0:T(8,128)S(1)} %get-tuple-element.29.once, f32[160,1024]{1,0:T(8,128)S(1)} %get-tuple-element.30.twice, f32[32,1024]{1,0:T(8,128)S(1)} %get-tuple-element.37.base_rim, ...), custom_call_target="tpu_custom_call" | custom-call | tf_op jit(solution)/shard_map/update/pallas_call | solution.py:597
Async XLA Ops:
  6.0 1.9 %collective-permute-start = (f32[88,1152]{1,0:T(8,128)S(1)}, f32[88,1152]{1,0:T(8,128)S(1)}, u32[]{:S(2)}, u32[]{:S(2)}) collective-permute-start(f32[88,1152]{1,0:T(8,128)S(1)} %get-tuple-element.23), channel_id=1, source_target_pairs={{0,1},{1,0},{2,3},{3,2},{4,5},{5,4},{6,7},{7,6},{8,9},{9,8},{10,11... | collective-permute-start | bytes 1216520 | tf_op jit(solution)/shard_map/ppermute | solution.py:534
  8.0 5.1 %collective-permute-start.1 = (f32[9,512,128]{2,1,0:T(8,128)S(1)}, f32[9,512,128]{2,1,0:T(8,128)S(1)}, u32[]{:S(2)}, u32[]{:S(2)}) collective-permute-start(f32[9,512,128]{2,1,0:T(8,128)S(1)} %get-tuple-element.27), channel_id=1, source_target_pairs={{0,1},{1,0},{2,3},{3,2},{4,5},{5,4},{6,7},{7,6},{8,9},{9,8},{10,11... | collective-permute-start | bytes 7077896 | tf_op jit(solution)/shard_map/ppermute | solution.py:555
  8.4 11.0 %collective-permute-start.2 = (f32[40,1152]{1,0:T(8,128)S(1)}, f32[40,1152]{1,0:T(8,128)S(1)}, u32[]{:S(2)}, u32[]{:S(2)}) collective-permute-start(f32[40,1152]{1,0:T(8,128)S(1)} %get-tuple-element.31), channel_id=1, source_target_pairs={{0,2},{2,0},{4,6},{6,4},{8,10},{10,8},{12,14},{14,12},{1,3},{3,1},... | collective-permute-start | bytes 552968 | tf_op jit(solution)/shard_map/ppermute | solution.py:559
  11.1 8.4 %collective-permute-start.3 = (f32[40,1152]{1,0:T(8,128)S(1)}, f32[40,1152]{1,0:T(8,128)S(1)}, u32[]{:S(2)}, u32[]{:S(2)}) collective-permute-start(f32[40,1152]{1,0:T(8,128)S(1)} %get-tuple-element.32), channel_id=1, source_target_pairs={{2,4},{4,2},{6,8},{8,6},{10,12},{12,10},{3,5},{5,3},{7,9},{9,7},{1... | collective-permute-start | bytes 552968 | tf_op jit(solution)/shard_map/ppermute | solution.py:558

commit v5 on v4

--- a/solution.py
+++ b/solution.py
@@ -121,18 +121,22 @@
     half = wide // 2
 
     def load(c):
-        if c < blocks:
-            start = jnp.where(me == 0, 0, half) if c < blocks // 2 else jnp.where(me == 0, half, 0)
-            start = start + (c % (blocks // 2)) * LANES
-            target = mine if c < blocks // 2 else theirs
-            at = c % (blocks // 2)
-        else:
-            start = jnp.where(me == c - blocks, half, half - LANES)
-            target = mine if c == blocks else theirs
-            at = blocks // 2
+        start = jnp.where(me == 0, 0, half) if c < blocks // 2 else jnp.where(me == 0, half, 0)
+        start = start + (c % (blocks // 2)) * LANES
+        target = mine if c < blocks // 2 else theirs
+        at = c % (blocks // 2)
         source = obs.at[:, pl.ds(pl.multiple_of(start, LANES), LANES)]
         return pltpu.make_async_copy(source, target.at[at], sems.at[c])
 
+    def halo(from_theirs):
+        last = blocks // 2 - 1
+        source, target = (theirs, mine) if from_theirs else (mine, theirs)
+        at = jnp.where(me == 0, 0, last) if from_theirs else jnp.where(me == 0, last, 0)
+        return pltpu.make_async_copy(
+            source.at[at], target.at[blocks // 2], sems.at[blocks + 1 if from_theirs else blocks]
+        )
+
+    ahead = min(8, blocks)
     small = [
         pltpu.make_async_copy(far, near, small_sems.at[i])
         for i, (far, near) in enumerate(
@@ -141,7 +145,7 @@
     ]
     for copy in small:
         copy.start()
-    for c in range(blocks + 2):
+    for c in range(ahead):
         load(c).start()
     nothing = jnp.zeros((128, wide), BF16)
     top[0:128, :] = nothing
@@ -159,16 +163,22 @@
     left = adjoint_weights(table)
     weights[...] = left
 
-    for c in range(0, blocks, 2):
-        load(c).wait()
-        load(c + 1).wait()
-        for d in range(2):
+    cuts = [0, blocks // 2, blocks]
+    for c, end in zip(cuts, cuts[1:]):
+        step = end - c
+        for d in range(step):
+            load(c + d).wait()
+            if c + d + ahead < blocks:
+                load(c + d + ahead).start()
             cols = slice((c + d) * LANES, (c + d + 1) * LANES)
-            landed, at = (mine, c + d) if c < blocks // 2 else (theirs, c + d - blocks // 2)
+            landed, at = (mine, c + d) if c + d < blocks // 2 else (theirs, c + d - blocks // 2)
             for r in range(3):
                 keep(top, 2 + r, cols, *split(landed[at, pl.ds(r, frames, stride=count), :]))
                 keep(bottom, r, cols, *split(landed[at, pl.ds(count - 3 + r, frames, stride=count), :]))
-        cols = slice(c * LANES, (c + 2) * LANES)
+        if end == blocks:
+            halo(False).start()
+            halo(True).start()
+        cols = slice(c * LANES, (c + step) * LANES)
         a, b = two_rows(left, top[0:256, cols])
         mixed[0:32, cols] = a
         mixed[32:64, cols] = b
@@ -185,8 +195,8 @@
         image = moved_image(mixed[r * 32 : r * 32 + 32, :], me)
         for g in range(2):
             put_halves(own, send, r * 16 + 8 * g, image[g], me)
-    load(blocks).wait()
-    load(blocks + 1).wait()
+    halo(False).wait()
+    halo(True).wait()
 
 
 def inner_sums(landed, left, stack, mixed):
@@ -211,7 +221,7 @@
     inner_sums(landed, weights[...], stack, mixed)
 
 
-def border_kernel(own, other, passed, first, second, onward):
+def border_kernel(own, other, passed, made, first, second, onward):
     even = lax.rem(lax.axis_index("tile"), 2) == 0
     edge = own[0:16] + other[0:16]
     phase = row_phase((8, own.shape[1]))
@@ -416,17 +426,22 @@
         value = finished(t, field, near)[:, :half]
         twice_rim[i * 16 : i * 16 + 16] = value
         totals[3] += folded(field[:, :half], value)
-    lines = jnp.concatenate([jnp.sum(t, axis=0, keepdims=True) for t in totals], axis=0)
-    lines = jnp.concatenate([lines, jnp.zeros((4, LANES), F32)], axis=0)
-    for p in range(sums.shape[0]):
-        sums[p] = lines
+    lane = lax.broadcasted_iota(I32, (1, LANES), 1) >> 5
+    line = jnp.zeros((1, LANES), F32)
+    for i, t in enumerate(totals):
+        part = jnp.sum(t, axis=0, keepdims=True)
+        part = part + pltpu.roll(part, 64, 1)
+        part = part + pltpu.roll(part, 32, 1)
+        line = jnp.where(lane == i, part, line)
+    sums[...] = jnp.broadcast_to(line, sums.shape)
 
 
 def update_kernel(base, once, twice, base_rim, once_rim, twice_rim, spread, sums, solution, residual, near_x, near_r, sems):
-    lanes = jnp.sum(sums[...], axis=0)
+    lanes = jnp.sum(sums[...], axis=0, keepdims=True)
+    kind = lax.broadcasted_iota(I32, lanes.shape, 1) >> 5
 
     def total(at):
-        return jnp.sum(lanes[at : at + 1], axis=1, keepdims=True)
+        return jnp.sum(jnp.where(kind == at, lanes, 0.0), axis=1, keepdims=True)
 
     bb, bm, mm, mmm = [total(at) for at in range(4)]
     alpha = bb / bm
@@ -546,12 +561,12 @@
     first, second, theirs = pl.pallas_call(
         border_kernel,
         out_shape=(shape((40, ext), F32), shape((40, ext), F32), shape(theirs.shape, F32)),
-        in_specs=vmem(3),
-        out_specs=tuple(vmem(3)),
+        in_specs=vmem(2) + [pl.BlockSpec(memory_space=pl.ANY)] * 2,
+        out_specs=tuple(vmem(2)) + (pl.BlockSpec(memory_space=pl.ANY),),
         input_output_aliases={2: 2},
         compiler_params=params(),
         name="border",
-    )(own, other, theirs)
+    )(own, other, theirs, ours)
     theirs = lax.ppermute(theirs, "frame", [(0, 1), (1, 0)])
     pairs = [(i, i ^ 1) for i in range(tiles) if i ^ 1 < tiles]
     odd_pairs = [p for i in range(1, tiles - 1, 2) for p in ((i, i + 1), (i + 1, i))]
@@ -584,7 +599,7 @@
             shape((32, half), F32),
             shape((64, half), F32),
             shape((96, half), F32),
-            shape((peers, 8, LANES), F32),
+            shape((peers, LANES), F32),
         ),
         in_specs=vmem(10),
         out_specs=tuple(vmem(4)),

time: 35.9 us -> 34.5 us (0.961)
  Pallas kernels: 14.5 us -> 13.6 us
  blocking collectives: 12.7 us -> 12.2 us
    ppermute x1, waiting for transfers between devices: 1.37 us -> 0.05 us  [per_device(): other = lax.ppermute(send, 'frame', [(0, 1), (1, 0)])]
    pallas_call x1, Pallas kernels: 5.38 us -> 4.34 us  [per_device(): pl.pallas_call(outer_kernel, out_shape=(shape((blocks // 2 + 1, frames *...]
    ppermute x1, waiting for transfers between devices: 0.01 us -> 0.78 us  [per_device(): theirs = lax.ppermute(theirs, 'frame', [(0, 1), (1, 0)])]
    ppermute x1, waiting for transfers between devices: 2.12 us -> 2.67 us  [per_device(): first = lax.ppermute(first, 'tile', pairs)]
    all_to_all x1, blocking collectives: 12.7 us -> 12.2 us  [per_device(): sums = lax.all_to_all(sums, ('tile', 'frame'), 0, 0)]
  transfers between devices with their start and end apart: 4 -> 4, of which waited for: 2 -> 3; matrix products, arithmetic and copies ran while one was open for 0% -> 0% of each run, Pallas kernels for 16% -> 16%
where the time goes in v5:
time: 34.5 us; the launch traced here: 34.2 us
  Pallas kernels  13.6 us (39%)
  blocking collectives  12.2 us (35%)
  starting transfers between devices  4.28 us (12%)
  waiting for transfers between devices  3.5 us (10%)
  between operations  0.67 us (2%)
    all_to_all x1, blocking collectives, per_device(): sums = lax.all_to_all(sums, ('tile', 'frame'), 0, 0)  12.2 us
    pallas_call x1, Pallas kernels, per_device(): pl.pallas_call(outer_kernel, out_shape=(shape((blocks // 2 + 1, frames *...  4.34 us
    pallas_call x1, Pallas kernels, per_device(): pl.pallas_call(interior_kernel, out_shape=(shape(((inner + 2) * 16, ext),...  4.25 us
    ppermute x1, starting transfers between devices, per_device(): first = lax.ppermute(first, 'tile', pairs)  2.71 us
    ppermute x1, waiting for transfers between devices, per_device(): first = lax.ppermute(first, 'tile', pairs)  2.67 us
    pallas_call x1, Pallas kernels, per_device(): pl.pallas_call(update_kernel, out_shape=(shape((count * 4, 4 * half), F32...  2.2 us
    pallas_call x1, Pallas kernels, per_device(): pl.pallas_call(rim_kernel, out_shape=(shape((32, half), F32), shape((64,...  1.41 us
    pallas_call x1, Pallas kernels, per_device(): pl.pallas_call(early_kernel, out_shape=shape((inner * 32, ext), F32), in_...  1.31 us
  transfers between devices with their start and end apart: 4, of which 3 were waited for; matrix products, arithmetic and copies ran while one was open for 0% of the time, Pallas kernels for 16%

profile of v5, /device:TPU:0, one launch (start us, length us, event | category | flops | bytes accessed | tf_op | source)
XLA Modules:
  0.0 34.2 jit_solution(12939165107558551187)
XLA Ops:
  0.6 4.3 %outer.1 = (f32[9,512,128]{2,1,0:T(8,128)S(1)}, f32[9,512,128]{2,1,0:T(8,128)S(1)}, f32[88,1152]{1,0:T(8,128)S(1)}, f32[88,1152]{1,0:T(8,128)S(1)}, bf16[128,256]{1,0:T(8,128)(2,1)S(1)}) custom-call(s32[2,32]{1,0:T(2,128)} %far_shift.1, s32[1,32]{1,0:T(1,128)} %far_ids.1, s32[1,32]{1,0:T(1,128)} %far_members.1, f32[5,8,5]{2,1,0:T(8,128)} %bitcast.9, ...), custom_call_target="tpu_custom_call" | custom-call | tf_op jit(solution)/shard_map/outer/pallas_call | solution.py:518
  5.0 0.5 %collective-permute-start = (f32[88,1152]{1,0:T(8,128)S(1)}, f32[88,1152]{1,0:T(8,128)S(1)}, u32[]{:S(2)}, u32[]{:S(2)}) collective-permute-start(f32[88,1152]{1,0:T(8,128)S(1)} %get-tuple-element.23), channel_id=1, source_target_pairs={{0,1},{1,0},{2,3},{3,2},{4,5},{5,4},{6,7},{7,6},{8,9},{9,8},{10,11... | collective-permute-start | bytes 1216520 | tf_op jit(solution)/shard_map/ppermute | solution.py:549
  5.5 1.3 %early.1.made.ours = f32[384,1152]{1,0:T(8,128)S(1)} custom-call(f32[9,512,128]{2,1,0:T(8,128)S(1)} %get-tuple-element.24.landed, bf16[128,256]{1,0:T(8,128)(2,1)S(1)} %get-tuple-element.25.weights), custom_call_target="tpu_custom_call" | custom-call | flops 1000000000 | bytes 4194304 | tf_op jit(solution)/shard_map/early/pallas_call | solution.py:551
  6.8 0.1 collective-permute-done.other.other1
  6.8 0.1 border.1
  6.9 0.4 %collective-permute-start.1 = (f32[9,512,128]{2,1,0:T(8,128)S(1)}, f32[9,512,128]{2,1,0:T(8,128)S(1)}, u32[]{:S(2)}, u32[]{:S(2)}) collective-permute-start(f32[9,512,128]{2,1,0:T(8,128)S(1)} %get-tuple-element.27), channel_id=1, source_target_pairs={{0,1},{1,0},{2,3},{3,2},{4,5},{5,4},{6,7},{7,6},{8,9},{9,8},{10,11... | collective-permute-start | bytes 7077896 | tf_op jit(solution)/shard_map/ppermute | solution.py:570
  7.3 2.7 %collective-permute-start.2 = (f32[40,1152]{1,0:T(8,128)S(1)}, f32[40,1152]{1,0:T(8,128)S(1)}, u32[]{:S(2)}, u32[]{:S(2)}) collective-permute-start(f32[40,1152]{1,0:T(8,128)S(1)} %get-tuple-element.31), channel_id=1, source_target_pairs={{0,2},{2,0},{4,6},{6,4},{8,10},{10,8},{12,14},{14,12},{1,3},{3,1},... | collective-permute-start | bytes 552968 | tf_op jit(solution)/shard_map/ppermute | solution.py:574
  10.0 0.7 %collective-permute-start.3 = (f32[40,1152]{1,0:T(8,128)S(1)}, f32[40,1152]{1,0:T(8,128)S(1)}, u32[]{:S(2)}, u32[]{:S(2)}) collective-permute-start(f32[40,1152]{1,0:T(8,128)S(1)} %get-tuple-element.32), channel_id=1, source_target_pairs={{2,4},{4,2},{6,8},{8,6},{10,12},{12,10},{3,5},{5,3},{7,9},{9,7},{1... | collective-permute-start | bytes 552968 | tf_op jit(solution)/shard_map/ppermute | solution.py:573
  10.7 0.8 %collective-permute-done.1.landed = f32[9,512,128]{2,1,0:T(8,128)S(1)} collective-permute-done((f32[9,512,128]{2,1,0:T(8,128)S(1)}, f32[9,512,128]{2,1,0:T(8,128)S(1)}, u32[]{:S(2)}, u32[]{:S(2)}) %collective-permute-start.1) | collective-permute-done | bytes 2359328 | tf_op jit(solution)/shard_map/ppermute | solution.py:570
  11.5 4.2 %interior.1 = (f32[224,1152]{1,0:T(8,128)S(1)}, f32[192,1152]{1,0:T(8,128)S(1)}, f32[160,1024]{1,0:T(8,128)S(1)}, bf16[896,1152]{1,0:T(8,128)(2,1)S(1)}, bf16[76...) custom-call(f32[88,1152]{1,0:T(8,128)S(1)} %get-tuple-element.22.own, ...), custom_call_target="tpu_custom_call" | custom-call | flops 10000000 | bytes 41943 | tf_op jit(solution)/shard_map/interior/pallas_call | solution.py:576
  15.7 2.7 %collective-permute-done.2.first = f32[40,1152]{1,0:T(8,128)S(1)} collective-permute-done((f32[40,1152]{1,0:T(8,128)S(1)}, f32[40,1152]{1,0:T(8,128)S(1)}, u32[]{:S(2)}, u32[]{:S(2)}) %collective-permute-start.2) | collective-permute-done | bytes 184352 | tf_op jit(solution)/shard_map/ppermute | solution.py:574
  18.4 0.0 collective-permute-done.3.second
  18.4 1.4 %rim.1 = (f32[32,1024]{1,0:T(8,128)S(1)}, f32[64,1024]{1,0:T(8,128)S(1)}, f32[96,1024]{1,0:T(8,128)S(1)}, f32[16,128]{1,0:T(8,128)S(1)}) custom-call(f32[88,1152]{1,0:T(8,128)S(1)} %get-tuple-element.22.own.own1, f32[88,1152]{1,0:T(8,128)S(1)} %collective-permute-done.other.other1, f32[40,1152]{1,0:T(8,128)S(1)} %collective-permute-done.2.first, ...), custom_call_target="tpu_custom_call" | custom-call | tf_op jit(solution)/shard_map/rim/pallas_call | solution.py:596
  19.8 12.2 %all_to_all.11 = f32[16,1,128]{2,1,0:T(1,128)S(1)} all-to-all(f32[16,1,128]{2,1,0:T(1,128)S(1)} %bitcast.7), channel_id=1, replica_groups=mesh['scene'=2,'tile'=8,'frame'=2] {'tile','frame'}, dimensions={0} | all-to-all | bytes 16384 | tf_op jit(solution)/shard_map/all_to_all | solution.py:610
  32.0 2.2 %update.1 = (f32[64,4096]{1,0:T(8,128)}, f32[64,4096]{1,0:T(8,128)}) custom-call(f32[224,1152]{1,0:T(8,128)S(1)} %get-tuple-element.28.base, f32[192,1152]{1,0:T(8,128)S(1)} %get-tuple-element.29.once, f32[160,1024]{1,0:T(8,128)S(1)} %get-tuple-element.30.twice, f32[32,1024]{1,0:T(8,128)S(1)} %get-tuple-element.37.base_rim, ...), custom_call_target="tpu_custom_call" | custom-call | tf_op jit(solution)/shard_map/update/pallas_call | solution.py:612
Async XLA Ops:
  5.0 1.8 %collective-permute-start = (f32[88,1152]{1,0:T(8,128)S(1)}, f32[88,1152]{1,0:T(8,128)S(1)}, u32[]{:S(2)}, u32[]{:S(2)}) collective-permute-start(f32[88,1152]{1,0:T(8,128)S(1)} %get-tuple-element.23), channel_id=1, source_target_pairs={{0,1},{1,0},{2,3},{3,2},{4,5},{5,4},{6,7},{7,6},{8,9},{9,8},{10,11... | collective-permute-start | bytes 1216520 | tf_op jit(solution)/shard_map/ppermute | solution.py:549
  6.9 4.6 %collective-permute-start.1 = (f32[9,512,128]{2,1,0:T(8,128)S(1)}, f32[9,512,128]{2,1,0:T(8,128)S(1)}, u32[]{:S(2)}, u32[]{:S(2)}) collective-permute-start(f32[9,512,128]{2,1,0:T(8,128)S(1)} %get-tuple-element.27), channel_id=1, source_target_pairs={{0,1},{1,0},{2,3},{3,2},{4,5},{5,4},{6,7},{7,6},{8,9},{9,8},{10,11... | collective-permute-start | bytes 7077896 | tf_op jit(solution)/shard_map/ppermute | solution.py:570
  7.3 11.1 %collective-permute-start.2 = (f32[40,1152]{1,0:T(8,128)S(1)}, f32[40,1152]{1,0:T(8,128)S(1)}, u32[]{:S(2)}, u32[]{:S(2)}) collective-permute-start(f32[40,1152]{1,0:T(8,128)S(1)} %get-tuple-element.31), channel_id=1, source_target_pairs={{0,2},{2,0},{4,6},{6,4},{8,10},{10,8},{12,14},{14,12},{1,3},{3,1},... | collective-permute-start | bytes 552968 | tf_op jit(solution)/shard_map/ppermute | solution.py:574
  10.0 8.4 %collective-permute-start.3 = (f32[40,1152]{1,0:T(8,128)S(1)}, f32[40,1152]{1,0:T(8,128)S(1)}, u32[]{:S(2)}, u32[]{:S(2)}) collective-permute-start(f32[40,1152]{1,0:T(8,128)S(1)} %get-tuple-element.32), channel_id=1, source_target_pairs={{2,4},{4,2},{6,8},{8,6},{10,12},{12,10},{3,5},{5,3},{7,9},{9,7},{1... | collective-permute-start | bytes 552968 | tf_op jit(solution)/shard_map/ppermute | solution.py:573

commit v6 on v5

--- a/solution.py
+++ b/solution.py
@@ -229,10 +229,35 @@
     below = jnp.where(phase < 2, edge[0:8], pltpu.roll(edge[8:16], 2, 0))
     top = own[16:48] + other[16:48]
     bottom = own[48:80] + other[48:80]
-    first[0:32] = jnp.where(even, bottom, top)
-    first[32:40] = jnp.where(even, below, above)
-    second[0:32] = jnp.where(even, top, bottom)
-    second[32:40] = jnp.where(even, above, below)
+    here = lax.axis_index("frame")
+    half = own.shape[1] - LANES
+    kind = lax.broadcasted_iota(I32, (8, LANES), 1) >> 3
+
+    def pack(ref, rows, last):
+        tail = jnp.zeros((8, LANES), F32)
+        for g in range(5):
+            value = last if g == 4 else rows[8 * g : 8 * g + 8]
+            for c in range(half // LANES):
+                ref[g * (half // LANES) + c] = value[:, c * LANES : (c + 1) * LANES]
+            spare = value[:, half:] if g == 0 else pltpu.roll(value[:, half:], 8 * g, 1)
+            tail = jnp.where(kind == jnp.where(here == 0, g, (15 + g) % 16), spare, tail)
+        ref[5 * (half // LANES)] = tail
+
+    pack(first, jnp.where(even, bottom, top), jnp.where(even, below, above))
+    pack(second, jnp.where(even, top, bottom), jnp.where(even, above, below))
+
+
+def unpacked(tiles):
+    per = tiles.shape[0] // 5
+    kind = lax.broadcasted_iota(I32, (8, LANES), 1) >> 3
+    mine = kind == jnp.where(lax.axis_index("frame") == 0, 0, 15)
+    groups = []
+    for g in range(5):
+        tail = tiles[5 * per] if g == 0 else pltpu.roll(tiles[5 * per], LANES - 8 * g, 1)
+        groups.append(
+            jnp.concatenate([tiles[g * per + c] for c in range(per)] + [jnp.where(mine, tail, 0.0)], axis=1)
+        )
+    return jnp.concatenate(groups, axis=0)
 
 
 def halo_mask():
@@ -376,8 +401,8 @@
     below2[0:128] = stack2[(inner - 4) * 64 : (inner - 2) * 64]
 
     edge = own[0:16] + other[0:16]
-    up = jnp.where(even, second[...], first[...])
-    down = jnp.where(even, first[...], second[...])
+    up = unpacked(jnp.where(even, second[...], first[...]))
+    down = unpacked(jnp.where(even, first[...], second[...]))
     rows = {-2: up[0:16]}
     rows[-1] = up[16:32] + has_up * jnp.where(phase >= 2, edge, 0.0)
     e = up[32:40]
@@ -558,9 +583,10 @@
         cost_estimate=cost(1),
         name="early",
     )(mine, weights)
+    halo = (5 * half // LANES + 1, 8, LANES)
     first, second, theirs = pl.pallas_call(
         border_kernel,
-        out_shape=(shape((40, ext), F32), shape((40, ext), F32), shape(theirs.shape, F32)),
+        out_shape=(shape(halo, F32), shape(halo, F32), shape(theirs.shape, F32)),
         in_specs=vmem(2) + [pl.BlockSpec(memory_space=pl.ANY)] * 2,
         out_specs=tuple(vmem(2)) + (pl.BlockSpec(memory_space=pl.ANY),),
         input_output_aliases={2: 2},

time: 34.5 us -> 34.2 us (level)
  waiting for transfers between devices: 3.5 us -> 2.84 us
    ppermute x1, waiting for transfers between devices: 2.67 us -> 2 us  [per_device(): first = lax.ppermute(first, 'tile', pairs)]
where the time goes in v6:
time: 34.2 us; the launch traced here: 34 us
  Pallas kernels  13.7 us (40%)
  blocking collectives  12.5 us (37%)
  starting transfers between devices  4.26 us (12%)
  waiting for transfers between devices  2.84 us (8%)
  between operations  0.66 us (2%)
    all_to_all x1, blocking collectives, per_device(): sums = lax.all_to_all(sums, ('tile', 'frame'), 0, 0)  12.5 us
    pallas_call x1, Pallas kernels, per_device(): pl.pallas_call(outer_kernel, out_shape=(shape((blocks // 2 + 1, frames *...  4.34 us
    pallas_call x1, Pallas kernels, per_device(): pl.pallas_call(interior_kernel, out_shape=(shape(((inner + 2) * 16, ext),...  4.25 us
    ppermute x1, starting transfers between devices, per_device(): first = lax.ppermute(first, 'tile', pairs)  2.71 us
    pallas_call x1, Pallas kernels, per_device(): pl.pallas_call(update_kernel, out_shape=(shape((count * 4, 4 * half), F32...  2.2 us
    ppermute x1, waiting for transfers between devices, per_device(): first = lax.ppermute(first, 'tile', pairs)  2 us
    pallas_call x1, Pallas kernels, per_device(): pl.pallas_call(rim_kernel, out_shape=(shape((32, half), F32), shape((64,...  1.51 us
    pallas_call x1, Pallas kernels, per_device(): pl.pallas_call(early_kernel, out_shape=shape((inner * 32, ext), F32), in_...  1.31 us
  transfers between devices with their start and end apart: 4, of which 3 were waited for; matrix products, arithmetic and copies ran while one was open for 0% of the time, Pallas kernels for 16%

profile of v6, /device:TPU:0, one launch (start us, length us, event | category | flops | bytes accessed | tf_op | source)
XLA Modules:
  0.0 34.0 jit_solution(15867469651630747944)
XLA Ops:
  0.6 4.3 %outer.1 = (f32[9,512,128]{2,1,0:T(8,128)S(1)}, f32[9,512,128]{2,1,0:T(8,128)S(1)}, f32[88,1152]{1,0:T(8,128)S(1)}, f32[88,1152]{1,0:T(8,128)S(1)}, bf16[128,256]{1,0:T(8,128)(2,1)S(1)}) custom-call(s32[2,32]{1,0:T(2,128)} %far_shift.1, s32[1,32]{1,0:T(1,128)} %far_ids.1, s32[1,32]{1,0:T(1,128)} %far_members.1, f32[5,8,5]{2,1,0:T(8,128)} %bitcast.9, ...), custom_call_target="tpu_custom_call" | custom-call | tf_op jit(solution)/shard_map/outer/pallas_call | solution.py:543
  5.0 0.5 %collective-permute-start = (f32[88,1152]{1,0:T(8,128)S(1)}, f32[88,1152]{1,0:T(8,128)S(1)}, u32[]{:S(2)}, u32[]{:S(2)}) collective-permute-start(f32[88,1152]{1,0:T(8,128)S(1)} %get-tuple-element.23), channel_id=1, source_target_pairs={{0,1},{1,0},{2,3},{3,2},{4,5},{5,4},{6,7},{7,6},{8,9},{9,8},{10,11... | collective-permute-start | bytes 1216520 | tf_op jit(solution)/shard_map/ppermute | solution.py:574
  5.5 1.3 %early.1.made.ours = f32[384,1152]{1,0:T(8,128)S(1)} custom-call(f32[9,512,128]{2,1,0:T(8,128)S(1)} %get-tuple-element.24.landed, bf16[128,256]{1,0:T(8,128)(2,1)S(1)} %get-tuple-element.25.weights), custom_call_target="tpu_custom_call" | custom-call | flops 1000000000 | bytes 4194304 | tf_op jit(solution)/shard_map/early/pallas_call | solution.py:576
  6.8 0.1 collective-permute-done.other.other1
  6.8 0.1 border.1
  6.9 0.4 %collective-permute-start.1 = (f32[9,512,128]{2,1,0:T(8,128)S(1)}, f32[9,512,128]{2,1,0:T(8,128)S(1)}, u32[]{:S(2)}, u32[]{:S(2)}) collective-permute-start(f32[9,512,128]{2,1,0:T(8,128)S(1)} %get-tuple-element.27), channel_id=1, source_target_pairs={{0,1},{1,0},{2,3},{3,2},{4,5},{5,4},{6,7},{7,6},{8,9},{9,8},{10,11... | collective-permute-start | bytes 7077896 | tf_op jit(solution)/shard_map/ppermute | solution.py:596
  7.3 2.7 %collective-permute-start.2 = (f32[41,8,128]{2,1,0:T(8,128)S(1)}, f32[41,8,128]{2,1,0:T(8,128)S(1)}, u32[]{:S(2)}, u32[]{:S(2)}) collective-permute-start(f32[41,8,128]{2,1,0:T(8,128)S(1)} %get-tuple-element.31), channel_id=1, source_target_pairs={{0,2},{2,0},{4,6},{6,4},{8,10},{10,8},{12,14},{14,12},{1,3},{3,1},... | collective-permute-start | bytes 503816 | tf_op jit(solution)/shard_map/ppermute | solution.py:600
  10.0 0.7 %collective-permute-start.3 = (f32[41,8,128]{2,1,0:T(8,128)S(1)}, f32[41,8,128]{2,1,0:T(8,128)S(1)}, u32[]{:S(2)}, u32[]{:S(2)}) collective-permute-start(f32[41,8,128]{2,1,0:T(8,128)S(1)} %get-tuple-element.32), channel_id=1, source_target_pairs={{2,4},{4,2},{6,8},{8,6},{10,12},{12,10},{3,5},{5,3},{7,9},{9,7},{1... | collective-permute-start | bytes 503816 | tf_op jit(solution)/shard_map/ppermute | solution.py:599
  10.7 0.8 %collective-permute-done.1.landed = f32[9,512,128]{2,1,0:T(8,128)S(1)} collective-permute-done((f32[9,512,128]{2,1,0:T(8,128)S(1)}, f32[9,512,128]{2,1,0:T(8,128)S(1)}, u32[]{:S(2)}, u32[]{:S(2)}) %collective-permute-start.1) | collective-permute-done | bytes 2359328 | tf_op jit(solution)/shard_map/ppermute | solution.py:596
  11.5 4.2 %interior.1 = (f32[224,1152]{1,0:T(8,128)S(1)}, f32[192,1152]{1,0:T(8,128)S(1)}, f32[160,1024]{1,0:T(8,128)S(1)}, bf16[896,1152]{1,0:T(8,128)(2,1)S(1)}, bf16[76...) custom-call(f32[88,1152]{1,0:T(8,128)S(1)} %get-tuple-element.22.own, ...), custom_call_target="tpu_custom_call" | custom-call | flops 10000000 | bytes 41943 | tf_op jit(solution)/shard_map/interior/pallas_call | solution.py:602
  15.8 2.0 %collective-permute-done.2.first = f32[41,8,128]{2,1,0:T(8,128)S(1)} collective-permute-done((f32[41,8,128]{2,1,0:T(8,128)S(1)}, f32[41,8,128]{2,1,0:T(8,128)S(1)}, u32[]{:S(2)}, u32[]{:S(2)}) %collective-permute-start.2) | collective-permute-done | bytes 167968 | tf_op jit(solution)/shard_map/ppermute | solution.py:600
  17.7 0.0 collective-permute-done.3.second
  17.8 1.5 %rim.1 = (f32[32,1024]{1,0:T(8,128)S(1)}, f32[64,1024]{1,0:T(8,128)S(1)}, f32[96,1024]{1,0:T(8,128)S(1)}, f32[16,128]{1,0:T(8,128)S(1)}) custom-call(f32[88,1152]{1,0:T(8,128)S(1)} %get-tuple-element.22.own.own1, f32[88,1152]{1,0:T(8,128)S(1)} %collective-permute-done.other.other1, f32[41,8,128]{2,1,0:T(8,128)S(1)} %collective-permute-done.2.first, ...), custom_call_target="tpu_custom_call" | custom-call | tf_op jit(solution)/shard_map/rim/pallas_call | solution.py:622
  19.3 12.5 %all_to_all.11 = f32[16,1,128]{2,1,0:T(1,128)S(1)} all-to-all(f32[16,1,128]{2,1,0:T(1,128)S(1)} %bitcast.7), channel_id=1, replica_groups=mesh['scene'=2,'tile'=8,'frame'=2] {'tile','frame'}, dimensions={0} | all-to-all | bytes 16384 | tf_op jit(solution)/shard_map/all_to_all | solution.py:636
  31.8 2.2 %update.1 = (f32[64,4096]{1,0:T(8,128)}, f32[64,4096]{1,0:T(8,128)}) custom-call(f32[224,1152]{1,0:T(8,128)S(1)} %get-tuple-element.28.base, f32[192,1152]{1,0:T(8,128)S(1)} %get-tuple-element.29.once, f32[160,1024]{1,0:T(8,128)S(1)} %get-tuple-element.30.twice, f32[32,1024]{1,0:T(8,128)S(1)} %get-tuple-element.37.base_rim, ...), custom_call_target="tpu_custom_call" | custom-call | tf_op jit(solution)/shard_map/update/pallas_call | solution.py:638
Async XLA Ops:
  5.0 1.8 %collective-permute-start = (f32[88,1152]{1,0:T(8,128)S(1)}, f32[88,1152]{1,0:T(8,128)S(1)}, u32[]{:S(2)}, u32[]{:S(2)}) collective-permute-start(f32[88,1152]{1,0:T(8,128)S(1)} %get-tuple-element.23), channel_id=1, source_target_pairs={{0,1},{1,0},{2,3},{3,2},{4,5},{5,4},{6,7},{7,6},{8,9},{9,8},{10,11... | collective-permute-start | bytes 1216520 | tf_op jit(solution)/shard_map/ppermute | solution.py:574
  6.9 4.6 %collective-permute-start.1 = (f32[9,512,128]{2,1,0:T(8,128)S(1)}, f32[9,512,128]{2,1,0:T(8,128)S(1)}, u32[]{:S(2)}, u32[]{:S(2)}) collective-permute-start(f32[9,512,128]{2,1,0:T(8,128)S(1)} %get-tuple-element.27), channel_id=1, source_target_pairs={{0,1},{1,0},{2,3},{3,2},{4,5},{5,4},{6,7},{7,6},{8,9},{9,8},{10,11... | collective-permute-start | bytes 7077896 | tf_op jit(solution)/shard_map/ppermute | solution.py:596
  7.3 10.4 %collective-permute-start.2 = (f32[41,8,128]{2,1,0:T(8,128)S(1)}, f32[41,8,128]{2,1,0:T(8,128)S(1)}, u32[]{:S(2)}, u32[]{:S(2)}) collective-permute-start(f32[41,8,128]{2,1,0:T(8,128)S(1)} %get-tuple-element.31), channel_id=1, source_target_pairs={{0,2},{2,0},{4,6},{6,4},{8,10},{10,8},{12,14},{14,12},{1,3},{3,1},... | collective-permute-start | bytes 503816 | tf_op jit(solution)/shard_map/ppermute | solution.py:600
  10.0 7.7 %collective-permute-start.3 = (f32[41,8,128]{2,1,0:T(8,128)S(1)}, f32[41,8,128]{2,1,0:T(8,128)S(1)}, u32[]{:S(2)}, u32[]{:S(2)}) collective-permute-start(f32[41,8,128]{2,1,0:T(8,128)S(1)} %get-tuple-element.32), channel_id=1, source_target_pairs={{2,4},{4,2},{6,8},{8,6},{10,12},{12,10},{3,5},{5,3},{7,9},{9,7},{1... | collective-permute-start | bytes 503816 | tf_op jit(solution)/shard_map/ppermute | solution.py:599

commit v7 on v6

--- a/solution.py
+++ b/solution.py
@@ -136,7 +136,7 @@
             source.at[at], target.at[blocks // 2], sems.at[blocks + 1 if from_theirs else blocks]
         )
 
-    ahead = min(8, blocks)
+    ahead = min(10, blocks)
     small = [
         pltpu.make_async_copy(far, near, small_sems.at[i])
         for i, (far, near) in enumerate(
@@ -147,9 +147,6 @@
         copy.start()
     for c in range(ahead):
         load(c).start()
-    nothing = jnp.zeros((128, wide), BF16)
-    top[0:128, :] = nothing
-    bottom[192:320, :] = nothing
     for copy in small:
         copy.wait()
     table = tap_table(shift, ids, members, kernels, gains)
@@ -163,7 +160,7 @@
     left = adjoint_weights(table)
     weights[...] = left
 
-    cuts = [0, blocks // 2, blocks]
+    cuts = [0, blocks // 2, 3 * blocks // 4, blocks]
     for c, end in zip(cuts, cuts[1:]):
         step = end - c
         for d in range(step):
@@ -173,18 +170,18 @@
             cols = slice((c + d) * LANES, (c + d + 1) * LANES)
             landed, at = (mine, c + d) if c + d < blocks // 2 else (theirs, c + d - blocks // 2)
             for r in range(3):
-                keep(top, 2 + r, cols, *split(landed[at, pl.ds(r, frames, stride=count), :]))
+                keep(top, r, cols, *split(landed[at, pl.ds(r, frames, stride=count), :]))
                 keep(bottom, r, cols, *split(landed[at, pl.ds(count - 3 + r, frames, stride=count), :]))
         if end == blocks:
             halo(False).start()
             halo(True).start()
         cols = slice(c * LANES, (c + step) * LANES)
-        a, b = two_rows(left, top[0:256, cols])
+        a, b = two_rows(left[:, 128:256], top[0:128, cols])
         mixed[0:32, cols] = a
         mixed[32:64, cols] = b
-        mixed[64:96, cols] = one_row(left, top[128:320, cols])
-        mixed[96:128, cols] = one_row(left, bottom[0:192, cols])
-        a, b = two_rows(left, bottom[64:320, cols])
+        mixed[64:96, cols] = one_row(left, top[:, cols])
+        mixed[96:128, cols] = one_row(left, bottom[:, cols])
+        a, b = two_rows(left[:, 0:128], bottom[64:192, cols])
         mixed[128:160, cols] = a
         mixed[160:192, cols] = b
 
@@ -552,8 +549,8 @@
         in_specs=[far] * 6,
         out_specs=tuple(vmem(5)),
         scratch_shapes=[
-            pltpu.VMEM((320, wide), BF16),
-            pltpu.VMEM((320, wide), BF16),
+            pltpu.VMEM((192, wide), BF16),
+            pltpu.VMEM((192, wide), BF16),
             pltpu.VMEM((192, wide), F32),
             pltpu.SemaphoreType.DMA((blocks + 2,)),
             pltpu.VMEM(frame_shift.shape, I32),

time: 34.2 us -> 34 us (level)
  no operation moved by 1% of the time
where the time goes in v7:
time: 34 us; the launch traced here: 33.8 us
  Pallas kernels  13.5 us (40%)
  blocking collectives  12.5 us (37%)
  starting transfers between devices  4.26 us (13%)
  waiting for transfers between devices  2.84 us (8%)
  between operations  0.66 us (2%)
    all_to_all x1, blocking collectives, per_device(): sums = lax.all_to_all(sums, ('tile', 'frame'), 0, 0)  12.5 us
    pallas_call x1, Pallas kernels, per_device(): pl.pallas_call(interior_kernel, out_shape=(shape(((inner + 2) * 16, ext),...  4.25 us
    pallas_call x1, Pallas kernels, per_device(): pl.pallas_call(outer_kernel, out_shape=(shape((blocks // 2 + 1, frames *...  4.13 us
    ppermute x1, starting transfers between devices, per_device(): first = lax.ppermute(first, 'tile', pairs)  2.67 us
    pallas_call x1, Pallas kernels, per_device(): pl.pallas_call(update_kernel, out_shape=(shape((count * 4, 4 * half), F32...  2.21 us
    ppermute x1, waiting for transfers between devices, per_device(): first = lax.ppermute(first, 'tile', pairs)  1.95 us
    pallas_call x1, Pallas kernels, per_device(): pl.pallas_call(rim_kernel, out_shape=(shape((32, half), F32), shape((64,...  1.51 us
    pallas_call x1, Pallas kernels, per_device(): pl.pallas_call(early_kernel, out_shape=shape((inner * 32, ext), F32), in_...  1.31 us
  transfers between devices with their start and end apart: 4, of which 3 were waited for; matrix products, arithmetic and copies ran while one was open for 0% of the time, Pallas kernels for 16%

profile of v7, /device:TPU:0, one launch (start us, length us, event | category | flops | bytes accessed | tf_op | source)
XLA Modules:
  0.0 33.8 jit_solution(8891829119481457854)
XLA Ops:
  0.6 4.1 %outer.1 = (f32[9,512,128]{2,1,0:T(8,128)S(1)}, f32[9,512,128]{2,1,0:T(8,128)S(1)}, f32[88,1152]{1,0:T(8,128)S(1)}, f32[88,1152]{1,0:T(8,128)S(1)}, bf16[128,256]{1,0:T(8,128)(2,1)S(1)}) custom-call(s32[2,32]{1,0:T(2,128)} %far_shift.1, s32[1,32]{1,0:T(1,128)} %far_ids.1, s32[1,32]{1,0:T(1,128)} %far_members.1, f32[5,8,5]{2,1,0:T(8,128)} %bitcast.9, ...), custom_call_target="tpu_custom_call" | custom-call | tf_op jit(solution)/shard_map/outer/pallas_call | solution.py:540
  4.8 0.5 %collective-permute-start = (f32[88,1152]{1,0:T(8,128)S(1)}, f32[88,1152]{1,0:T(8,128)S(1)}, u32[]{:S(2)}, u32[]{:S(2)}) collective-permute-start(f32[88,1152]{1,0:T(8,128)S(1)} %get-tuple-element.23), channel_id=1, source_target_pairs={{0,1},{1,0},{2,3},{3,2},{4,5},{5,4},{6,7},{7,6},{8,9},{9,8},{10,11... | collective-permute-start | bytes 1216520 | tf_op jit(solution)/shard_map/ppermute | solution.py:571
  5.3 1.3 %early.1.made.ours = f32[384,1152]{1,0:T(8,128)S(1)} custom-call(f32[9,512,128]{2,1,0:T(8,128)S(1)} %get-tuple-element.24.landed, bf16[128,256]{1,0:T(8,128)(2,1)S(1)} %get-tuple-element.25.weights), custom_call_target="tpu_custom_call" | custom-call | flops 1000000000 | bytes 4194304 | tf_op jit(solution)/shard_map/early/pallas_call | solution.py:573
  6.6 0.1 collective-permute-done.other.other1
  6.7 0.1 border.1
  6.8 0.4 %collective-permute-start.1 = (f32[9,512,128]{2,1,0:T(8,128)S(1)}, f32[9,512,128]{2,1,0:T(8,128)S(1)}, u32[]{:S(2)}, u32[]{:S(2)}) collective-permute-start(f32[9,512,128]{2,1,0:T(8,128)S(1)} %get-tuple-element.27), channel_id=1, source_target_pairs={{0,1},{1,0},{2,3},{3,2},{4,5},{5,4},{6,7},{7,6},{8,9},{9,8},{10,11... | collective-permute-start | bytes 7077896 | tf_op jit(solution)/shard_map/ppermute | solution.py:593
  7.2 2.7 %collective-permute-start.2 = (f32[41,8,128]{2,1,0:T(8,128)S(1)}, f32[41,8,128]{2,1,0:T(8,128)S(1)}, u32[]{:S(2)}, u32[]{:S(2)}) collective-permute-start(f32[41,8,128]{2,1,0:T(8,128)S(1)} %get-tuple-element.31), channel_id=1, source_target_pairs={{0,2},{2,0},{4,6},{6,4},{8,10},{10,8},{12,14},{14,12},{1,3},{3,1},... | collective-permute-start | bytes 503816 | tf_op jit(solution)/shard_map/ppermute | solution.py:597
  9.8 0.7 %collective-permute-start.3 = (f32[41,8,128]{2,1,0:T(8,128)S(1)}, f32[41,8,128]{2,1,0:T(8,128)S(1)}, u32[]{:S(2)}, u32[]{:S(2)}) collective-permute-start(f32[41,8,128]{2,1,0:T(8,128)S(1)} %get-tuple-element.32), channel_id=1, source_target_pairs={{2,4},{4,2},{6,8},{8,6},{10,12},{12,10},{3,5},{5,3},{7,9},{9,7},{1... | collective-permute-start | bytes 503816 | tf_op jit(solution)/shard_map/ppermute | solution.py:596
  10.5 0.8 %collective-permute-done.1.landed = f32[9,512,128]{2,1,0:T(8,128)S(1)} collective-permute-done((f32[9,512,128]{2,1,0:T(8,128)S(1)}, f32[9,512,128]{2,1,0:T(8,128)S(1)}, u32[]{:S(2)}, u32[]{:S(2)}) %collective-permute-start.1) | collective-permute-done | bytes 2359328 | tf_op jit(solution)/shard_map/ppermute | solution.py:593
  11.3 4.2 %interior.1 = (f32[224,1152]{1,0:T(8,128)S(1)}, f32[192,1152]{1,0:T(8,128)S(1)}, f32[160,1024]{1,0:T(8,128)S(1)}, bf16[896,1152]{1,0:T(8,128)(2,1)S(1)}, bf16[76...) custom-call(f32[88,1152]{1,0:T(8,128)S(1)} %get-tuple-element.22.own, ...), custom_call_target="tpu_custom_call" | custom-call | flops 10000000 | bytes 41943 | tf_op jit(solution)/shard_map/interior/pallas_call | solution.py:599
  15.6 2.0 %collective-permute-done.2.first = f32[41,8,128]{2,1,0:T(8,128)S(1)} collective-permute-done((f32[41,8,128]{2,1,0:T(8,128)S(1)}, f32[41,8,128]{2,1,0:T(8,128)S(1)}, u32[]{:S(2)}, u32[]{:S(2)}) %collective-permute-start.2) | collective-permute-done | bytes 167968 | tf_op jit(solution)/shard_map/ppermute | solution.py:597
  17.5 0.0 collective-permute-done.3.second
  17.5 1.5 %rim.1 = (f32[32,1024]{1,0:T(8,128)S(1)}, f32[64,1024]{1,0:T(8,128)S(1)}, f32[96,1024]{1,0:T(8,128)S(1)}, f32[16,128]{1,0:T(8,128)S(1)}) custom-call(f32[88,1152]{1,0:T(8,128)S(1)} %get-tuple-element.22.own.own1, f32[88,1152]{1,0:T(8,128)S(1)} %collective-permute-done.other.other1, f32[41,8,128]{2,1,0:T(8,128)S(1)} %collective-permute-done.2.first, ...), custom_call_target="tpu_custom_call" | custom-call | tf_op jit(solution)/shard_map/rim/pallas_call | solution.py:619
  19.1 12.5 %all_to_all.11 = f32[16,1,128]{2,1,0:T(1,128)S(1)} all-to-all(f32[16,1,128]{2,1,0:T(1,128)S(1)} %bitcast.7), channel_id=1, replica_groups=mesh['scene'=2,'tile'=8,'frame'=2] {'tile','frame'}, dimensions={0} | all-to-all | bytes 16384 | tf_op jit(solution)/shard_map/all_to_all | solution.py:633
  31.6 2.2 %update.1 = (f32[64,4096]{1,0:T(8,128)}, f32[64,4096]{1,0:T(8,128)}) custom-call(f32[224,1152]{1,0:T(8,128)S(1)} %get-tuple-element.28.base, f32[192,1152]{1,0:T(8,128)S(1)} %get-tuple-element.29.once, f32[160,1024]{1,0:T(8,128)S(1)} %get-tuple-element.30.twice, f32[32,1024]{1,0:T(8,128)S(1)} %get-tuple-element.37.base_rim, ...), custom_call_target="tpu_custom_call" | custom-call | tf_op jit(solution)/shard_map/update/pallas_call | solution.py:635
Async XLA Ops:
  4.8 1.9 %collective-permute-start = (f32[88,1152]{1,0:T(8,128)S(1)}, f32[88,1152]{1,0:T(8,128)S(1)}, u32[]{:S(2)}, u32[]{:S(2)}) collective-permute-start(f32[88,1152]{1,0:T(8,128)S(1)} %get-tuple-element.23), channel_id=1, source_target_pairs={{0,1},{1,0},{2,3},{3,2},{4,5},{5,4},{6,7},{7,6},{8,9},{9,8},{10,11... | collective-permute-start | bytes 1216520 | tf_op jit(solution)/shard_map/ppermute | solution.py:571
  6.8 4.6 %collective-permute-start.1 = (f32[9,512,128]{2,1,0:T(8,128)S(1)}, f32[9,512,128]{2,1,0:T(8,128)S(1)}, u32[]{:S(2)}, u32[]{:S(2)}) collective-permute-start(f32[9,512,128]{2,1,0:T(8,128)S(1)} %get-tuple-element.27), channel_id=1, source_target_pairs={{0,1},{1,0},{2,3},{3,2},{4,5},{5,4},{6,7},{7,6},{8,9},{9,8},{10,11... | collective-permute-start | bytes 7077896 | tf_op jit(solution)/shard_map/ppermute | solution.py:593
  7.2 10.4 %collective-permute-start.2 = (f32[41,8,128]{2,1,0:T(8,128)S(1)}, f32[41,8,128]{2,1,0:T(8,128)S(1)}, u32[]{:S(2)}, u32[]{:S(2)}) collective-permute-start(f32[41,8,128]{2,1,0:T(8,128)S(1)} %get-tuple-element.31), channel_id=1, source_target_pairs={{0,2},{2,0},{4,6},{6,4},{8,10},{10,8},{12,14},{14,12},{1,3},{3,1},... | collective-permute-start | bytes 503816 | tf_op jit(solution)/shard_map/ppermute | solution.py:597
  9.8 7.7 %collective-permute-start.3 = (f32[41,8,128]{2,1,0:T(8,128)S(1)}, f32[41,8,128]{2,1,0:T(8,128)S(1)}, u32[]{:S(2)}, u32[]{:S(2)}) collective-permute-start(f32[41,8,128]{2,1,0:T(8,128)S(1)} %get-tuple-element.32), channel_id=1, source_target_pairs={{2,4},{4,2},{6,8},{8,6},{10,12},{12,10},{3,5},{5,3},{7,9},{9,7},{1... | collective-permute-start | bytes 503816 | tf_op jit(solution)/shard_map/ppermute | solution.py:596

commit v8 on v7

--- a/solution.py
+++ b/solution.py
@@ -20,9 +20,7 @@
 
 
 def paired(table):
-    high, low = split(table)
-    second = (lax.broadcasted_iota(I32, table.shape, 1) >> 5) & 1
-    return jnp.concatenate([high, jnp.where(second == 0, low.astype(F32), 0.0).astype(BF16)], axis=0)
+    return jnp.concatenate(split(table), axis=0)
 
 
 def row_phase(shape):

time: 34 us -> 34 us (level)
  no operation moved by 1% of the time
where the time goes in v8:
time: 34 us; the launch traced here: 33.8 us
  Pallas kernels  13.5 us (40%)
  blocking collectives  12.5 us (37%)
  starting transfers between devices  4.26 us (13%)
  waiting for transfers between devices  2.82 us (8%)
  between operations  0.67 us (2%)
    all_to_all x1, blocking collectives, per_device(): sums = lax.all_to_all(sums, ('tile', 'frame'), 0, 0)  12.5 us
    pallas_call x1, Pallas kernels, per_device(): pl.pallas_call(interior_kernel, out_shape=(shape(((inner + 2) * 16, ext),...  4.26 us
    pallas_call x1, Pallas kernels, per_device(): pl.pallas_call(outer_kernel, out_shape=(shape((blocks // 2 + 1, frames *...  4.13 us
    ppermute x1, starting transfers between devices, per_device(): first = lax.ppermute(first, 'tile', pairs)  2.67 us
    pallas_call x1, Pallas kernels, per_device(): pl.pallas_call(update_kernel, out_shape=(shape((count * 4, 4 * half), F32...  2.2 us
    ppermute x1, waiting for transfers between devices, per_device(): first = lax.ppermute(first, 'tile', pairs)  1.94 us
    pallas_call x1, Pallas kernels, per_device(): pl.pallas_call(rim_kernel, out_shape=(shape((32, half), F32), shape((64,...  1.51 us
    pallas_call x1, Pallas kernels, per_device(): pl.pallas_call(early_kernel, out_shape=shape((inner * 32, ext), F32), in_...  1.31 us
  transfers between devices with their start and end apart: 4, of which 3 were waited for; matrix products, arithmetic and copies ran while one was open for 0% of the time, Pallas kernels for 16%

profile of v8, /device:TPU:0, one launch (start us, length us, event | category | flops | bytes accessed | tf_op | source)
XLA Modules:
  0.0 33.8 jit_solution(1610244204621658574)
XLA Ops:
  0.6 4.1 %outer.1 = (f32[9,512,128]{2,1,0:T(8,128)S(1)}, f32[9,512,128]{2,1,0:T(8,128)S(1)}, f32[88,1152]{1,0:T(8,128)S(1)}, f32[88,1152]{1,0:T(8,128)S(1)}, bf16[128,256]{1,0:T(8,128)(2,1)S(1)}) custom-call(s32[2,32]{1,0:T(2,128)} %far_shift.1, s32[1,32]{1,0:T(1,128)} %far_ids.1, s32[1,32]{1,0:T(1,128)} %far_members.1, f32[5,8,5]{2,1,0:T(8,128)} %bitcast.9, ...), custom_call_target="tpu_custom_call" | custom-call | tf_op jit(solution)/shard_map/outer/pallas_call | solution.py:538
  4.8 0.5 %collective-permute-start = (f32[88,1152]{1,0:T(8,128)S(1)}, f32[88,1152]{1,0:T(8,128)S(1)}, u32[]{:S(2)}, u32[]{:S(2)}) collective-permute-start(f32[88,1152]{1,0:T(8,128)S(1)} %get-tuple-element.23), channel_id=1, source_target_pairs={{0,1},{1,0},{2,3},{3,2},{4,5},{5,4},{6,7},{7,6},{8,9},{9,8},{10,11... | collective-permute-start | bytes 1216520 | tf_op jit(solution)/shard_map/ppermute | solution.py:569
  5.3 1.3 %early.1.made.ours = f32[384,1152]{1,0:T(8,128)S(1)} custom-call(f32[9,512,128]{2,1,0:T(8,128)S(1)} %get-tuple-element.24.landed, bf16[128,256]{1,0:T(8,128)(2,1)S(1)} %get-tuple-element.25.weights), custom_call_target="tpu_custom_call" | custom-call | flops 1000000000 | bytes 4194304 | tf_op jit(solution)/shard_map/early/pallas_call | solution.py:571
  6.6 0.1 collective-permute-done.other.other1
  6.7 0.1 border.1
  6.8 0.4 %collective-permute-start.1 = (f32[9,512,128]{2,1,0:T(8,128)S(1)}, f32[9,512,128]{2,1,0:T(8,128)S(1)}, u32[]{:S(2)}, u32[]{:S(2)}) collective-permute-start(f32[9,512,128]{2,1,0:T(8,128)S(1)} %get-tuple-element.27), channel_id=1, source_target_pairs={{0,1},{1,0},{2,3},{3,2},{4,5},{5,4},{6,7},{7,6},{8,9},{9,8},{10,11... | collective-permute-start | bytes 7077896 | tf_op jit(solution)/shard_map/ppermute | solution.py:591
  7.2 2.7 %collective-permute-start.2 = (f32[41,8,128]{2,1,0:T(8,128)S(1)}, f32[41,8,128]{2,1,0:T(8,128)S(1)}, u32[]{:S(2)}, u32[]{:S(2)}) collective-permute-start(f32[41,8,128]{2,1,0:T(8,128)S(1)} %get-tuple-element.31), channel_id=1, source_target_pairs={{0,2},{2,0},{4,6},{6,4},{8,10},{10,8},{12,14},{14,12},{1,3},{3,1},... | collective-permute-start | bytes 503816 | tf_op jit(solution)/shard_map/ppermute | solution.py:595
  9.8 0.7 %collective-permute-start.3 = (f32[41,8,128]{2,1,0:T(8,128)S(1)}, f32[41,8,128]{2,1,0:T(8,128)S(1)}, u32[]{:S(2)}, u32[]{:S(2)}) collective-permute-start(f32[41,8,128]{2,1,0:T(8,128)S(1)} %get-tuple-element.32), channel_id=1, source_target_pairs={{2,4},{4,2},{6,8},{8,6},{10,12},{12,10},{3,5},{5,3},{7,9},{9,7},{1... | collective-permute-start | bytes 503816 | tf_op jit(solution)/shard_map/ppermute | solution.py:594
  10.5 0.8 %collective-permute-done.1.landed = f32[9,512,128]{2,1,0:T(8,128)S(1)} collective-permute-done((f32[9,512,128]{2,1,0:T(8,128)S(1)}, f32[9,512,128]{2,1,0:T(8,128)S(1)}, u32[]{:S(2)}, u32[]{:S(2)}) %collective-permute-start.1) | collective-permute-done | bytes 2359328 | tf_op jit(solution)/shard_map/ppermute | solution.py:591
  11.3 4.3 %interior.1 = (f32[224,1152]{1,0:T(8,128)S(1)}, f32[192,1152]{1,0:T(8,128)S(1)}, f32[160,1024]{1,0:T(8,128)S(1)}, bf16[896,1152]{1,0:T(8,128)(2,1)S(1)}, bf16[76...) custom-call(f32[88,1152]{1,0:T(8,128)S(1)} %get-tuple-element.22.own, ...), custom_call_target="tpu_custom_call" | custom-call | flops 10000000 | bytes 41943 | tf_op jit(solution)/shard_map/interior/pallas_call | solution.py:597
  15.6 1.9 %collective-permute-done.2.first = f32[41,8,128]{2,1,0:T(8,128)S(1)} collective-permute-done((f32[41,8,128]{2,1,0:T(8,128)S(1)}, f32[41,8,128]{2,1,0:T(8,128)S(1)}, u32[]{:S(2)}, u32[]{:S(2)}) %collective-permute-start.2) | collective-permute-done | bytes 167968 | tf_op jit(solution)/shard_map/ppermute | solution.py:595
  17.5 0.0 collective-permute-done.3.second
  17.5 1.5 %rim.1 = (f32[32,1024]{1,0:T(8,128)S(1)}, f32[64,1024]{1,0:T(8,128)S(1)}, f32[96,1024]{1,0:T(8,128)S(1)}, f32[16,128]{1,0:T(8,128)S(1)}) custom-call(f32[88,1152]{1,0:T(8,128)S(1)} %get-tuple-element.22.own.own1, f32[88,1152]{1,0:T(8,128)S(1)} %collective-permute-done.other.other1, f32[41,8,128]{2,1,0:T(8,128)S(1)} %collective-permute-done.2.first, ...), custom_call_target="tpu_custom_call" | custom-call | tf_op jit(solution)/shard_map/rim/pallas_call | solution.py:617
  19.1 12.5 %all_to_all.11 = f32[16,1,128]{2,1,0:T(1,128)S(1)} all-to-all(f32[16,1,128]{2,1,0:T(1,128)S(1)} %bitcast.7), channel_id=1, replica_groups=mesh['scene'=2,'tile'=8,'frame'=2] {'tile','frame'}, dimensions={0} | all-to-all | bytes 16384 | tf_op jit(solution)/shard_map/all_to_all | solution.py:631
  31.6 2.2 %update.1 = (f32[64,4096]{1,0:T(8,128)}, f32[64,4096]{1,0:T(8,128)}) custom-call(f32[224,1152]{1,0:T(8,128)S(1)} %get-tuple-element.28.base, f32[192,1152]{1,0:T(8,128)S(1)} %get-tuple-element.29.once, f32[160,1024]{1,0:T(8,128)S(1)} %get-tuple-element.30.twice, f32[32,1024]{1,0:T(8,128)S(1)} %get-tuple-element.37.base_rim, ...), custom_call_target="tpu_custom_call" | custom-call | tf_op jit(solution)/shard_map/update/pallas_call | solution.py:633
Async XLA Ops:
  4.8 1.9 %collective-permute-start = (f32[88,1152]{1,0:T(8,128)S(1)}, f32[88,1152]{1,0:T(8,128)S(1)}, u32[]{:S(2)}, u32[]{:S(2)}) collective-permute-start(f32[88,1152]{1,0:T(8,128)S(1)} %get-tuple-element.23), channel_id=1, source_target_pairs={{0,1},{1,0},{2,3},{3,2},{4,5},{5,4},{6,7},{7,6},{8,9},{9,8},{10,11... | collective-permute-start | bytes 1216520 | tf_op jit(solution)/shard_map/ppermute | solution.py:569
  6.8 4.6 %collective-permute-start.1 = (f32[9,512,128]{2,1,0:T(8,128)S(1)}, f32[9,512,128]{2,1,0:T(8,128)S(1)}, u32[]{:S(2)}, u32[]{:S(2)}) collective-permute-start(f32[9,512,128]{2,1,0:T(8,128)S(1)} %get-tuple-element.27), channel_id=1, source_target_pairs={{0,1},{1,0},{2,3},{3,2},{4,5},{5,4},{6,7},{7,6},{8,9},{9,8},{10,11... | collective-permute-start | bytes 7077896 | tf_op jit(solution)/shard_map/ppermute | solution.py:591
  7.2 10.4 %collective-permute-start.2 = (f32[41,8,128]{2,1,0:T(8,128)S(1)}, f32[41,8,128]{2,1,0:T(8,128)S(1)}, u32[]{:S(2)}, u32[]{:S(2)}) collective-permute-start(f32[41,8,128]{2,1,0:T(8,128)S(1)} %get-tuple-element.31), channel_id=1, source_target_pairs={{0,2},{2,0},{4,6},{6,4},{8,10},{10,8},{12,14},{14,12},{1,3},{3,1},... | collective-permute-start | bytes 503816 | tf_op jit(solution)/shard_map/ppermute | solution.py:595
  9.8 7.7 %collective-permute-start.3 = (f32[41,8,128]{2,1,0:T(8,128)S(1)}, f32[41,8,128]{2,1,0:T(8,128)S(1)}, u32[]{:S(2)}, u32[]{:S(2)}) collective-permute-start(f32[41,8,128]{2,1,0:T(8,128)S(1)} %get-tuple-element.32), channel_id=1, source_target_pairs={{2,4},{4,2},{6,8},{8,6},{10,12},{12,10},{3,5},{5,3},{7,9},{9,7},{1... | collective-permute-start | bytes 503816 | tf_op jit(solution)/shard_map/ppermute | solution.py:594
